TPU v7x, 128 devices: a whole 4x4x4 slice. The times are simulated.
128 devices in a mesh: grp: 8 (over x, core), dev: 16 (over y, z).
Axes of the slice: x: 4, y: 4, z: 4, core: 2. Of those that a mesh axis runs over, the one named last changes fastest.
Arguments:
- q_nope: bfloat16 [1024, 8192], P('grp', 'dev'), may hold values from -6 to 6
- q_rope: bfloat16 [1024, 4096], P('grp', 'dev'), may hold values from -60 to 60
- w_absorb_k: bfloat16 [64, 128, 512], P('dev'), may hold values from -0.5 to 0.5
- latent_cache: bfloat16 [1024, 512, 512], P(('grp', 'dev')), may hold values from -6 to 6
- rope_keys: bfloat16 [1024, 64, 512], P(('grp', 'dev')), may hold values from -9 to 9
- cache_lengths: int32 [1024], P(('grp', 'dev')), may hold values from 2 to 512, as said below
- w_absorb_v: bfloat16 [64, 512, 128], P('dev'), may hold values from -0.25 to 0.25
- w_out: bfloat16 [8192, 7168], P('dev'), may hold values from -0.0625 to 0.0625
- norm_gain: float32 [7168], replicated, may hold values from 0.5 to 1.5
- routes: int32 [1024, 4], P(('grp', 'dev')), may hold values from 0 to 15, all different within a row; in each aligned block of 8 rows (0 to 7, 8 to 15, ...) at most 4 rows name the same one
- expert_probs: float32 [1024, 4], P(('grp', 'dev')), may hold values from 0.05 to 1
- group_probs: float32 [1024, 8], P(('grp', 'dev')), may hold values from 0.1 to 1
- w_gate: bfloat16 [128, 7168, 256], P(('grp', 'dev')), may hold values from -0.0625 to 0.0625
- w_up: bfloat16 [128, 7168, 256], P(('grp', 'dev')), may hold values from -0.0625 to 0.0625
- w_down: bfloat16 [128, 256, 7168], P(('grp', 'dev')), may hold values from -0.125 to 0.125
Outputs:
- moe_out: bfloat16 [1024, 7168], P(('grp', 'dev'))
Inputs may be any that keep to these rules, and one draw needn't show every extreme that they name: `routes`: in each aligned block of 8 rows (the rows of one device) no expert is named by more than 4 rows, a bound that some block reaches; a row names 4 different experts. A request's live cache positions are the first cache_lengths of its 512; some request holds all 512.
All inputs are finite; a program needn't handle non-finite values.
Results may differ from a plain program's by a relative error of at most 0.035.
Values may be sent and summed in bfloat16 or wider, within the bound.
No kernel may reach another device: no remote copies, remote signals or barrier semaphores. Data moves between devices by JAX's collectives and lax.ppermute only.
A program may use at most 128 MiB of HBM per device.

v0:
```python
import jax
import jax.numpy as jnp
from jax import lax
from jax.sharding import PartitionSpec as P

EXP_GRP = 2
CAP = 4


def expert_block(rows_in, gate_shard, up_shard, down_shard):
    gate_value = jnp.dot(rows_in, gate_shard, preferred_element_type=jnp.float32)
    up_value = jnp.dot(rows_in, up_shard, preferred_element_type=jnp.float32)
    hidden = (jax.nn.silu(gate_value) * up_value).astype(jnp.bfloat16)
    return jnp.dot(hidden, down_shard, preferred_element_type=jnp.float32)


def per_device(
    q_nope,
    q_rope,
    w_absorb_k,
    latent_cache,
    rope_keys,
    cache_lengths,
    w_absorb_v,
    w_out,
    norm_gain,
    routes,
    expert_probs,
    group_probs,
    w_gate,
    w_up,
    w_down,
):
    batch_rows = q_nope.shape[0]
    heads_local = w_absorb_k.shape[0]
    nope_width = w_absorb_k.shape[1]
    latent_width = w_absorb_k.shape[2]
    rope_width = q_rope.shape[1] // heads_local
    value_width = w_absorb_v.shape[2]
    model_width = w_out.shape[1]
    requests = rope_keys.shape[0]
    cache_len = rope_keys.shape[2]
    softmax_scale = float(nope_width + rope_width) ** (-0.5)
    query_heads = q_nope.reshape(batch_rows, heads_local, nope_width)
    query_latent = jnp.einsum(
        "bhn,hnc->bhc", query_heads, w_absorb_k, preferred_element_type=jnp.float32
    )
    query_latent = query_latent.astype(jnp.bfloat16).reshape(batch_rows, heads_local * latent_width)
    owner_latent, owner_rope = (
        lax.all_to_all(query_latent, "dev", split_axis=0, concat_axis=1, tiled=True),
        lax.all_to_all(q_rope, "dev", split_axis=0, concat_axis=1, tiled=True),
    )
    head_total = owner_latent.shape[1] // latent_width
    owner_latent = owner_latent.reshape(requests, head_total, latent_width)
    owner_rope = owner_rope.reshape(requests, head_total, rope_width)
    scores = jnp.einsum(
        "rhc,rlc->rhl", owner_latent, latent_cache, preferred_element_type=jnp.float32
    )
    scores = scores + jnp.einsum(
        "rhp,rpl->rhl", owner_rope, rope_keys, preferred_element_type=jnp.float32
    )
    scores = scores * softmax_scale
    visible = jnp.arange(cache_len)[None, None, :] < cache_lengths[:, None, None]
    scores = jnp.where(visible, scores, -jnp.inf)
    top_score = jnp.max(scores, axis=2, keepdims=True)
    exponent = jnp.exp(scores - top_score)
    softmax_probs = (exponent / jnp.sum(exponent, axis=2, keepdims=True)).astype(jnp.bfloat16)
    latent_out = jnp.einsum(
        "rhl,rlc->rhc", softmax_probs, latent_cache, preferred_element_type=jnp.float32
    )
    latent_out = latent_out.astype(jnp.bfloat16).reshape(requests, head_total * latent_width)
    head_latent = lax.all_to_all(latent_out, "dev", split_axis=1, concat_axis=0, tiled=True)
    head_latent = head_latent.reshape(batch_rows, heads_local, latent_width)
    head_values = jnp.einsum(
        "bhc,hcv->bhv", head_latent, w_absorb_v, preferred_element_type=jnp.float32
    )
    head_values = head_values.astype(jnp.bfloat16).reshape(batch_rows, heads_local * value_width)
    attended = lax.psum_scatter(
        jnp.dot(head_values, w_out, preferred_element_type=jnp.float32).astype(jnp.bfloat16),
        "dev",
        scatter_dimension=0,
        tiled=True,
    )
    attended_wide = attended.astype(jnp.float32)
    mean_square = jnp.mean(attended_wide * attended_wide, axis=1, keepdims=True)
    normed = (attended_wide * lax.rsqrt(mean_square + 1e-06) * norm_gain[None, :]).astype(
        jnp.bfloat16
    )
    top_count = routes.shape[1]
    group_count = group_probs.shape[1]
    expert_count = EXP_GRP * group_count
    capacity = CAP
    flat_routes = routes.reshape(requests * top_count)
    chosen = (flat_routes[:, None] == jnp.arange(expert_count)[None, :]).astype(jnp.int32)
    earlier = jnp.cumsum(chosen, axis=0) - chosen
    rank_in = jnp.sum(earlier * chosen, axis=1)
    slot_index = flat_routes * capacity + rank_in
    slot_ids = jnp.arange(expert_count * capacity)
    placed = slot_index.reshape(requests, top_count)[None, :, :] == slot_ids[:, None, None]
    dispatch = jnp.any(placed, axis=2).astype(jnp.bfloat16)
    outgoing = jnp.dot(dispatch, normed, preferred_element_type=jnp.float32).astype(jnp.bfloat16)
    shard_count = lax.axis_size("dev") // EXP_GRP
    arriving = lax.all_to_all(
        outgoing.reshape(group_count, EXP_GRP * capacity, model_width),
        "grp",
        split_axis=0,
        concat_axis=0,
        tiled=True,
    )
    arriving = arriving.reshape(1, group_count, EXP_GRP, capacity, model_width)
    own_expert = lax.axis_index("dev") // shard_count
    owned = jnp.arange(EXP_GRP)[None, None, :, None, None] == own_expert
    block_rows = lax.all_gather(arriving, "dev", axis=0, tiled=True)
    sources = block_rows.shape[0]
    picked = lax.dynamic_index_in_dim(block_rows, own_expert, 2, keepdims=False)
    shard_part = expert_block(
        picked.reshape(sources * group_count * capacity, model_width), w_gate[0], w_up[0], w_down[0]
    )
    shard_part = shard_part.astype(jnp.bfloat16).astype(jnp.float32)
    shard_part = shard_part.reshape(sources, group_count, 1, capacity, model_width)
    terms = jnp.where(owned, shard_part, 0.0)
    summed = lax.psum_scatter(terms.astype(jnp.bfloat16), "dev", scatter_dimension=0, tiled=True)
    returned = lax.all_to_all(
        summed.reshape(group_count, EXP_GRP * capacity, model_width),
        "grp",
        split_axis=0,
        concat_axis=0,
        tiled=True,
    )
    expert_out = returned.reshape(expert_count * capacity, model_width)
    pair_rows = expert_out[slot_index].reshape(requests, top_count, model_width).astype(jnp.float32)
    route_groups = routes // EXP_GRP
    group_match = route_groups[:, :, None] == jnp.arange(group_count)[None, None, :]
    group_weight = jnp.sum(jnp.where(group_match, group_probs[:, None, :], 0.0), axis=2)
    pair_weight = group_weight * expert_probs
    mixed = jnp.sum(pair_weight[:, :, None] * pair_rows, axis=1)
    return mixed.astype(jnp.bfloat16)


def solution(mesh):
    placed = (
        P("grp", "dev"),
        P("grp", "dev"),
        P("dev", None, None),
        P(("grp", "dev"), None, None),
        P(("grp", "dev"), None, None),
        P(("grp", "dev")),
        P("dev", None, None),
        P("dev", None),
        P(),
        P(("grp", "dev"), None),
        P(("grp", "dev"), None),
        P(("grp", "dev"), None),
        P(("grp", "dev"), None, None),
        P(("grp", "dev"), None, None),
        P(("grp", "dev"), None, None),
    )
    return jax.shard_map(
        per_device, mesh=mesh, in_specs=placed, out_specs=P(("grp", "dev"), None), check_vma=False
    )
```

profile of v0, /device:TPU:1, one launch (start us, length us, event | category | flops | bytes accessed | tf_op | source)
XLA Modules:
  0.0 485.3 jit_solution(8191776889134964832)
XLA Ops:
  6.5 8.7 %all-to-all-start.1 = ((bf16[16,8,256]{2,1,0:T(8,128)(2,1)}), bf16[16,8,256]{2,1,0:T(8,128)(2,1)S(1)}, u32[]{:S(2)}, u32[]{:S(2)}) async-start(bf16[16,8,256]{2,1,0:T(8,128)(2,1)} %bitcast.66), calls=%async_computation.1 | async-start | bytes 131072 | tf_op jit(solution)/shard_map/all_to_all | solution.py:51
  15.3 1.3 fusion.12
  17.0 1.2 all_to_all.42
  18.1 3.7 all-to-all-done.1
  21.8 3.6 all-to-all-start
  25.4 0.7 iota_compare_fusion
  26.3 8.2 %all-to-all-done = bf16[16,8,2048]{2,1,0:T(8,128)(2,1)S(1)} async-done(((bf16[16,8,2048]{2,1,0:T(8,128)(2,1)}), bf16[16,8,2048]{2,1,0:T(8,128)(2,1)S(1)}, u32[]{:S(2)}, u32[]{:S(2)}) %all-to-all-start) | async-done | bytes 524320 | tf_op jit(solution)/shard_map/all_to_all | solution.py:50
  35.1 3.6 fusion.48
  39.3 3.2 convolution_convert_fusion.3
  43.1 12.2 %all_to_all.58 = bf16[8,16,2048]{2,0,1:T(8,128)(2,1)S(1)} all-to-all(bf16[8,16,2048]{2,0,1:T(8,128)(2,1)S(1)} %copy.77), channel_id=1, replica_groups=mesh['grp'=8,'dev'=16] {'dev'}, dimensions={1} | all-to-all | bytes 1048576 | tf_op jit(solution)/shard_map/all_to_all | solution.py:72
  56.1 5.5 %convolution_convert_fusion.1 = bf16[128,7168]{1,0:T(8,128)(2,1)} fusion(bf16[128,512]{0,1:T(8,128)(2,1)S(1)} %bitcast.64, bf16[512,7168]{1,0:T(8,128)(2,1)} %param.22), kind=kOutput, calls=%fused_computation.5 | convolution fusion | flops 940441600 | bytes 9306112 | tf_op jit(solution)/shard_map/dot_general | solution.py:79
  62.3 0.6 dynamic-slice
  63.6 87.9 %all-reduce.4.cloned.1.call-done = bf16[128,7168]{1,0:T(8,128)(2,1)} async-done(((bf16[128,7168]{1,0:T(8,128)(2,1)}), bf16[128,7168]{1,0:T(8,128)(2,1)}) %all-reduce.4.cloned.1.call-update) | async-done | bytes 1835024
  151.6 1.1 fusion.29
  152.7 1.4 fusion.2
  154.0 19.8 %all_to_all.59 = bf16[8,8,7168]{2,1,0:T(8,128)(2,1)S(1)} all-to-all(bf16[8,8,7168]{2,1,0:T(8,128)(2,1)S(1)} %fusion.2), channel_id=1, replica_groups=mesh['grp'=8,'dev'=16] {'grp'}, dimensions={0} | all-to-all | bytes 1835008 | tf_op jit(solution)/shard_map/all_to_all | solution.py:103
  173.9 1.4 copy.80
  175.6 98.2 %all-gather.2.cloned.1.call-done = bf16[16,8,2,4,7168]{4,1,3,2,0:T(8,128)(2,1)} async-done(((bf16[1,8,2,4,7168]{4,1,3,2,0:T(8,128)(2,1)}), bf16[16,8,2,4,7168]{4,1,3,2,0:T(8,128)(2,1)}) %all-gather.2.cloned.1.call-update) | async-done | bytes 14680080 | tf_op jit(solution)/shard_map/all_gather | solution.py:113
  273.8 6.7 %constant_dynamic-slice_fusion = bf16[16,8,1,4,7168]{4,1,3,2,0:T(8,128)(2,1)} fusion(bf16[16,8,2,4,7168]{4,1,3,2,0:T(8,128)(2,1)} %all-gather.2.cloned.1.call-done, s32[]{:T(128)S(6)} %select_n.40), kind=kLoop, calls=%fused_computation.68 | loop fusion | bytes 14680068 | tf_op jit(solution)/shard_map/jit(dynamic_index_in_dim)/dynamic_slice | solution.py:115
  280.4 12.2 %copy.81 = bf16[16,8,1,4,7168]{4,3,1,0,2:T(4,128)(2,1)} copy(bf16[16,8,1,4,7168]{4,1,3,2,0:T(8,128)(2,1)} %constant_dynamic-slice_fusion) | data formatting | bytes 14680064 | tf_op jit(solution)/shard_map/jit(dynamic_index_in_dim)/dynamic_slice | solution.py:115
  292.6 12.1 %reshape.135 = bf16[512,7168]{1,0:T(8,128)(2,1)} reshape(bf16[16,8,1,4,7168]{4,3,1,0,2:T(4,128)(2,1)} %copy.81) | data formatting | bytes 14680064 | tf_op jit(solution)/shard_map/reshape | solution.py:117
  304.7 6.2 %fusion.6 = f32[512,256]{1,0:T(8,128)S(1)} fusion(bf16[512,7168]{1,0:T(8,128)(2,1)} %reshape.135, bf16[1,7168,256]{2,1,0:T(8,128)(2,1)} %param.27), kind=kOutput, calls=%fused_computation.11 | convolution fusion | flops 1879048192 | bytes 11534336 | tf_op jit(solution)/shard_map/dot_general | solution.py:11
  310.9 16.0 %fusion.1 = bf16[512,7168]{1,0:T(8,128)(2,1)} fusion(bf16[1,256,7168]{2,1,0:T(8,128)(2,1)} %param.29, bf16[512,7168]{1,0:T(8,128)(2,1)} %reshape.135, bf16[1,7168,256]{2,1,0:T(8,128)(2,1)} %param.28, f32[512,256]{1,0:T(8,128)S(1)} %fusion.6), kind=kOutput, calls=%fused_computation.4 | convolution fusion | flops 3762552832 | bytes 22544384 | tf_op jit(solution)/shard_map/dot_general | solution.py:14
  326.9 12.6 %reshape.138 = bf16[16,8,4,7168]{3,2,1,0:T(4,128)(2,1)} reshape(bf16[512,7168]{1,0:T(8,128)(2,1)} %fusion.1) | data formatting | bytes 14680064 | tf_op jit(solution)/shard_map/jit(_where)/broadcast_in_dim | solution.py:121
  339.5 5.6 %copy.82 = bf16[16,8,4,7168]{3,1,2,0:T(8,128)(2,1)S(1)} copy(bf16[16,8,4,7168]{3,2,1,0:T(4,128)(2,1)} %reshape.138) | data formatting | bytes 14680064 | tf_op jit(solution)/shard_map/jit(_where)/broadcast_in_dim | solution.py:121
  345.1 8.3 %select_convert_fusion = bf16[16,8,2,4,7168]{4,1,3,2,0:T(8,128)(2,1)} fusion(bf16[16,8,4,7168]{3,1,2,0:T(8,128)(2,1)S(1)} %copy.82, pred[2]{0:T(512)(128)(4,1)S(1)} %iota_compare_fusion.4), kind=kLoop, calls=%fused_computation.2 | loop fusion | flops 7340032 | bytes 22020098 | tf_op jit(solution)/shard_map/convert_element_type | solution.py:122
  353.5 101.2 %reduce-scatter.4.cloned.1.call-done = bf16[1,8,2,4,7168]{4,1,3,2,0:T(8,128)(2,1)} async-done(((bf16[16,8,2,4,7168]{4,1,3,2,0:T(8,128)(2,1)}), bf16[1,8,2,4,7168]{4,1,3,2,0:T(8,128)(2,1)}) %reduce-scatter.4.cloned.1.call-update) | async-done | bytes 917520
  454.7 2.6 copy.83
  457.3 5.3 %all-to-all-start.4 = ((bf16[8,8,7168]{2,1,0:T(8,128)(2,1)}), bf16[8,8,7168]{2,1,0:T(8,128)(2,1)S(1)}, u32[]{:S(2)}, u32[]{:S(2)}) async-start(bf16[8,8,7168]{2,1,0:T(8,128)(2,1)} %copy.83), calls=%async_computation.4 | async-start | bytes 1835008 | tf_op jit(solution)/shard_map/all_to_all | solution.py:123
  463.0 13.3 %all-to-all-done.4 = bf16[8,8,7168]{2,1,0:T(8,128)(2,1)S(1)} async-done(((bf16[8,8,7168]{2,1,0:T(8,128)(2,1)}), bf16[8,8,7168]{2,1,0:T(8,128)(2,1)S(1)}, u32[]{:S(2)}, u32[]{:S(2)}) %all-to-all-start.4) | async-done | bytes 917536 | tf_op jit(solution)/shard_map/all_to_all | solution.py:123
  476.3 0.8 gather_fusion
  477.4 1.3 multiply_reduce_fusion
  (54 shorter events, 4.8 us)
Async XLA Ops:
  6.5 8.7 %copy-start = (bf16[4,128,512]{2,1,0:T(8,128)(2,1)S(1)}, bf16[4,128,512]{2,1,0:T(8,128)(2,1)}, u32[]{:S(2)}) copy-start(bf16[4,128,512]{2,1,0:T(8,128)(2,1)} %param.17) | copy-start | bytes 1572868
  6.5 32.2 %copy-start.3 = (bf16[8,64,512]{2,1,0:T(8,128)(2,1)S(1)}, bf16[8,64,512]{2,1,0:T(8,128)(2,1)}, u32[]{:S(2)}) copy-start(bf16[8,64,512]{2,1,0:T(8,128)(2,1)} %param.19) | copy-start | bytes 1572868
  6.5 15.3 %all-to-all-start.1 = ((bf16[16,8,256]{2,1,0:T(8,128)(2,1)}), bf16[16,8,256]{2,1,0:T(8,128)(2,1)S(1)}, u32[]{:S(2)}, u32[]{:S(2)}) async-start(bf16[16,8,256]{2,1,0:T(8,128)(2,1)} %bitcast.66), calls=%async_computation.1 | async-start | bytes 131072 | tf_op jit(solution)/shard_map/all_to_all | solution.py:51
  21.8 12.7 %all-to-all-start = ((bf16[16,8,2048]{2,1,0:T(8,128)(2,1)}), bf16[16,8,2048]{2,1,0:T(8,128)(2,1)S(1)}, u32[]{:S(2)}, u32[]{:S(2)}) async-start(bf16[16,8,2048]{2,1,0:T(8,128)(2,1)} %all_to_all.42), calls=%async_computation | async-start | bytes 1048576 | tf_op jit(solution)/shard_map/all_to_all | solution.py:50
  25.4 126.2 %all-reduce.4.cloned.1.call-start = ((), (), s32[]{:S(2)}) async-start(), calls=%async_computation.7 | async-start | bytes 3670016
  38.7 17.0 %copy-start.2 = (bf16[4,512,128]{2,1,0:T(8,128)(2,1)S(1)}, bf16[4,512,128]{2,1,0:T(8,128)(2,1)}, u32[]{:S(2)}) copy-start(bf16[4,512,128]{2,1,0:T(8,128)(2,1)} %param.21) | copy-start | bytes 1572868
  56.1 5.6 %copy-start.5 = (s32[8,4]{0,1:T(4,128)S(1)}, s32[8,4]{0,1:T(4,128)}, u32[]{:S(2)}) copy-start(s32[8,4]{0,1:T(4,128)} %param.24) | copy-start | bytes 388
  56.1 6.3 %copy-start.8 = (u32[128]{0:T(128)S(1)}, u32[128]{0:T(128)}, u32[]{:S(2)}) copy-start(u32[128]{0:T(128)} %constant.75) | copy-start | bytes 1540
  56.1 96.6 %copy-start.4 = (f32[7168]{0:T(1024)S(1)}, f32[7168]{0:T(1024)}, u32[]{:S(2)}) copy-start(f32[7168]{0:T(1024)} %param.23) | copy-start | bytes 86020
  61.6 212.2 %all-gather.2.cloned.1.call-start = ((), (), s32[]{:S(2)}) async-start(), calls=%async_computation.6 | async-start | bytes 15597568 | tf_op jit(solution)/shard_map/all_gather | solution.py:113
  175.3 279.3 %reduce-scatter.4.cloned.1.call-start = ((), (), s32[]{:S(2)}) async-start(), calls=%async_computation.8 | async-start | bytes 15597568
  353.4 109.3 %copy-start.6 = (f32[8,8]{1,0:T(8,128)S(1)}, f32[8,8]{1,0:T(8,128)}, u32[]{:S(2)}) copy-start(f32[8,8]{1,0:T(8,128)} %param.26) | copy-start | bytes 772
  353.4 109.4 %copy-start.7 = (f32[8,4]{0,1:T(4,128)S(1)}, f32[8,4]{0,1:T(4,128)}, u32[]{:S(2)}) copy-start(f32[8,4]{0,1:T(4,128)} %param.25) | copy-start | bytes 388
  353.5 125.3 %copy-start.1 = (bf16[4,128,512]{2,1,0:T(8,128)(2,1)S(1)}, bf16[4,128,512]{2,1,0:T(8,128)(2,1)}, u32[]{:S(2)}) copy-start(bf16[4,128,512]{2,1,0:T(8,128)(2,1)} %param.17) | copy-start | bytes 1572868
  457.3 19.0 %all-to-all-start.4 = ((bf16[8,8,7168]{2,1,0:T(8,128)(2,1)}), bf16[8,8,7168]{2,1,0:T(8,128)(2,1)S(1)}, u32[]{:S(2)}, u32[]{:S(2)}) async-start(bf16[8,8,7168]{2,1,0:T(8,128)(2,1)} %copy.83), calls=%async_computation.4 | async-start | bytes 1835008 | tf_op jit(solution)/shard_map/all_to_all | solution.py:123
Sparse Core Ops, SparseCore 0:
  61.7 89.8 all-reduce.3
  175.5 98.2 all-gather.1
  353.6 101.0 reduce-scatter.3
where the time goes:
time: 487 us; the launch traced here: 485 us
  waiting for transfers between devices  313 us (64%)
  local copies, waits for them, and re-layouts  58.8 us (12%)
  matrix products  37.6 us (8%)
  blocking collectives  32 us (7%)
  starting transfers between devices  17.9 us (4%)
  between operations  14 us (3%)
  other arithmetic  12.3 us (3%)
    unnamed x5, waiting for transfers between devices  189 us
    all_gather x1, waiting for transfers between devices, per_device(): block_rows = lax.all_gather(arriving, 'dev', axis=0, tiled=True)  98.2 us
    all_to_all x1, blocking collectives, per_device(): lax.all_to_all(outgoing.reshape(group_count, EXP_GRP * capacity, model_wi...  19.8 us
    dynamic_slice x2, local copies, waits for them, and re-layouts, per_device(): picked = lax.dynamic_index_in_dim(block_rows, own_expert, 2, keepdims=False)  18.9 us
    broadcast_in_dim x2, local copies, waits for them, and re-layouts, per_device(): terms = jnp.where(owned, shard_part, 0.0)  18.3 us
    dot_general x1, matrix products, expert_block(): return jnp.dot(hidden, down_shard, preferred_element_type=jnp.float32)  16 us
    all_to_all x1, waiting for transfers between devices, per_device(): lax.all_to_all(summed.reshape(group_count, EXP_GRP * capacity, model_widt...  13.3 us
    all_to_all x1, blocking collectives, per_device(): lax.all_to_all(latent_out, 'dev', split_axis=1, concat_axis=0, tiled=True)  12.2 us
  transfers between devices with their start and end apart: 6, of which 6 were waited for; matrix products, arithmetic and copies ran while one was open for 1% of the time, Pallas kernels for 0%

commit v1 on v0

v1 whole, which is shorter than its diff:
```python
import functools

import jax
import jax.numpy as jnp
from jax import lax
from jax.experimental import pallas as pl
from jax.experimental.pallas import tpu as pltpu
from jax.sharding import PartitionSpec as P

EXP_GRP = 2
CAP = 4
F32 = jnp.float32
BF16 = jnp.bfloat16


def hidden_kernel(count, *refs):
    row_refs = refs[:count]
    gate_ref, up_ref, out_ref, gate_sum, up_sum = refs[count:]
    step = pl.program_id(0)

    @pl.when(step == 0)
    def _():
        gate_sum[...] = jnp.zeros_like(gate_sum)
        up_sum[...] = jnp.zeros_like(up_sum)

    rows = jnp.concatenate([ref[...] for ref in row_refs], axis=0)
    gate_sum[...] += jnp.dot(rows, gate_ref[0], preferred_element_type=F32)
    up_sum[...] += jnp.dot(rows, up_ref[0], preferred_element_type=F32)

    @pl.when(step == pl.num_programs(0) - 1)
    def _():
        gate = gate_sum[...]
        out_ref[...] = (gate * jax.nn.sigmoid(gate) * up_sum[...]).astype(BF16)


def expert_hidden(blocks, w_gate, w_up, tile=1024):
    rows = sum(block.shape[0] for block in blocks)
    width, units = w_gate.shape[1:]
    return pl.pallas_call(
        functools.partial(hidden_kernel, len(blocks)),
        grid=(width // tile,),
        out_shape=jax.ShapeDtypeStruct((rows, units), BF16),
        in_specs=[pl.BlockSpec((block.shape[0], tile), lambda i: (0, i)) for block in blocks]
        + [pl.BlockSpec((1, tile, units), lambda i: (0, i, 0))] * 2,
        out_specs=pl.BlockSpec((rows, units), lambda i: (0, 0)),
        scratch_shapes=[pltpu.VMEM((rows, units), F32)] * 2,
        compiler_params=pltpu.CompilerParams(vmem_limit_bytes=24 * 1024 * 1024),
        cost_estimate=pl.CostEstimate(
            flops=4 * rows * width * units,
            bytes_accessed=2 * width * (2 * units + rows),
            transcendentals=rows * units,
        ),
    )(*blocks, w_gate, w_up)


def per_device(
    q_nope,
    q_rope,
    w_absorb_k,
    latent_cache,
    rope_keys,
    cache_lengths,
    w_absorb_v,
    w_out,
    norm_gain,
    routes,
    expert_probs,
    group_probs,
    w_gate,
    w_up,
    w_down,
):
    batch_rows = q_nope.shape[0]
    heads_local, nope_width, latent_width = w_absorb_k.shape
    rope_width = q_rope.shape[1] // heads_local
    value_width = w_absorb_v.shape[2]
    model_width = w_out.shape[1]
    requests, _, cache_len = rope_keys.shape
    devs = lax.axis_size("dev")
    groups = lax.axis_size("grp")
    shards = devs // EXP_GRP
    experts = EXP_GRP * groups
    top_count = routes.shape[1]
    softmax_scale = float(nope_width + rope_width) ** (-0.5)
    halves = [[half * shards + s for s in range(shards)] for half in range(EXP_GRP)]

    units = w_down.shape[1]
    slice_width = model_width // shards
    down = w_down[0].reshape(units, shards, slice_width).transpose(1, 0, 2)
    down = lax.all_to_all(
        down, "dev", split_axis=0, concat_axis=0, tiled=True, axis_index_groups=halves
    )

    query_heads = q_nope.reshape(batch_rows, heads_local, nope_width)
    query_latent = jnp.einsum("bhn,hnc->bhc", query_heads, w_absorb_k, preferred_element_type=F32)
    query_latent = query_latent.astype(BF16).reshape(batch_rows, heads_local * latent_width)
    query = jnp.concatenate([query_latent, q_rope], axis=1)
    query = query.reshape(devs, requests, query.shape[1])
    query = lax.all_to_all(query, "dev", split_axis=0, concat_axis=0, tiled=True)
    split = heads_local * latent_width
    heads = devs * heads_local
    owner_latent = (
        query[:, :, :split]
        .reshape(devs, requests, heads_local, latent_width)
        .transpose(1, 0, 2, 3)
        .reshape(requests, heads, latent_width)
    )
    owner_rope = (
        query[:, :, split:]
        .reshape(devs, requests, heads_local, rope_width)
        .transpose(1, 0, 2, 3)
        .reshape(requests, heads, rope_width)
    )
    scores = jnp.einsum("rhc,rlc->rhl", owner_latent, latent_cache, preferred_element_type=F32)
    scores = scores + jnp.einsum("rhp,rpl->rhl", owner_rope, rope_keys, preferred_element_type=F32)
    scores = scores * softmax_scale
    visible = jnp.arange(cache_len)[None, None, :] < cache_lengths[:, None, None]
    scores = jnp.where(visible, scores, -jnp.inf)
    top_score = jnp.max(scores, axis=2, keepdims=True)
    exponent = jnp.exp(scores - top_score)
    softmax_probs = (exponent / jnp.sum(exponent, axis=2, keepdims=True)).astype(BF16)
    latent_out = jnp.einsum("rhl,rlc->rhc", softmax_probs, latent_cache, preferred_element_type=F32)
    latent_out = (
        latent_out.astype(BF16)
        .reshape(requests, devs, heads_local * latent_width)
        .transpose(1, 0, 2)
    )
    head_latent = lax.all_to_all(latent_out, "dev", split_axis=0, concat_axis=0, tiled=True)
    head_latent = head_latent.reshape(batch_rows, heads_local, latent_width)
    head_values = jnp.einsum("bhc,hcv->bhv", head_latent, w_absorb_v, preferred_element_type=F32)
    head_values = head_values.astype(BF16).reshape(batch_rows, heads_local * value_width)
    partial = jnp.dot(head_values, w_out, preferred_element_type=F32).astype(BF16)
    partial = lax.all_to_all(
        partial.reshape(devs, requests, model_width),
        "dev",
        split_axis=0,
        concat_axis=0,
        tiled=True,
    )
    attended = jnp.sum(partial.astype(F32), axis=0).astype(BF16)
    attended_wide = attended.astype(F32)
    mean_square = jnp.mean(attended_wide * attended_wide, axis=1, keepdims=True)
    normed = (attended_wide * lax.rsqrt(mean_square + 1e-06) * norm_gain[None, :]).astype(BF16)

    flat_routes = routes.reshape(requests * top_count)
    chosen = (flat_routes[:, None] == jnp.arange(experts)[None, :]).astype(jnp.int32)
    earlier = jnp.cumsum(chosen, axis=0) - chosen
    rank_in = jnp.sum(earlier * chosen, axis=1)
    slot_index = (flat_routes * CAP + rank_in).reshape(requests, top_count)
    slot_ids = jnp.arange(experts * CAP)
    placed = slot_index[None, :, :] == slot_ids[:, None, None]
    dispatch = jnp.any(placed, axis=2).astype(BF16)
    outgoing = jnp.dot(dispatch, normed, preferred_element_type=F32).astype(BF16)

    peers = [
        [g * devs + half * shards + p for g in range(groups) for half in range(EXP_GRP)]
        for p in range(shards)
    ]
    own = lax.all_to_all(
        outgoing.reshape(experts, CAP, model_width),
        ("grp", "dev"),
        split_axis=0,
        concat_axis=0,
        tiled=True,
        axis_index_groups=peers,
    ).reshape(experts * CAP, model_width)

    ring = shards // 2
    z_up = [(i, i // ring * ring + (i + 1) % ring) for i in range(devs)]
    z_down = [(i, i // ring * ring + (i + ring - 1) % ring) for i in range(devs)]
    y_pair = [(i, i ^ ring) for i in range(devs)]
    half_rows = own.shape[0] // 2
    lo, hi = slice(0, half_rows), slice(half_rows, None)

    def send(value, way):
        return lax.ppermute(value, "dev", way)

    below = send(own, z_up)
    above = send(own, z_down)
    beside = send(own, y_pair)
    first = expert_hidden([own, below, above, beside], w_gate, w_up)
    far_lo = send(below[lo], z_up)
    far_hi = send(above[hi], z_down)
    beside_below_lo = send(beside[lo], z_up)
    beside_above_hi = send(beside[hi], z_down)
    beside_below_hi = send(below[hi], y_pair)
    beside_above_lo = send(above[lo], y_pair)
    second = expert_hidden(
        [far_lo, far_hi, beside_below_lo, beside_below_hi, beside_above_lo, beside_above_hi],
        w_gate,
        w_up,
    )
    beside_far_lo = send(beside_below_lo, z_up)
    beside_far_hi = send(beside_above_hi, z_down)
    third = expert_hidden([beside_far_lo, beside_far_hi], w_gate, w_up)
    rows = own.shape[0]
    relative = jnp.concatenate([first, second, third], axis=0).reshape(shards, rows, units)
    order = jnp.array([0, 1, 4, 2, 3, 5, 7, 6], jnp.int32)
    place = lax.axis_index("dev") % shards
    position = jnp.arange(shards, dtype=jnp.int32)
    other = (position // ring) ^ (place // ring)
    steps = (place % ring - position % ring) % ring
    hidden = relative[order[other * ring + steps]].reshape(shards * rows, units)

    everyone = lax.all_to_all(
        jnp.broadcast_to(hidden[None], (shards, shards * rows, units)),
        "dev",
        split_axis=0,
        concat_axis=0,
        tiled=True,
        axis_index_groups=halves,
    )
    result = jnp.einsum("smk,skd->md", everyone, down, preferred_element_type=F32).astype(BF16)
    result = (
        result.reshape(shards, groups, EXP_GRP, CAP, slice_width)
        .transpose(1, 2, 0, 3, 4)
        .reshape(groups * devs, CAP, slice_width)
    )
    result = lax.all_to_all(result, ("grp", "dev"), split_axis=0, concat_axis=0, tiled=True)
    expert_out = (
        result.reshape(experts, shards, CAP, slice_width)
        .transpose(0, 2, 1, 3)
        .reshape(experts * CAP, model_width)
    )
    pair_rows = expert_out[slot_index.reshape(-1)].reshape(requests, top_count, model_width)
    group_match = (routes // EXP_GRP)[:, :, None] == jnp.arange(groups)[None, None, :]
    group_weight = jnp.sum(jnp.where(group_match, group_probs[:, None, :], 0.0), axis=2)
    pair_weight = group_weight * expert_probs
    mixed = jnp.sum(pair_weight[:, :, None] * pair_rows.astype(F32), axis=1)
    return mixed.astype(BF16)


def solution(mesh):
    placed = (
        P("grp", "dev"),
        P("grp", "dev"),
        P("dev", None, None),
        P(("grp", "dev"), None, None),
        P(("grp", "dev"), None, None),
        P(("grp", "dev")),
        P("dev", None, None),
        P("dev", None),
        P(),
        P(("grp", "dev"), None),
        P(("grp", "dev"), None),
        P(("grp", "dev"), None),
        P(("grp", "dev"), None, None),
        P(("grp", "dev"), None, None),
        P(("grp", "dev"), None, None),
    )
    return jax.shard_map(
        per_device, mesh=mesh, in_specs=placed, out_specs=P(("grp", "dev"), None), check_vma=False
    )
```

time: 487 us -> 283 us (0.58)
  waiting for transfers between devices: 313 us -> 124 us
  local copies, waits for them, and re-layouts: 58.8 us -> 24.1 us
  blocking collectives: 32 us -> 64.6 us
  matrix products: 37.6 us -> 19 us
  starting transfers between devices: 17.9 us -> 36 us
  between operations: 14 us -> 0.53 us
  Pallas kernels: 0 us -> 8.96 us
  other arithmetic: 12.3 us -> 4.43 us
    unnamed x5 -> x0, waiting for transfers between devices: 189 us -> none
    all_gather x1 -> x0, waiting for transfers between devices: 98.2 us -> none  [per_device(): block_rows = lax.all_gather(arriving, 'dev', axis=0, tiled=True)]
    ppermute x0 -> x11, waiting for transfers between devices: none -> 74 us  [send(): return lax.ppermute(value, 'dev', way)]
    all_to_all x2 -> x3, blocking collectives: 32 us -> 64.6 us  [the longest x1 26.6 us: per_device(): lax.all_to_all(jnp.broadcast_to(hidden[None], (shards, shards * rows, uni...]
    all_to_all x3 -> x4, waiting for transfers between devices: 25.2 us -> 50.1 us  [the longest x1 21.7 us: per_device(): lax.all_to_all(partial.reshape(devs, requests, model_width), 'dev', split...]
    dynamic_slice x2 -> x0, local copies, waits for them, and re-layouts: 18.9 us -> none  [per_device(): picked = lax.dynamic_index_in_dim(block_rows, own_expert, 2, keepdims=False)]
    dot_general x4 -> x3, matrix products: 29 us -> 10.3 us  [the longest x1 5.49 us: per_device(): jnp.dot(head_values, w_out, preferred_element_type=F32).astype(BF16)]
    broadcast_in_dim x2 -> x1, local copies, waits for them, and re-layouts: 18.3 us -> 0.14 us  [per_device(): jnp.broadcast_to(hidden[None], (shards, shards * rows, units))]
  transfers between devices with their start and end apart: 6 -> 15, of which waited for: 6 -> 8; matrix products, arithmetic and copies ran while one was open for 1% -> 5% of each run, Pallas kernels for 0% -> 3%
where the time goes in v1:
time: 283 us; the launch traced here: 282 us
  waiting for transfers between devices  124 us (44%)
  blocking collectives  64.6 us (23%)
  starting transfers between devices  36 us (13%)
  local copies, waits for them, and re-layouts  24.1 us (9%)
  matrix products  19 us (7%)
  Pallas kernels  8.96 us (3%)
  other arithmetic  4.43 us (2%)
    ppermute x11, waiting for transfers between devices, send(): return lax.ppermute(value, 'dev', way)  74 us
    all_to_all x1, blocking collectives, per_device(): lax.all_to_all(jnp.broadcast_to(hidden[None], (shards, shards * rows, uni...  26.6 us
    all_to_all x1, blocking collectives, per_device(): lax.all_to_all(outgoing.reshape(experts, CAP, model_width), ('grp', 'dev'...  25.5 us
    all_to_all x1, waiting for transfers between devices, per_device(): lax.all_to_all(partial.reshape(devs, requests, model_width), 'dev', split...  21.7 us
    all_to_all x1, waiting for transfers between devices, per_device(): lax.all_to_all(result, ('grp', 'dev'), split_axis=0, concat_axis=0, tiled...  17.5 us
    all_to_all x1, blocking collectives, per_device(): lax.all_to_all(latent_out, 'dev', split_axis=0, concat_axis=0, tiled=True)  12.5 us
    ppermute x11, starting transfers between devices, send(): return lax.ppermute(value, 'dev', way)  11.8 us
    all_to_all x1, waiting for transfers between devices, per_device(): lax.all_to_all(query, 'dev', split_axis=0, concat_axis=0, tiled=True)  10.9 us
  transfers between devices with their start and end apart: 15, of which 8 were waited for; matrix products, arithmetic and copies ran while one was open for 5% of the time, Pallas kernels for 3%

profile of v1, /device:TPU:1, one launch (start us, length us, event | category | flops | bytes accessed | tf_op | source)
XLA Modules:
  0.0 281.6 jit_solution(18155296909642055032)
XLA Ops:
  1.0 1.3 fusion.6
  3.1 1.7 pad_maximum_fusion
  4.8 8.6 %all-to-all-start = ((bf16[16,8,2304]{2,1,0:T(8,128)(2,1)}), bf16[16,8,2304]{2,1,0:T(8,128)(2,1)S(1)}, u32[]{:S(2)}, u32[]{:S(2)}) async-start(bf16[16,8,2304]{2,1,0:T(8,128)(2,1)} %pad_maximum_fusion), calls=%async_computation | async-start | bytes 1179648 | tf_op jit(solution)/shard_map/all_to_all | solution.py:99
  13.5 10.9 %all-to-all-done = bf16[16,8,2304]{2,1,0:T(8,128)(2,1)S(1)} async-done(((bf16[16,8,2304]{2,1,0:T(8,128)(2,1)}), bf16[16,8,2304]{2,1,0:T(8,128)(2,1)S(1)}, u32[]{:S(2)}, u32[]{:S(2)}) %all-to-all-start) | async-done | bytes 589856 | tf_op jit(solution)/shard_map/all_to_all | solution.py:99
  25.1 3.6 %fusion.35 = f32[8,64,512]{2,1,0:T(8,128)S(1)} fusion(bf16[8,64,512]{2,1,0:T(8,128)(2,1)S(1)} %reshape.246, bf16[8,512,512]{2,1,0:T(8,128)(2,1)} %param.19), kind=kOutput, calls=%fused_computation.81 | convolution fusion | flops 268435456 | bytes 5767168 | tf_op jit(solution)/shard_map/rhc,rlc->rhl/dot_general | solution.py:114
  29.2 3.2 %convolution_convert_fusion.2 = bf16[8,64,512]{2,1,0:T(8,128)(2,1)S(1)} fusion(bf16[8,512,512]{2,1,0:T(8,128)(2,1)} %param.19, f32[8,64]{1,0:T(8,128)S(1)} %fusion.34, f32[8,64,512]{2,1,0:T(8,128)S(1)} %fusion.5), kind=kOutput, calls=%fused_computation.13 | convolution fusion | flops 269485056 | bytes 5769216 | tf_op jit(solution)/shard_map/rhl,rlc->rhc/dot_general | solution.py:122
  33.1 12.5 %all_to_all.35 = bf16[16,8,2048]{2,1,0:T(8,128)(2,1)S(1)} all-to-all(bf16[16,8,2048]{2,1,0:T(8,128)(2,1)S(1)} %bitcast.75), channel_id=1, replica_groups=mesh['grp'=8,'dev'=16] {'dev'}, dimensions={0} | all-to-all | bytes 1048576 | tf_op jit(solution)/shard_map/all_to_all | solution.py:128
  46.3 5.5 %fusion.1 = bf16[16,8,7168]{2,1,0:T(8,128)(2,1)} fusion(bf16[128,512]{0,1:T(8,128)(2,1)S(1)} %bitcast.79, bf16[512,7168]{1,0:T(8,128)(2,1)} %param.23), kind=kOutput, calls=%fused_computation.5 | convolution fusion | flops 940441600 | bytes 9306112 | tf_op jit(solution)/shard_map/dot_general | solution.py:132
  51.8 3.8 %all-to-all-start.2 = ((bf16[16,8,7168]{2,1,0:T(8,128)(2,1)}), bf16[16,8,7168]{2,1,0:T(8,128)(2,1)S(1)}, u32[]{:S(2)}, u32[]{:S(2)}) async-start(bf16[16,8,7168]{2,1,0:T(8,128)(2,1)} %fusion.1), calls=%async_computation.2 | async-start | bytes 3670016 | tf_op jit(solution)/shard_map/all_to_all | solution.py:133
  56.4 21.7 %all-to-all-done.2 = bf16[16,8,7168]{2,1,0:T(8,128)(2,1)S(1)} async-done(((bf16[16,8,7168]{2,1,0:T(8,128)(2,1)}), bf16[16,8,7168]{2,1,0:T(8,128)(2,1)S(1)}, u32[]{:S(2)}, u32[]{:S(2)}) %all-to-all-start.2) | async-done | bytes 1835040 | tf_op jit(solution)/shard_map/all_to_all | solution.py:133
  79.3 25.5 %all_to_all.36 = bf16[16,4,7168]{2,1,0:T(4,128)(2,1)S(1)} all-to-all(bf16[16,4,7168]{2,1,0:T(4,128)(2,1)S(1)} %reshape.253), channel_id=1, replica_groups={{0,8,16,24,32,40,48,56,64,72,80,88,96,104,112,120},{1,9,17,25,33,41,49,..., dimensions={0} | all-to-all | bytes 1835008 | tf_op jit(solution)/shard_map/all_to_all | solution.py:159
  106.0 5.9 %copy.73 = bf16[1,256,7168]{1,2,0:T(8,128)(2,1)} copy(bf16[1,256,7168]{2,1,0:T(8,128)(2,1)} %param.30) | data formatting | bytes 7340032 | tf_op args[14]
  111.9 6.3 %copy.74 = bf16[256,8,896]{2,0,1:T(8,128)(2,1)} copy(bf16[256,8,896]{0,2,1:T(8,128)(2,1)} %bitcast.70) | data formatting | bytes 7340032 | tf_op jit(solution)/shard_map/reshape;squeeze | solution.py:89
  118.2 4.6 %all-to-all-start.5 = ((bf16[8,256,896]{2,1,0:T(8,128)(2,1)}), bf16[8,256,896]{2,1,0:T(8,128)(2,1)}, u32[]{:S(2)}, u32[]{:S(2)}) async-start(bf16[8,256,896]{2,1,0:T(8,128)(2,1)} %bitcast.69), calls=%async_computation.5 | async-start | bytes 7340032 | tf_op jit(solution)/shard_map/all_to_all | solution.py:90
  123.5 1.4 collective-permute-start
  124.9 1.4 collective-permute-start.1
  127.0 2.4 collective-permute-start.8
  129.4 55.9 %collective-permute-done.refs_1_ = bf16[64,7168]{1,0:T(8,128)(2,1)S(1)} collective-permute-done((bf16[64,7168]{1,0:T(8,128)(2,1)S(1)}, bf16[64,7168]{1,0:T(8,128)(2,1)S(1)}, u32[]{:S(2)}, u32[]{:S(2)}) %collective-permute-start) | collective-permute-done | bytes 917536 | tf_op jit(solution)/shard_map/ppermute | solution.py:176
  185.6 2.9 %collective-permute-start.4 = (bf16[32,7168]{1,0:T(8,128)(2,1)S(1)}, bf16[32,7168]{1,0:T(8,128)(2,1)S(1)}, u32[]{:S(2)}, u32[]{:S(2)}) collective-permute-start(bf16[32,7168]{1,0:T(8,128)(2,1)S(1)} %get-tuple-element.6), channel_id=1, source_target_pairs={{0,3},{1,0},{2,1},{3,2},{4,7},{5,4},{6,5},{7,6},{8,11},{9,8},{10,9... | collective-permute-start | bytes 1376264 | tf_op jit(solution)/shard_map/ppermute | solution.py:176
  189.7 5.5 %collective-permute-done.5.refs_2_ = bf16[32,7168]{1,0:T(8,128)(2,1)S(1)} collective-permute-done((bf16[32,7168]{1,0:T(8,128)(2,1)S(1)}, bf16[32,7168]{1,0:T(8,128)(2,1)S(1)}, u32[]{:S(2)}, u32[]{:S(2)}) %collective-permute-start.5) | collective-permute-done | bytes 458784 | tf_op jit(solution)/shard_map/ppermute | solution.py:176
  196.4 8.6 %collective-permute-done.3.refs_0_ = bf16[32,7168]{1,0:T(8,128)(2,1)S(1)} collective-permute-done((bf16[32,7168]{1,0:T(8,128)(2,1)S(1)}, bf16[32,7168]{1,0:T(8,128)(2,1)S(1)}, u32[]{:S(2)}, u32[]{:S(2)}) %collective-permute-start.3) | collective-permute-done | bytes 458784 | tf_op jit(solution)/shard_map/ppermute | solution.py:176
  205.1 2.0 copy-done.3
  207.1 3.5 %shard_map.154 = bf16[256,256]{1,0:T(8,128)(2,1)S(1)} custom-call(bf16[64,7168]{1,0:T(8,128)(2,1)S(1)} %reshape.254.refs_0_, bf16[64,7168]{1,0:T(8,128)(2,1)S(1)} %collective-permute-done.refs_1_, bf16[64,7168]{1,0:T(8,128)(2,1)S(1)} %collective-permute-done.1.refs_2_, bf16[64,7168]{1,0:T(8,128)(2,1)S(1)} %collective-permute-done.2.refs_3_, ...), custom_call_target="tpu_custom_call" | custom-call | flops 1879048192 | bytes 11010048 | tf_op jit(solution)/shard_map/pallas_call | solution.py:39
  210.7 3.1 %shard_map.155 = bf16[192,256]{1,0:T(8,128)(2,1)S(1)} custom-call(bf16[32,7168]{1,0:T(8,128)(2,1)S(1)} %collective-permute-done.3.refs_0_, bf16[32,7168]{1,0:T(8,128)(2,1)S(1)} %collective-permute-done.4.refs_1_, bf16[32,7168]{1,0:T(8,128)(2,1)S(1)} %collective-permute-done.5.refs_2_, bf16[32,7168]{1,0:T(8,128)(2,1)S(1)} %collective-permute-done.6.refs_3_, ...), custom_call_target="tpu_custom_call" | custom-call | flops 1409286144 | bytes 10092544 | tf_op jit(solution)/shard_map/pallas_call | solution.py:39
  213.8 3.6 %collective-permute-done.9.refs_0_ = bf16[32,7168]{1,0:T(8,128)(2,1)S(1)} collective-permute-done((bf16[32,7168]{1,0:T(8,128)(2,1)S(1)}, bf16[32,7168]{1,0:T(8,128)(2,1)S(1)}, u32[]{:S(2)}, u32[]{:S(2)}) %collective-permute-start.9) | collective-permute-done | bytes 458784 | tf_op jit(solution)/shard_map/ppermute | solution.py:176
  217.4 2.3 shard_map.156
  220.5 26.6 %all_to_all.37 = bf16[8,512,256]{2,1,0:T(8,128)(2,1)S(1)} all-to-all(bf16[8,512,256]{2,1,0:T(8,128)(2,1)S(1)} %broadcast_in_dim.33), channel_id=1, replica_groups={{0,1,2,3,4,5,6,7},{8,9,10,11,12,13,14,15},{16,17,18,19,20,21,22,23},{24..., dimensions={0} | all-to-all | bytes 4194304 | tf_op jit(solution)/shard_map/all_to_all | solution.py:205
  247.1 4.4 %bitcast_convert_fusion = bf16[512,896]{1,0:T(8,128)(2,1)S(1)} fusion(bf16[8,512,256]{2,1,0:T(8,128)(2,1)S(1)} %all_to_all.37, bf16[8,256,896]{2,1,0:T(8,128)(2,1)} %all-to-all-done.5), kind=kOutput, calls=%fused_computation.7 | convolution fusion | flops 1879506944 | bytes 6684672 | tf_op jit(solution)/shard_map/smk,skd->md/dot_general | solution.py:213
  252.2 1.7 copy.76
  253.9 7.1 %all-to-all-start.6 = ((bf16[128,4,896]{2,1,0:T(4,128)(2,1)}), bf16[128,4,896]{2,1,0:T(4,128)(2,1)S(1)}, u32[]{:S(2)}, u32[]{:S(2)}) async-start(bf16[128,4,896]{2,1,0:T(4,128)(2,1)} %copy.76), calls=%async_computation.6 | async-start | bytes 1835008 | tf_op jit(solution)/shard_map/all_to_all | solution.py:219
  261.4 17.5 %all-to-all-done.6 = bf16[128,4,896]{2,1,0:T(4,128)(2,1)S(1)} async-done(((bf16[128,4,896]{2,1,0:T(4,128)(2,1)}), bf16[128,4,896]{2,1,0:T(4,128)(2,1)S(1)}, u32[]{:S(2)}, u32[]{:S(2)}) %all-to-all-start.6) | async-done | bytes 917536 | tf_op jit(solution)/shard_map/all_to_all | solution.py:219
  280.3 1.3 multiply_reduce_fusion
  (95 shorter events, 14.9 us)
Async XLA Ops:
  0.0 1.0 copy-start
  0.0 13.4 %copy-start.12 = (s32[8]{0:T(128)S(1)}, s32[8]{0:T(128)}, u32[]{:S(2)}) copy-start(s32[8]{0:T(128)} %param.21) | copy-start | bytes 100
  4.8 19.6 %all-to-all-start = ((bf16[16,8,2304]{2,1,0:T(8,128)(2,1)}), bf16[16,8,2304]{2,1,0:T(8,128)(2,1)S(1)}, u32[]{:S(2)}, u32[]{:S(2)}) async-start(bf16[16,8,2304]{2,1,0:T(8,128)(2,1)} %pad_maximum_fusion), calls=%async_computation | async-start | bytes 1179648 | tf_op jit(solution)/shard_map/all_to_all | solution.py:99
  24.7 3.9 %copy-start.7 = (bf16[8,64,512]{2,1,0:T(8,128)(2,1)S(1)}, bf16[8,64,512]{2,1,0:T(8,128)(2,1)}, u32[]{:S(2)}) copy-start(bf16[8,64,512]{2,1,0:T(8,128)(2,1)} %param.20) | copy-start | bytes 1572868
  32.4 13.5 %copy-start.6 = (bf16[4,512,128]{2,1,0:T(8,128)(2,1)S(1)}, bf16[4,512,128]{2,1,0:T(8,128)(2,1)}, u32[]{:S(2)}) copy-start(bf16[4,512,128]{2,1,0:T(8,128)(2,1)} %param.22) | copy-start | bytes 1572868
  51.8 3.9 %copy-start.9 = (s32[8,4]{0,1:T(4,128)S(1)}, s32[8,4]{0,1:T(4,128)}, u32[]{:S(2)}) copy-start(s32[8,4]{0,1:T(4,128)} %param.25) | copy-start | bytes 388
  51.8 26.7 %copy-start.8 = (f32[7168]{0:T(1024)S(1)}, f32[7168]{0:T(1024)}, u32[]{:S(2)}) copy-start(f32[7168]{0:T(1024)} %param.24) | copy-start | bytes 86020
  51.8 26.3 %all-to-all-start.2 = ((bf16[16,8,7168]{2,1,0:T(8,128)(2,1)}), bf16[16,8,7168]{2,1,0:T(8,128)(2,1)S(1)}, u32[]{:S(2)}, u32[]{:S(2)}) async-start(bf16[16,8,7168]{2,1,0:T(8,128)(2,1)} %fusion.1), calls=%async_computation.2 | async-start | bytes 3670016 | tf_op jit(solution)/shard_map/all_to_all | solution.py:133
  105.0 21.6 %collective-permute-start.2 = (bf16[64,7168]{1,0:T(8,128)(2,1)S(1)}, bf16[64,7168]{1,0:T(8,128)(2,1)S(1)}, u32[]{:S(2)}, u32[]{:S(2)}) collective-permute-start(bf16[64,7168]{1,0:T(8,128)(2,1)S(1)} %reshape.254.refs_0_), channel_id=1, source_target_pairs={{0,4},{1,5},{2,6},{3,7},{4,0},{5,1},{6,2},{7,3},{8,12},{9,13},{10,... | collective-permute-start | bytes 2752520 | tf_op jit(solution)/shard_map/ppermute | solution.py:176
  118.2 4.7 %copy-start.5 = (s32[8]{0:T(128)S(1)}, s32[8]{0:T(128)}, u32[]{:S(2)}) copy-start(s32[8]{0:T(128)} %constant.105.clone) | copy-start | bytes 100
  118.2 102.2 %all-to-all-start.5 = ((bf16[8,256,896]{2,1,0:T(8,128)(2,1)}), bf16[8,256,896]{2,1,0:T(8,128)(2,1)}, u32[]{:S(2)}, u32[]{:S(2)}) async-start(bf16[8,256,896]{2,1,0:T(8,128)(2,1)} %bitcast.69), calls=%async_computation.5 | async-start | bytes 7340032 | tf_op jit(solution)/shard_map/all_to_all | solution.py:90
  123.5 81.5 %copy-start.2 = (bf16[1,7168,256]{2,1,0:T(8,128)(2,1)S(1)}, bf16[1,7168,256]{2,1,0:T(8,128)(2,1)}, u32[]{:S(2)}) copy-start(bf16[1,7168,256]{2,1,0:T(8,128)(2,1)} %refs_2_.1) | copy-start | bytes 11010052
  123.5 61.8 %collective-permute-start = (bf16[64,7168]{1,0:T(8,128)(2,1)S(1)}, bf16[64,7168]{1,0:T(8,128)(2,1)S(1)}, u32[]{:S(2)}, u32[]{:S(2)}) collective-permute-start(bf16[64,7168]{1,0:T(8,128)(2,1)S(1)} %reshape.254.refs_0_), channel_id=1, source_target_pairs={{0,1},{1,2},{2,3},{3,0},{4,5},{5,6},{6,7},{7,4},{8,9},{9,10},{10,1... | collective-permute-start | bytes 2752520 | tf_op jit(solution)/shard_map/ppermute | solution.py:176
  124.9 60.6 %collective-permute-start.1 = (bf16[64,7168]{1,0:T(8,128)(2,1)S(1)}, bf16[64,7168]{1,0:T(8,128)(2,1)S(1)}, u32[]{:S(2)}, u32[]{:S(2)}) collective-permute-start(bf16[64,7168]{1,0:T(8,128)(2,1)S(1)} %reshape.254.refs_0_), channel_id=1, source_target_pairs={{0,3},{1,0},{2,1},{3,2},{4,7},{5,4},{6,5},{7,6},{8,11},{9,8},{10,9... | collective-permute-start | bytes 2752520 | tf_op jit(solution)/shard_map/ppermute | solution.py:176
  126.7 68.5 %collective-permute-start.5 = (bf16[32,7168]{1,0:T(8,128)(2,1)S(1)}, bf16[32,7168]{1,0:T(8,128)(2,1)S(1)}, u32[]{:S(2)}, u32[]{:S(2)}) collective-permute-start(bf16[32,7168]{1,0:T(8,128)(2,1)S(1)} %get-tuple-element.10), channel_id=1, source_target_pairs={{0,1},{1,2},{2,3},{3,0},{4,5},{5,6},{6,7},{7,4},{8,9},{9,10},{10,1... | collective-permute-start | bytes 1376264 | tf_op jit(solution)/shard_map/ppermute | solution.py:176
  127.0 69.4 %collective-permute-start.8 = (bf16[32,7168]{1,0:T(8,128)(2,1)S(1)}, bf16[32,7168]{1,0:T(8,128)(2,1)S(1)}, u32[]{:S(2)}, u32[]{:S(2)}) collective-permute-start(bf16[32,7168]{1,0:T(8,128)(2,1)S(1)} %get-tuple-element.9), channel_id=1, source_target_pairs={{0,3},{1,0},{2,1},{3,2},{4,7},{5,4},{6,5},{7,6},{8,11},{9,8},{10,9... | collective-permute-start | bytes 1376264 | tf_op jit(solution)/shard_map/ppermute | solution.py:176
  185.4 19.6 %collective-permute-start.3 = (bf16[32,7168]{1,0:T(8,128)(2,1)S(1)}, bf16[32,7168]{1,0:T(8,128)(2,1)S(1)}, u32[]{:S(2)}, u32[]{:S(2)}) collective-permute-start(bf16[32,7168]{1,0:T(8,128)(2,1)S(1)} %get-tuple-element.8), channel_id=1, source_target_pairs={{0,1},{1,2},{2,3},{3,0},{4,5},{5,6},{6,7},{7,4},{8,9},{9,10},{10,1... | collective-permute-start | bytes 1376264 | tf_op jit(solution)/shard_map/ppermute | solution.py:176
  185.6 25.1 %collective-permute-start.4 = (bf16[32,7168]{1,0:T(8,128)(2,1)S(1)}, bf16[32,7168]{1,0:T(8,128)(2,1)S(1)}, u32[]{:S(2)}, u32[]{:S(2)}) collective-permute-start(bf16[32,7168]{1,0:T(8,128)(2,1)S(1)} %get-tuple-element.6), channel_id=1, source_target_pairs={{0,3},{1,0},{2,1},{3,2},{4,7},{5,4},{6,5},{7,6},{8,11},{9,8},{10,9... | collective-permute-start | bytes 1376264 | tf_op jit(solution)/shard_map/ppermute | solution.py:176
  188.5 22.2 %collective-permute-start.6 = (bf16[32,7168]{1,0:T(8,128)(2,1)S(1)}, bf16[32,7168]{1,0:T(8,128)(2,1)S(1)}, u32[]{:S(2)}, u32[]{:S(2)}) collective-permute-start(bf16[32,7168]{1,0:T(8,128)(2,1)S(1)} %get-tuple-element.7), channel_id=1, source_target_pairs={{0,4},{1,5},{2,6},{3,7},{4,0},{5,1},{6,2},{7,3},{8,12},{9,13},{10,... | collective-permute-start | bytes 1376264 | tf_op jit(solution)/shard_map/ppermute | solution.py:176
  195.2 15.5 %collective-permute-start.7 = (bf16[32,7168]{1,0:T(8,128)(2,1)S(1)}, bf16[32,7168]{1,0:T(8,128)(2,1)S(1)}, u32[]{:S(2)}, u32[]{:S(2)}) collective-permute-start(bf16[32,7168]{1,0:T(8,128)(2,1)S(1)} %get-tuple-element.5), channel_id=1, source_target_pairs={{0,4},{1,5},{2,6},{3,7},{4,0},{5,1},{6,2},{7,3},{8,12},{9,13},{10,... | collective-permute-start | bytes 1376264 | tf_op jit(solution)/shard_map/ppermute | solution.py:176
  196.4 17.4 %collective-permute-start.10 = (bf16[32,7168]{1,0:T(8,128)(2,1)S(1)}, bf16[32,7168]{1,0:T(8,128)(2,1)S(1)}, u32[]{:S(2)}, u32[]{:S(2)}) collective-permute-start(bf16[32,7168]{1,0:T(8,128)(2,1)S(1)} %collective-permute-done.8.refs_5_), channel_id=1, source_target_pairs={{0,3},{1,0},{2,1},{3,2},{4,7},{5,4},{6,5},{7,6},{8,11},{9,8},{10,9... | collective-permute-start | bytes 1376264 | tf_op jit(solution)/shard_map/ppermute | solution.py:176
  205.0 12.4 %collective-permute-start.9 = (bf16[32,7168]{1,0:T(8,128)(2,1)S(1)}, bf16[32,7168]{1,0:T(8,128)(2,1)S(1)}, u32[]{:S(2)}, u32[]{:S(2)}) collective-permute-start(bf16[32,7168]{1,0:T(8,128)(2,1)S(1)} %collective-permute-done.5.refs_2_), channel_id=1, source_target_pairs={{0,1},{1,2},{2,3},{3,0},{4,5},{5,6},{6,7},{7,4},{8,9},{9,10},{10,1... | collective-permute-start | bytes 1376264 | tf_op jit(solution)/shard_map/ppermute | solution.py:176
  205.0 2.0 copy-start.3
  210.6 6.8 %copy-start.4 = (bf16[1,7168,256]{2,1,0:T(8,128)(2,1)S(1)}, bf16[1,7168,256]{2,1,0:T(8,128)(2,1)}, u32[]{:S(2)}) copy-start(bf16[1,7168,256]{2,1,0:T(8,128)(2,1)} %refs_3_.1) | copy-start | bytes 11010052
  251.5 9.6 %copy-start.10 = (f32[8,8]{1,0:T(8,128)S(1)}, f32[8,8]{1,0:T(8,128)}, u32[]{:S(2)}) copy-start(f32[8,8]{1,0:T(8,128)} %param.27) | copy-start | bytes 772
  251.5 9.8 %copy-start.11 = (f32[8,4]{0,1:T(4,128)S(1)}, f32[8,4]{0,1:T(4,128)}, u32[]{:S(2)}) copy-start(f32[8,4]{0,1:T(4,128)} %param.26) | copy-start | bytes 388
  253.9 25.0 %all-to-all-start.6 = ((bf16[128,4,896]{2,1,0:T(4,128)(2,1)}), bf16[128,4,896]{2,1,0:T(4,128)(2,1)S(1)}, u32[]{:S(2)}, u32[]{:S(2)}) async-start(bf16[128,4,896]{2,1,0:T(4,128)(2,1)} %copy.76), calls=%async_computation.6 | async-start | bytes 1835008 | tf_op jit(solution)/shard_map/all_to_all | solution.py:219
  279.0 2.6 copy-start.1

commit v2 on v1

v2 whole, which is shorter than its diff:
```python
import functools

import jax
import jax.numpy as jnp
from jax import lax
from jax.experimental import pallas as pl
from jax.experimental.pallas import tpu as pltpu
from jax.sharding import PartitionSpec as P

EXP_GRP = 2
CAP = 4
LIMIT = 56 * 1024 * 1024
F32 = jnp.float32
BF16 = jnp.bfloat16


def hidden_kernel(count, *refs):
    row_refs = refs[:count]
    gate_ref, up_ref, out_ref, gate_sum, up_sum = refs[count:]
    step = pl.program_id(0)

    @pl.when(step == 0)
    def _():
        gate_sum[...] = jnp.zeros_like(gate_sum)
        up_sum[...] = jnp.zeros_like(up_sum)

    rows = jnp.concatenate([ref[...] for ref in row_refs], axis=0)
    gate_sum[...] += jnp.dot(rows, gate_ref[0], preferred_element_type=F32)
    up_sum[...] += jnp.dot(rows, up_ref[0], preferred_element_type=F32)

    @pl.when(step == pl.num_programs(0) - 1)
    def _():
        gate = gate_sum[...]
        out_ref[...] = (gate * jax.nn.sigmoid(gate) * up_sum[...]).astype(BF16)


def expert_hidden(blocks, w_gate, w_up, tile=1024):
    rows = sum(block.shape[0] for block in blocks)
    width, units = w_gate.shape[1:]
    return pl.pallas_call(
        functools.partial(hidden_kernel, len(blocks)),
        grid=(width // tile,),
        out_shape=jax.ShapeDtypeStruct((rows, units), BF16),
        in_specs=[pl.BlockSpec((block.shape[0], tile), lambda i: (0, i)) for block in blocks]
        + [pl.BlockSpec((1, tile, units), lambda i: (0, i, 0))] * 2,
        out_specs=pl.BlockSpec((rows, units), lambda i: (0, 0)),
        scratch_shapes=[pltpu.VMEM((rows, units), F32)] * 2,
        compiler_params=pltpu.CompilerParams(vmem_limit_bytes=24 * 1024 * 1024),
        cost_estimate=pl.CostEstimate(
            flops=4 * rows * width * units,
            bytes_accessed=2 * width * (2 * units + rows),
            transcendentals=rows * units,
        ),
    )(*blocks, w_gate, w_up)


def relay_kernel(count, order_ref, weight_ref, *refs):
    out_refs, held, in_sems, out_sems = refs[:count], *refs[count:]
    width = out_refs[0].shape[1]
    arriving, leaving = [], []
    for k in range(count):
        start = pl.multiple_of(order_ref[k] * width, 128)
        copy = pltpu.make_async_copy(
            weight_ref.at[0, :, pl.ds(start, width)], held.at[k], in_sems.at[k]
        )
        copy.start()
        arriving.append(copy)
    for k in range(count):
        arriving[k].wait()
        copy = pltpu.make_async_copy(held.at[k], out_refs[k], out_sems.at[k])
        copy.start()
        leaving.append(copy)
    for copy in leaving:
        copy.wait()


def column_blocks(weight, order):
    _, rows, columns = weight.shape
    count = order.shape[0]
    width = columns // count
    return pl.pallas_call(
        functools.partial(relay_kernel, count),
        out_shape=[jax.ShapeDtypeStruct((rows, width), weight.dtype)] * count,
        in_specs=[pl.BlockSpec(memory_space=pltpu.SMEM), pl.BlockSpec(memory_space=pl.ANY)],
        out_specs=[pl.BlockSpec(memory_space=pl.ANY)] * count,
        scratch_shapes=[
            pltpu.VMEM((count, rows, width), weight.dtype),
            pltpu.SemaphoreType.DMA((count,)),
            pltpu.SemaphoreType.DMA((count,)),
        ],
        compiler_params=pltpu.CompilerParams(vmem_limit_bytes=LIMIT),
        cost_estimate=pl.CostEstimate(
            flops=0, bytes_accessed=4 * rows * columns, transcendentals=0
        ),
    )(order, weight)


def down_kernel(groups, order_ref, hidden_ref, *refs):
    ring, total, units = hidden_ref.shape
    pieces = len(refs) - 3
    down_refs, out_ref, down, sems = refs[:pieces], *refs[pieces:]
    width = down_refs[0].shape[1]
    share = pieces // ring
    copies = [
        pltpu.make_async_copy(
            down_refs[i],
            down.at[pl.ds(i // share * units, units), pl.ds(i % share * width, width)],
            sems.at[i],
        )
        for i in range(pieces)
    ]
    for copy in copies:
        copy.start()
    for copy in copies:
        copy.wait()
    peers = groups * EXP_GRP
    rows = peers * CAP
    places = total // rows
    parts = 2
    tall = total // parts
    for part in range(parts):
        hidden = jnp.concatenate(
            [hidden_ref[order_ref[k], part * tall : (part + 1) * tall] for k in range(ring)],
            axis=1,
        )
        value = jnp.dot(hidden, down[...], preferred_element_type=F32).astype(BF16)
        for place in range(places // parts):
            for peer in range(peers):
                row = place * rows + peer * CAP
                out_ref[peer * places + part * (places // parts) + place] = value[row : row + CAP]


def expert_down(hidden, down, order, groups):
    ring, rows, units = hidden.shape
    width = down[0].shape[1] * len(down) // ring
    return pl.pallas_call(
        functools.partial(down_kernel, groups),
        out_shape=jax.ShapeDtypeStruct((rows // CAP, CAP, width), BF16),
        in_specs=[
            pl.BlockSpec(memory_space=pltpu.SMEM),
            pl.BlockSpec(memory_space=pltpu.VMEM),
        ]
        + [pl.BlockSpec(memory_space=pl.ANY)] * len(down),
        out_specs=pl.BlockSpec(memory_space=pltpu.VMEM),
        scratch_shapes=[
            pltpu.VMEM((ring * units, width), BF16),
            pltpu.SemaphoreType.DMA((len(down),)),
        ],
        compiler_params=pltpu.CompilerParams(vmem_limit_bytes=LIMIT),
        cost_estimate=pl.CostEstimate(
            flops=2 * ring * rows * units * width,
            bytes_accessed=2 * (ring * units * (rows + width) + rows * width),
            transcendentals=0,
        ),
    )(order, hidden, *down)


def absorb_kernel(nope_ref, rope_ref, weight_ref, out_ref, nope, rope, weight, sems):
    copies = [
        pltpu.make_async_copy(source, target, sems.at[i])
        for i, (source, target) in enumerate(
            ((nope_ref, nope), (weight_ref, weight), (rope_ref, rope))
        )
    ]
    for copy in copies:
        copy.start()
    copies[0].wait()
    copies[1].wait()
    heads, width, latent = weight.shape
    for h in range(heads):
        out_ref[:, h * latent : (h + 1) * latent] = jnp.dot(
            nope[:, h * width : (h + 1) * width], weight[h], preferred_element_type=F32
        ).astype(BF16)
    copies[2].wait()
    out_ref[:, heads * latent :] = rope[...]


def absorb(q_nope, q_rope, w_absorb_k):
    rows = q_nope.shape[0]
    heads, width, latent = w_absorb_k.shape
    columns = heads * latent + q_rope.shape[1]
    return pl.pallas_call(
        absorb_kernel,
        out_shape=jax.ShapeDtypeStruct((rows, columns), BF16),
        in_specs=[pl.BlockSpec(memory_space=pl.ANY)] * 3,
        out_specs=pl.BlockSpec(memory_space=pltpu.VMEM),
        scratch_shapes=[
            pltpu.VMEM(q_nope.shape, BF16),
            pltpu.VMEM(q_rope.shape, BF16),
            pltpu.VMEM(w_absorb_k.shape, BF16),
            pltpu.SemaphoreType.DMA((3,)),
        ],
        compiler_params=pltpu.CompilerParams(vmem_limit_bytes=LIMIT),
        cost_estimate=pl.CostEstimate(
            flops=2 * rows * heads * width * latent,
            bytes_accessed=2 * (rows * columns + heads * width * latent),
            transcendentals=0,
        ),
    )(q_nope, q_rope, w_absorb_k)


def attend_kernel(heads, scale, length_ref, query_ref, cache_ref, keys_ref, out_ref, wide, total):
    request = pl.program_id(0)
    devs = query_ref.shape[0]
    latent = cache_ref.shape[2]
    rope = keys_ref.shape[1]

    @pl.when(request == 0)
    def _():
        wide[...] = query_ref[...].astype(F32)

    query = wide[:, pl.ds(request, 1), :].reshape(devs, wide.shape[2]).astype(BF16)
    split = heads * latent
    parts = [query[:, h * latent : (h + 1) * latent] for h in range(heads)]
    ropes = [query[:, split + h * rope : split + (h + 1) * rope] for h in range(heads)]
    cache = cache_ref[0]
    scores = lax.dot_general(
        jnp.concatenate(parts, axis=0),
        cache,
        (((1,), (1,)), ((), ())),
        preferred_element_type=F32,
    )
    scores += jnp.dot(jnp.concatenate(ropes, axis=0), keys_ref[0], preferred_element_type=F32)
    scores *= scale
    live = lax.broadcasted_iota(jnp.int32, scores.shape, 1) < length_ref[request]
    scores = jnp.where(live, scores, -jnp.inf)
    exponent = jnp.exp(scores - jnp.max(scores, axis=1, keepdims=True))
    probs = (exponent / jnp.sum(exponent, axis=1, keepdims=True)).astype(BF16)
    value = jnp.dot(probs, cache, preferred_element_type=F32)
    value = jnp.concatenate([value[h * devs : (h + 1) * devs] for h in range(heads)], axis=1)
    total[:, pl.ds(request, 1), :] = value.reshape(devs, 1, split)

    @pl.when(request == pl.num_programs(0) - 1)
    def _():
        out_ref[...] = total[...].astype(BF16)


def attend(query, latent_cache, rope_keys, lengths, heads, scale):
    devs, requests, columns = query.shape
    _, rope, positions = rope_keys.shape
    latent = latent_cache.shape[2]
    rows = heads * devs
    return pl.pallas_call(
        functools.partial(attend_kernel, heads, scale),
        grid=(requests,),
        out_shape=jax.ShapeDtypeStruct((devs, requests, heads * latent), BF16),
        in_specs=[
            pl.BlockSpec(memory_space=pltpu.SMEM),
            pl.BlockSpec((devs, requests, columns), lambda r: (0, 0, 0)),
            pl.BlockSpec((1, positions, latent), lambda r: (r, 0, 0)),
            pl.BlockSpec((1, rope, positions), lambda r: (r, 0, 0)),
        ],
        out_specs=pl.BlockSpec((devs, requests, heads * latent), lambda r: (0, 0, 0)),
        scratch_shapes=[
            pltpu.VMEM((devs, requests, columns), F32),
            pltpu.VMEM((devs, requests, heads * latent), F32),
        ],
        compiler_params=pltpu.CompilerParams(vmem_limit_bytes=10 * 1024 * 1024),
        cost_estimate=pl.CostEstimate(
            flops=2 * requests * rows * positions * (2 * latent + rope),
            bytes_accessed=2 * requests * positions * (latent + rope),
            transcendentals=requests * rows * positions,
        ),
    )(lengths, query, latent_cache, rope_keys)


def project_kernel(latent_ref, absorb_hbm, weight_hbm, out_ref, absorb_ref, weight, sems):
    heads, latent, width = absorb_ref.shape
    tiles = sems.shape[0] - 1
    tile = weight.shape[1] // tiles
    copies = [pltpu.make_async_copy(absorb_hbm, absorb_ref, sems.at[tiles])] + [
        pltpu.make_async_copy(
            weight_hbm.at[:, pl.ds(t * tile, tile)], weight.at[:, pl.ds(t * tile, tile)], sems.at[t]
        )
        for t in range(tiles)
    ]
    for copy in copies:
        copy.start()
    copies[0].wait()
    values = jnp.concatenate(
        [
            jnp.dot(
                latent_ref[:, h * latent : (h + 1) * latent],
                absorb_ref[h],
                preferred_element_type=F32,
            ).astype(BF16)
            for h in range(heads)
        ],
        axis=1,
    )
    for t in range(tiles):
        copies[t + 1].wait()
        out_ref[:, t * tile : (t + 1) * tile] = jnp.dot(
            values, weight[:, t * tile : (t + 1) * tile], preferred_element_type=F32
        ).astype(BF16)


def project(head_latent, w_absorb_v, w_out, tiles=7):
    rows = head_latent.shape[0]
    depth, columns = w_out.shape
    return pl.pallas_call(
        project_kernel,
        out_shape=jax.ShapeDtypeStruct((rows, columns), BF16),
        in_specs=[
            pl.BlockSpec(memory_space=pltpu.VMEM),
            pl.BlockSpec(memory_space=pl.ANY),
            pl.BlockSpec(memory_space=pl.ANY),
        ],
        out_specs=pl.BlockSpec(memory_space=pltpu.VMEM),
        scratch_shapes=[
            pltpu.VMEM(w_absorb_v.shape, BF16),
            pltpu.VMEM(w_out.shape, BF16),
            pltpu.SemaphoreType.DMA((tiles + 1,)),
        ],
        compiler_params=pltpu.CompilerParams(vmem_limit_bytes=LIMIT),
        cost_estimate=pl.CostEstimate(
            flops=2 * rows * (depth * columns + w_absorb_v.size),
            bytes_accessed=2 * (depth * columns + rows * columns),
            transcendentals=0,
        ),
    )(head_latent, w_absorb_v, w_out)


def dispatch_kernel(partial_ref, gain_ref, place_ref, out_ref, wide):
    devs, requests, width = partial_ref.shape
    tile = width // 8
    square = jnp.zeros((requests, 1), F32)
    for t in range(0, width, tile):
        total = partial_ref[0, :, t : t + tile].astype(F32)
        for d in range(1, devs):
            total += partial_ref[d, :, t : t + tile].astype(F32)
        attended = total.astype(BF16).astype(F32)
        wide[:, t : t + tile] = attended
        square += jnp.sum(attended * attended, axis=1, keepdims=True)
    factor = lax.rsqrt(square / width + 1e-06)
    for t in range(0, width, tile):
        normed = (wide[:, t : t + tile] * factor * gain_ref[:, t : t + tile]).astype(BF16)
        rows = jnp.dot(place_ref[...], normed, preferred_element_type=F32).astype(BF16)
        for e in range(out_ref.shape[0]):
            out_ref[e, :, t : t + tile] = rows[e * CAP : (e + 1) * CAP]


def dispatch_rows(partial, gain, place):
    _, requests, width = partial.shape
    slots = place.shape[0]
    return pl.pallas_call(
        dispatch_kernel,
        out_shape=jax.ShapeDtypeStruct((slots // CAP, CAP, width), BF16),
        in_specs=[pl.BlockSpec(memory_space=pltpu.VMEM)] * 3,
        out_specs=pl.BlockSpec(memory_space=pltpu.VMEM),
        scratch_shapes=[pltpu.VMEM((requests, width), F32)],
        compiler_params=pltpu.CompilerParams(vmem_limit_bytes=10 * 1024 * 1024),
        cost_estimate=pl.CostEstimate(
            flops=2 * slots * requests * width,
            bytes_accessed=2 * partial.size,
            transcendentals=0,
        ),
    )(partial, gain, place)


def mix_kernel(ring, weight_ref, rows_ref, out_ref):
    width = rows_ref.shape[2]
    slots = weight_ref.shape[1]
    experts = slots // CAP
    shards = rows_ref.shape[0] // experts
    for z in range(ring):
        rows = jnp.concatenate(
            [
                sum(rows_ref[e * shards + s].astype(F32) for s in range(z, shards, ring))
                for e in range(experts)
            ],
            axis=0,
        )
        out_ref[:, z * width : (z + 1) * width] = jnp.dot(
            weight_ref[...], rows, precision=lax.Precision.HIGHEST, preferred_element_type=F32
        ).astype(BF16)


def mix(weight, rows, ring):
    requests, slots = weight.shape
    width = rows.shape[2]
    return pl.pallas_call(
        functools.partial(mix_kernel, ring),
        out_shape=jax.ShapeDtypeStruct((requests, ring * width), BF16),
        in_specs=[pl.BlockSpec(memory_space=pltpu.VMEM)] * 2,
        out_specs=pl.BlockSpec(memory_space=pltpu.VMEM),
        compiler_params=pltpu.CompilerParams(vmem_limit_bytes=10 * 1024 * 1024),
        cost_estimate=pl.CostEstimate(
            flops=2 * requests * slots * ring * width,
            bytes_accessed=2 * rows.size,
            transcendentals=0,
        ),
    )(weight, rows)


def per_device(
    q_nope,
    q_rope,
    w_absorb_k,
    latent_cache,
    rope_keys,
    cache_lengths,
    w_absorb_v,
    w_out,
    norm_gain,
    routes,
    expert_probs,
    group_probs,
    w_gate,
    w_up,
    w_down,
):
    batch_rows = q_nope.shape[0]
    heads_local, nope_width, latent_width = w_absorb_k.shape
    rope_width = q_rope.shape[1] // heads_local
    model_width = w_out.shape[1]
    requests, _, cache_len = rope_keys.shape
    devs = lax.axis_size("dev")
    groups = lax.axis_size("grp")
    shards = devs // EXP_GRP
    experts = EXP_GRP * groups
    top_count = routes.shape[1]
    softmax_scale = float(nope_width + rope_width) ** (-0.5)

    ring = shards // 2
    z_up = [(i, i // ring * ring + (i + 1) % ring) for i in range(devs)]
    z_down = [(i, i // ring * ring + (i + ring - 1) % ring) for i in range(devs)]
    y_pair = [(i, i ^ ring) for i in range(devs)]

    units = w_down.shape[1]
    place = lax.axis_index("dev") % shards
    step = jnp.arange(ring, dtype=jnp.int32)
    targets = (place + step) % ring
    sources = (place + ring - step) % ring
    split = shards // ring
    down_out = column_blocks(
        w_down, (targets[:, None] * split + jnp.arange(split, dtype=jnp.int32)).reshape(shards)
    )

    def relay(k, half):
        way = [(i, i // ring * ring + (i + k) % ring) for i in range(devs)]
        return lax.ppermute(down_out[k * split + half], "dev", way)

    query = absorb(q_nope, q_rope, w_absorb_k)
    query = query.reshape(devs, requests, query.shape[1])
    query = lax.all_to_all(query, "dev", split_axis=0, concat_axis=0, tiled=True)
    down = {(0, half): down_out[half] for half in range(split)}
    down |= {(1, 0): relay(1, 0), (3, 0): relay(3, 0)}
    latent_out = attend(
        query, latent_cache, rope_keys, cache_lengths, heads_local, softmax_scale
    )
    latent_out, down, down_out = lax.optimization_barrier((latent_out, down, down_out))
    down |= {(1, 1): relay(1, 1), (3, 1): relay(3, 1)}
    head_latent = lax.all_to_all(latent_out, "dev", split_axis=0, concat_axis=0, tiled=True)
    partial = project(
        head_latent.reshape(batch_rows, heads_local * latent_width), w_absorb_v, w_out
    )
    partial, down, down_out = lax.optimization_barrier((partial, down, down_out))
    partial = lax.all_to_all(
        partial.reshape(devs, requests, model_width),
        "dev",
        split_axis=0,
        concat_axis=0,
        tiled=True,
    )
    partial, down_out = lax.optimization_barrier((partial, down_out))
    down |= {(2, 0): relay(2, 0), (2, 1): relay(2, 1)}

    flat_routes = routes.reshape(requests * top_count)
    chosen = (flat_routes[:, None] == jnp.arange(experts)[None, :]).astype(jnp.int32)
    earlier = jnp.cumsum(chosen, axis=0) - chosen
    rank_in = jnp.sum(earlier * chosen, axis=1)
    slot_index = (flat_routes * CAP + rank_in).reshape(requests, top_count)
    slot_ids = jnp.arange(experts * CAP)
    placed = slot_index[None, :, :] == slot_ids[:, None, None]
    dispatch = jnp.any(placed, axis=2).astype(BF16)
    group_match = (routes // EXP_GRP)[:, :, None] == jnp.arange(groups)[None, None, :]
    group_weight = jnp.sum(jnp.where(group_match, group_probs[:, None, :], 0.0), axis=2)
    pair_weight = group_weight * expert_probs
    slot_weight = jnp.sum(jnp.where(placed, pair_weight[None], 0.0), axis=2).T
    outgoing = dispatch_rows(partial, norm_gain[None, :], dispatch)

    peers = [
        [g * devs + half * shards + p for g in range(groups) for half in range(EXP_GRP)]
        for p in range(shards)
    ]
    own = lax.all_to_all(
        outgoing,
        ("grp", "dev"),
        split_axis=0,
        concat_axis=0,
        tiled=True,
        axis_index_groups=peers,
    ).reshape(experts * CAP, model_width)

    own, down = lax.optimization_barrier((own, down))

    half_rows = own.shape[0] // 2
    lo, hi = slice(0, half_rows), slice(half_rows, None)

    def send(value, way):
        return lax.ppermute(value, "dev", way)

    below = send(own, z_up)
    above = send(own, z_down)
    beside = send(own, y_pair)
    first = expert_hidden([own, below, above, beside], w_gate, w_up)
    far_lo = send(below[lo], z_up)
    far_hi = send(above[hi], z_down)
    beside_below_lo = send(beside[lo], z_up)
    beside_above_hi = send(beside[hi], z_down)
    beside_below_hi = send(below[hi], y_pair)
    beside_above_lo = send(above[lo], y_pair)
    second = expert_hidden(
        [far_lo, far_hi, beside_below_lo, beside_below_hi, beside_above_lo, beside_above_hi],
        w_gate,
        w_up,
    )
    beside_far_lo = send(beside_below_lo, z_up)
    beside_far_hi = send(beside_above_hi, z_down)
    beside_far_lo, beside_far_hi, first, second = lax.optimization_barrier(
        (beside_far_lo, beside_far_hi, first, second)
    )
    third = expert_hidden([beside_far_lo, beside_far_hi], w_gate, w_up)
    rows = own.shape[0]
    relative = jnp.concatenate([first, second, third], axis=0).reshape(shards, rows, units)
    order = jnp.array([0, 1, 4, 2, 3, 5, 7, 6], jnp.int32)
    position = jnp.arange(shards, dtype=jnp.int32)
    other = (position // ring) ^ (place // ring)
    steps = (place % ring - position % ring) % ring
    hidden = relative[order[other * ring + steps]].reshape(shards * rows, units)
    everyone = jnp.broadcast_to(hidden[None], (ring, shards * rows, units))
    rings = [[start + z for z in range(ring)] for start in range(0, devs, ring)]
    everyone = lax.all_to_all(
        everyone, "dev", split_axis=0, concat_axis=0, tiled=True, axis_index_groups=rings
    )
    result = expert_down(
        everyone,
        [down[k, half] for k in range(ring) for half in range(split)],
        sources,
        groups,
    )
    result = lax.all_to_all(result, ("grp", "dev"), split_axis=0, concat_axis=0, tiled=True)
    return mix(slot_weight, result, ring)


def solution(mesh):
    placed = (
        P("grp", "dev"),
        P("grp", "dev"),
        P("dev", None, None),
        P(("grp", "dev"), None, None),
        P(("grp", "dev"), None, None),
        P(("grp", "dev")),
        P("dev", None, None),
        P("dev", None),
        P(),
        P(("grp", "dev"), None),
        P(("grp", "dev"), None),
        P(("grp", "dev"), None),
        P(("grp", "dev"), None, None),
        P(("grp", "dev"), None, None),
        P(("grp", "dev"), None, None),
    )
    return jax.shard_map(
        per_device, mesh=mesh, in_specs=placed, out_specs=P(("grp", "dev"), None), check_vma=False
    )
```

time: 283 us -> 239 us (0.84)
  blocking collectives: 64.6 us -> 0 us
  Pallas kernels: 8.96 us -> 38.2 us
  starting transfers between devices: 36 us -> 63.4 us
  matrix products: 19 us -> 0 us
  local copies, waits for them, and re-layouts: 24.1 us -> 10.6 us
  other arithmetic: 4.43 us -> 1.32 us
    all_to_all x3 -> x0, blocking collectives: 64.6 us -> none  [the longest x1 26.6 us: per_device(): lax.all_to_all(jnp.broadcast_to(hidden[None], (shards, shards * rows, uni...]
    ppermute x11, waiting for transfers between devices: 74 us -> 31.8 us  [send(): return lax.ppermute(value, 'dev', way)]
    all_to_all x1 -> x3, waiting for transfers between devices: 0.01 us -> 32.3 us  [the longest x1 14.9 us: per_device(): lax.all_to_all(outgoing, ('grp', 'dev'), split_axis=0, concat_axis=0, til...]
    pallas_call x0 -> x7, Pallas kernels: none -> 29 us  [the longest x1 7.08 us: attend(): pl.pallas_call(functools.partial(attend_kernel, heads, scale), grid=(requ...]
    dot_general x8 -> x0, matrix products: 19 us -> none  [the longest x1 5.49 us: per_device(): jnp.dot(head_values, w_out, preferred_element_type=F32).astype(BF16)]
    all_to_all x1 -> x3, starting transfers between devices: 4.63 us -> 17.4 us  [the longest x1 10.2 us: per_device(): lax.all_to_all(outgoing, ('grp', 'dev'), split_axis=0, concat_axis=0, til...]
    all_to_all x1, waiting for transfers between devices: 17.5 us -> 26.5 us  [per_device(): lax.all_to_all(result, ('grp', 'dev'), split_axis=0, concat_axis=0, tiled...]
    ppermute x0 -> x6, starting transfers between devices: none -> 8.46 us  [relay(): return lax.ppermute(down_out[k * split + half], 'dev', way)]
  transfers between devices with their start and end apart: 15 -> 23, of which waited for: 8 -> 13; matrix products, arithmetic and copies ran while one was open for 5% -> 1% of each run, Pallas kernels for 3% -> 10%
where the time goes in v2:
time: 239 us; the launch traced here: 238 us
  waiting for transfers between devices  124 us (52%)
  starting transfers between devices  63.4 us (27%)
  Pallas kernels  38.2 us (16%)
  local copies, waits for them, and re-layouts  10.6 us (4%)
    ppermute x11, waiting for transfers between devices, send(): return lax.ppermute(value, 'dev', way)  31.8 us
    all_to_all x1, waiting for transfers between devices, per_device(): lax.all_to_all(result, ('grp', 'dev'), split_axis=0, concat_axis=0, tiled...  26.5 us
    all_to_all x1, waiting for transfers between devices, per_device(): lax.all_to_all(partial.reshape(devs, requests, model_width), 'dev', split...  22.1 us
    all_to_all x1, waiting for transfers between devices, per_device(): lax.all_to_all(outgoing, ('grp', 'dev'), split_axis=0, concat_axis=0, til...  14.9 us
    all_to_all x1, starting transfers between devices, per_device(): lax.all_to_all(result, ('grp', 'dev'), split_axis=0, concat_axis=0, tiled...  12.6 us
    ppermute x11, starting transfers between devices, send(): return lax.ppermute(value, 'dev', way)  10.4 us
    all_to_all x1, starting transfers between devices, per_device(): lax.all_to_all(outgoing, ('grp', 'dev'), split_axis=0, concat_axis=0, til...  10.2 us
    all_to_all x1, waiting for transfers between devices, per_device(): lax.all_to_all(everyone, 'dev', split_axis=0, concat_axis=0, tiled=True,...  9.9 us
  transfers between devices with their start and end apart: 23, of which 13 were waited for; matrix products, arithmetic and copies ran while one was open for 1% of the time, Pallas kernels for 10%

profile of v2, /device:TPU:1, one launch (start us, length us, event | category | flops | bytes accessed | tf_op | source)
XLA Modules:
  0.0 238.1 jit_solution(15102797879618071081)
XLA Ops:
  0.0 2.3 shard_map.154
  2.3 8.6 %all-to-all-start = ((bf16[16,8,2304]{2,1,0:T(8,128)(2,1)}), bf16[16,8,2304]{2,1,0:T(8,128)(2,1)S(1)}, u32[]{:S(2)}, u32[]{:S(2)}) async-start(bf16[16,8,2304]{2,1,0:T(8,128)(2,1)} %bitcast.16), calls=%async_computation | async-start | bytes 1179648 | tf_op jit(solution)/shard_map/all_to_all | solution.py:446
  11.6 3.8 %shard_map.156 = (bf16[256,896]{1,0:T(8,128)(2,1)}, bf16[256,896]{1,0:T(8,128)(2,1)}, bf16[256,896]{1,0:T(8,128)(2,1)}, bf16[256,896]{1,0:T(8,128)(2,1)}, bf16[2...) custom-call(s32[8]{0:T(128)} %add.130.order_ref, ...), custom_call_target="tpu_custom_call" | custom-call | bytes 7340032 | tf_op jit(solution)/shard_map/pallas_call | solution.py:81
  18.2 3.8 %all-to-all-done.query_ref = bf16[16,8,2304]{2,1,0:T(8,128)(2,1)S(1)} async-done(((bf16[16,8,2304]{2,1,0:T(8,128)(2,1)}), bf16[16,8,2304]{2,1,0:T(8,128)(2,1)S(1)}, u32[]{:S(2)}, u32[]{:S(2)}) %all-to-all-start) | async-done | bytes 589856 | tf_op jit(solution)/shard_map/all_to_all | solution.py:446
  22.0 2.2 copy-done.3
  24.2 7.1 %shard_map.155 = bf16[16,8,2048]{2,1,0:T(8,128)(2,1)} custom-call(s32[8]{0:T(128)S(1)} %copy-done.6, bf16[16,8,2304]{2,1,0:T(8,128)(2,1)S(1)} %all-to-all-done.query_ref, bf16[8,512,512]{2,1,0:T(8,128)(2,1)S(1)} %copy-done.3, bf16[8,64,512]{2,1,0:T(8,128)(2,1)S(1)} %copy-done.4), custom_call_target="tpu_custom_call" | custom-call | flops 570425344 | bytes 4718592 | tf_op jit(solution)/shard_map/pallas_call | solution.py:243
  32.6 3.6 %all-to-all-start.1 = ((bf16[16,8,2048]{2,1,0:T(8,128)(2,1)}), bf16[16,8,2048]{2,1,0:T(8,128)(2,1)S(1)}, u32[]{:S(2)}, u32[]{:S(2)}) async-start(bf16[16,8,2048]{2,1,0:T(8,128)(2,1)} %shard_map.155), calls=%async_computation.1 | async-start | bytes 1048576 | tf_op jit(solution)/shard_map/all_to_all | solution.py:454
  38.9 7.5 %all-to-all-done.1 = bf16[16,8,2048]{2,1,0:T(8,128)(2,1)S(1)} async-done(((bf16[16,8,2048]{2,1,0:T(8,128)(2,1)}), bf16[16,8,2048]{2,1,0:T(8,128)(2,1)S(1)}, u32[]{:S(2)}, u32[]{:S(2)}) %all-to-all-start.1) | async-done | bytes 524320 | tf_op jit(solution)/shard_map/all_to_all | solution.py:454
  47.2 6.0 %shard_map.157 = bf16[128,7168]{1,0:T(8,128)(2,1)} custom-call(bf16[128,2048]{1,0:T(8,128)(2,1)} %bitcast.17, bf16[4,512,128]{2,1,0:T(8,128)(2,1)} %absorb_hbm.1, bf16[512,7168]{1,0:T(8,128)(2,1)} %weight_hbm.1), custom_call_target="tpu_custom_call" | custom-call | flops 1006632960 | bytes 9175040 | tf_op jit(solution)/shard_map/pallas_call | solution.py:301
  55.1 6.0 %all-to-all-start.2 = ((bf16[16,8,7168]{2,1,0:T(8,128)(2,1)}), bf16[16,8,7168]{2,1,0:T(8,128)(2,1)S(1)}, u32[]{:S(2)}, u32[]{:S(2)}) async-start(bf16[16,8,7168]{2,1,0:T(8,128)(2,1)} %bitcast.15), calls=%async_computation.2 | async-start | bytes 3670016 | tf_op jit(solution)/shard_map/all_to_all | solution.py:459
  61.9 22.1 %all-to-all-done.2.partial_ref = bf16[16,8,7168]{2,1,0:T(8,128)(2,1)S(1)} async-done(((bf16[16,8,7168]{2,1,0:T(8,128)(2,1)}), bf16[16,8,7168]{2,1,0:T(8,128)(2,1)S(1)}, u32[]{:S(2)}, u32[]{:S(2)}) %all-to-all-start.2) | async-done | bytes 1835040 | tf_op jit(solution)/shard_map/all_to_all | solution.py:459
  84.1 1.7 shard_map.158
  85.7 10.2 %all-to-all-start.3 = ((bf16[16,4,7168]{2,1,0:T(4,128)(2,1)}), bf16[16,4,7168]{2,1,0:T(4,128)(2,1)S(1)}, u32[]{:S(2)}, u32[]{:S(2)}) async-start(bf16[16,4,7168]{2,1,0:T(4,128)(2,1)} %shard_map.158), calls=%async_computation.3 | async-start | bytes 1835008 | tf_op jit(solution)/shard_map/all_to_all | solution.py:487
  97.0 1.8 collective-permute-start.5
  98.8 14.9 %all-to-all-done.3 = bf16[16,4,7168]{2,1,0:T(4,128)(2,1)S(1)} async-done(((bf16[16,4,7168]{2,1,0:T(4,128)(2,1)}), bf16[16,4,7168]{2,1,0:T(4,128)(2,1)S(1)}, u32[]{:S(2)}, u32[]{:S(2)}) %all-to-all-start.3) | async-done | bytes 917536 | tf_op jit(solution)/shard_map/all_to_all | solution.py:487
  114.0 5.4 %collective-permute-done.5.refs_5_ = bf16[256,896]{1,0:T(8,128)(2,1)S(1)} collective-permute-done((bf16[256,896]{1,0:T(8,128)(2,1)S(1)}, bf16[256,896]{1,0:T(8,128)(2,1)S(1)}, u32[]{:S(2)}, u32[]{:S(2)}) %collective-permute-start.5) | collective-permute-done | bytes 458784 | tf_op jit(solution)/shard_map/ppermute | solution.py:442
  120.4 2.4 %collective-permute-start.12 = (bf16[64,7168]{1,0:T(8,128)(2,1)S(1)}, bf16[64,7168]{1,0:T(8,128)(2,1)S(1)}, u32[]{:S(2)}, u32[]{:S(2)}) collective-permute-start(bf16[64,7168]{1,0:T(8,128)(2,1)S(1)} %reshape.167.refs_0_), channel_id=1, source_target_pairs={{0,3},{1,0},{2,1},{3,2},{4,7},{5,4},{6,5},{7,6},{8,11},{9,8},{10,9... | collective-permute-start | bytes 2752520 | tf_op jit(solution)/shard_map/ppermute | solution.py:502
  122.8 17.4 %collective-permute-done.6.refs_3_ = bf16[64,7168]{1,0:T(8,128)(2,1)S(1)} collective-permute-done((bf16[64,7168]{1,0:T(8,128)(2,1)S(1)}, bf16[64,7168]{1,0:T(8,128)(2,1)S(1)}, u32[]{:S(2)}, u32[]{:S(2)}) %collective-permute-start.6) | collective-permute-done | bytes 917536 | tf_op jit(solution)/shard_map/ppermute | solution.py:502
  140.7 2.4 %collective-permute-start.9 = (bf16[32,7168]{1,0:T(8,128)(2,1)S(1)}, bf16[32,7168]{1,0:T(8,128)(2,1)S(1)}, u32[]{:S(2)}, u32[]{:S(2)}) collective-permute-start(bf16[32,7168]{1,0:T(8,128)(2,1)S(1)} %get-tuple-element.93), channel_id=1, source_target_pairs={{0,3},{1,0},{2,1},{3,2},{4,7},{5,4},{6,5},{7,6},{8,11},{9,8},{10,9... | collective-permute-start | bytes 1376264 | tf_op jit(solution)/shard_map/ppermute | solution.py:502
  143.3 2.7 %collective-permute-start.14 = (bf16[32,7168]{1,0:T(8,128)(2,1)S(1)}, bf16[32,7168]{1,0:T(8,128)(2,1)S(1)}, u32[]{:S(2)}, u32[]{:S(2)}) collective-permute-start(bf16[32,7168]{1,0:T(8,128)(2,1)S(1)} %get-tuple-element.90), channel_id=1, source_target_pairs={{0,3},{1,0},{2,1},{3,2},{4,7},{5,4},{6,5},{7,6},{8,11},{9,8},{10,9... | collective-permute-start | bytes 1376264 | tf_op jit(solution)/shard_map/ppermute | solution.py:502
  146.3 5.4 %collective-permute-done.7.refs_2_ = bf16[32,7168]{1,0:T(8,128)(2,1)S(1)} collective-permute-done((bf16[32,7168]{1,0:T(8,128)(2,1)S(1)}, bf16[32,7168]{1,0:T(8,128)(2,1)S(1)}, u32[]{:S(2)}, u32[]{:S(2)}) %collective-permute-start.7) | collective-permute-done | bytes 458784 | tf_op jit(solution)/shard_map/ppermute | solution.py:502
  151.7 1.8 collective-permute-start.16
  153.5 8.1 %collective-permute-done.13.refs_0_ = bf16[32,7168]{1,0:T(8,128)(2,1)S(1)} collective-permute-done((bf16[32,7168]{1,0:T(8,128)(2,1)S(1)}, bf16[32,7168]{1,0:T(8,128)(2,1)S(1)}, u32[]{:S(2)}, u32[]{:S(2)}) %collective-permute-start.13) | collective-permute-done | bytes 458784 | tf_op jit(solution)/shard_map/ppermute | solution.py:502
  161.6 2.0 copy-done.1
  163.6 3.6 %shard_map.159 = bf16[256,256]{1,0:T(8,128)(2,1)S(1)} custom-call(bf16[64,7168]{1,0:T(8,128)(2,1)S(1)} %reshape.167.refs_0_, bf16[64,7168]{1,0:T(8,128)(2,1)S(1)} %collective-permute-done.11.refs_1_, bf16[64,7168]{1,0:T(8,128)(2,1)S(1)} %collective-permute-done.12.refs_2_, bf16[64,7168]{1,0:T(8,128)(2,1)S(1)} %collective-permute-done.6.refs_3_, ...), custom_call_target="tpu_custom_call" | custom-call | flops 1879048192 | bytes 11010048 | tf_op jit(solution)/shard_map/pallas_call | solution.py:40
  167.3 3.2 %shard_map.160 = bf16[192,256]{1,0:T(8,128)(2,1)S(1)} custom-call(bf16[32,7168]{1,0:T(8,128)(2,1)S(1)} %collective-permute-done.13.refs_0_, bf16[32,7168]{1,0:T(8,128)(2,1)S(1)} %collective-permute-done.14.refs_1_, bf16[32,7168]{1,0:T(8,128)(2,1)S(1)} %collective-permute-done.7.refs_2_, bf16[32,7168]{1,0:T(8,128)(2,1)S(1)} %collective-permute-done.15.refs_3_, ...), custom_call_target="tpu_custom_call" | custom-call | flops 1409286144 | bytes 10092544 | tf_op jit(solution)/shard_map/pallas_call | solution.py:40
  171.4 2.4 shard_map.161
  175.4 3.7 %all-to-all-start.4 = ((bf16[4,512,256]{2,1,0:T(8,128)(2,1)}), bf16[4,512,256]{2,1,0:T(8,128)(2,1)S(1)}, u32[]{:S(2)}, u32[]{:S(2)}) async-start(bf16[4,512,256]{2,1,0:T(8,128)(2,1)} %broadcast_in_dim.50), calls=%async_computation.4 | async-start | bytes 2097152 | tf_op jit(solution)/shard_map/all_to_all | solution.py:534
  179.6 9.9 %all-to-all-done.4.hidden_ref = bf16[4,512,256]{2,1,0:T(8,128)(2,1)S(1)} async-done(((bf16[4,512,256]{2,1,0:T(8,128)(2,1)}), bf16[4,512,256]{2,1,0:T(8,128)(2,1)S(1)}, u32[]{:S(2)}, u32[]{:S(2)}) %all-to-all-start.4) | async-done | bytes 1048608 | tf_op jit(solution)/shard_map/all_to_all | solution.py:534
  190.5 6.6 %shard_map.162 = bf16[128,4,1792]{2,1,0:T(4,128)(2,1)} custom-call(s32[4]{0:T(128)} %and_select_fusion.4.order_ref, bf16[4,512,256]{2,1,0:T(8,128)(2,1)} %copy-done.9, bf16[256,896]{1,0:T(8,128)(2,1)} %get-tuple-element.81.refs_0_, bf16[256,896]{1,0:T(8,128)(2,1)} %get-tuple-element.82.refs_1_, bf16[256,896]{1,0:T(8,128)(2,1)} %copy-done.13, ...), custom_call_target="tpu_custom_call" | custom-call | flops 1879048192 | bytes 6553600 | tf_op jit(solution)/shard_map/pallas_call | solution.py:136
  197.2 12.6 %all-to-all-start.5 = ((bf16[128,4,1792]{2,1,0:T(4,128)(2,1)}), bf16[128,4,1792]{2,1,0:T(4,128)(2,1)S(1)}, u32[]{:S(2)}, u32[]{:S(2)}) async-start(bf16[128,4,1792]{2,1,0:T(4,128)(2,1)} %shard_map.162), calls=%async_computation.5 | async-start | bytes 3670016 | tf_op jit(solution)/shard_map/all_to_all | solution.py:543
  210.0 26.5 %all-to-all-done.5.rows_ref = bf16[128,4,1792]{2,1,0:T(4,128)(2,1)S(1)} async-done(((bf16[128,4,1792]{2,1,0:T(4,128)(2,1)}), bf16[128,4,1792]{2,1,0:T(4,128)(2,1)S(1)}, u32[]{:S(2)}, u32[]{:S(2)}) %all-to-all-start.5) | async-done | bytes 1835040 | tf_op jit(solution)/shard_map/all_to_all | solution.py:543
  (99 shorter events, 20.3 us)
Async XLA Ops:
  2.3 19.6 %all-to-all-start = ((bf16[16,8,2304]{2,1,0:T(8,128)(2,1)}), bf16[16,8,2304]{2,1,0:T(8,128)(2,1)S(1)}, u32[]{:S(2)}, u32[]{:S(2)}) async-start(bf16[16,8,2304]{2,1,0:T(8,128)(2,1)} %bitcast.16), calls=%async_computation | async-start | bytes 1179648 | tf_op jit(solution)/shard_map/all_to_all | solution.py:446
  15.4 17.1 %collective-permute-start = (bf16[256,896]{1,0:T(8,128)(2,1)}, bf16[256,896]{1,0:T(8,128)(2,1)S(1)}, u32[]{:S(2)}, u32[]{:S(2)}) collective-permute-start(bf16[256,896]{1,0:T(8,128)(2,1)} %get-tuple-element.49), channel_id=1, source_target_pairs={{0,1},{1,2},{2,3},{3,0},{4,5},{5,6},{6,7},{7,4},{8,9},{9,10},{10,1... | collective-permute-start | bytes 1376264 | tf_op jit(solution)/shard_map/ppermute | solution.py:442
  16.8 15.7 %collective-permute-start.1 = (bf16[256,896]{1,0:T(8,128)(2,1)}, bf16[256,896]{1,0:T(8,128)(2,1)S(1)}, u32[]{:S(2)}, u32[]{:S(2)}) collective-permute-start(bf16[256,896]{1,0:T(8,128)(2,1)} %get-tuple-element.50), channel_id=1, source_target_pairs={{0,3},{1,0},{2,1},{3,2},{4,7},{5,4},{6,5},{7,6},{8,11},{9,8},{10,9... | collective-permute-start | bytes 1376264 | tf_op jit(solution)/shard_map/ppermute | solution.py:442
  32.6 13.8 %all-to-all-start.1 = ((bf16[16,8,2048]{2,1,0:T(8,128)(2,1)}), bf16[16,8,2048]{2,1,0:T(8,128)(2,1)S(1)}, u32[]{:S(2)}, u32[]{:S(2)}) async-start(bf16[16,8,2048]{2,1,0:T(8,128)(2,1)} %shard_map.155), calls=%async_computation.1 | async-start | bytes 1048576 | tf_op jit(solution)/shard_map/all_to_all | solution.py:454
  36.2 18.1 %collective-permute-start.2 = (bf16[256,896]{1,0:T(8,128)(2,1)S(1)}, bf16[256,896]{1,0:T(8,128)(2,1)S(1)}, u32[]{:S(2)}, u32[]{:S(2)}) collective-permute-start(bf16[256,896]{1,0:T(8,128)(2,1)S(1)} %copy-done.21), channel_id=1, source_target_pairs={{0,1},{1,2},{2,3},{3,0},{4,5},{5,6},{6,7},{7,4},{8,9},{9,10},{10,1... | collective-permute-start | bytes 1376264 | tf_op jit(solution)/shard_map/ppermute | solution.py:442
  37.5 16.8 %collective-permute-start.3 = (bf16[256,896]{1,0:T(8,128)(2,1)S(1)}, bf16[256,896]{1,0:T(8,128)(2,1)S(1)}, u32[]{:S(2)}, u32[]{:S(2)}) collective-permute-start(bf16[256,896]{1,0:T(8,128)(2,1)S(1)} %copy-done.20), channel_id=1, source_target_pairs={{0,3},{1,0},{2,1},{3,2},{4,7},{5,4},{6,5},{7,6},{8,11},{9,8},{10,9... | collective-permute-start | bytes 1376264 | tf_op jit(solution)/shard_map/ppermute | solution.py:442
  53.2 30.8 %copy-start.5 = (f32[7168]{0:T(1024)S(1)}, f32[7168]{0:T(1024)}, u32[]{:S(2)}) copy-start(f32[7168]{0:T(1024)} %param.24) | copy-start | bytes 86020
  54.2 31.5 %copy-start.15 = (bf16[256,896]{1,0:T(8,128)(2,1)}, bf16[256,896]{1,0:T(8,128)(2,1)S(1)}, u32[]{:S(2)}) copy-start(bf16[256,896]{1,0:T(8,128)(2,1)S(1)} %collective-permute-done.2.refs_3_) | copy-start | bytes 1376260
  54.2 42.8 %copy-start.19 = (bf16[256,896]{1,0:T(8,128)(2,1)S(1)}, bf16[256,896]{1,0:T(8,128)(2,1)}, u32[]{:S(2)}) copy-start(bf16[256,896]{1,0:T(8,128)(2,1)} %get-tuple-element.73) | copy-start | bytes 1376260
  55.1 29.0 %all-to-all-start.2 = ((bf16[16,8,7168]{2,1,0:T(8,128)(2,1)}), bf16[16,8,7168]{2,1,0:T(8,128)(2,1)S(1)}, u32[]{:S(2)}, u32[]{:S(2)}) async-start(bf16[16,8,7168]{2,1,0:T(8,128)(2,1)} %bitcast.15), calls=%async_computation.2 | async-start | bytes 3670016 | tf_op jit(solution)/shard_map/all_to_all | solution.py:459
  61.1 58.3 %copy-start.7 = (s32[8]{0:T(128)S(1)}, s32[8]{0:T(128)}, u32[]{:S(2)}) copy-start(s32[8]{0:T(128)} %constant.105.clone) | copy-start | bytes 100
  85.7 28.0 %all-to-all-start.3 = ((bf16[16,4,7168]{2,1,0:T(4,128)(2,1)}), bf16[16,4,7168]{2,1,0:T(4,128)(2,1)S(1)}, u32[]{:S(2)}, u32[]{:S(2)}) async-start(bf16[16,4,7168]{2,1,0:T(4,128)(2,1)} %shard_map.158), calls=%async_computation.3 | async-start | bytes 1835008 | tf_op jit(solution)/shard_map/all_to_all | solution.py:487
  95.9 18.1 %collective-permute-start.4 = (bf16[256,896]{1,0:T(8,128)(2,1)}, bf16[256,896]{1,0:T(8,128)(2,1)S(1)}, u32[]{:S(2)}, u32[]{:S(2)}) collective-permute-start(bf16[256,896]{1,0:T(8,128)(2,1)} %get-tuple-element.72), channel_id=1, source_target_pairs={{0,2},{1,3},{2,0},{3,1},{4,6},{5,7},{6,4},{7,5},{8,10},{9,11},{10,... | collective-permute-start | bytes 1376264 | tf_op jit(solution)/shard_map/ppermute | solution.py:442
  97.0 22.3 %collective-permute-start.5 = (bf16[256,896]{1,0:T(8,128)(2,1)S(1)}, bf16[256,896]{1,0:T(8,128)(2,1)S(1)}, u32[]{:S(2)}, u32[]{:S(2)}) collective-permute-start(bf16[256,896]{1,0:T(8,128)(2,1)S(1)} %copy-done.19), channel_id=1, source_target_pairs={{0,2},{1,3},{2,0},{3,1},{4,6},{5,7},{6,4},{7,5},{8,10},{9,11},{10,... | collective-permute-start | bytes 1376264 | tf_op jit(solution)/shard_map/ppermute | solution.py:442
  114.0 53.2 %copy-start.17 = (bf16[256,896]{1,0:T(8,128)(2,1)}, bf16[256,896]{1,0:T(8,128)(2,1)S(1)}, u32[]{:S(2)}) copy-start(bf16[256,896]{1,0:T(8,128)(2,1)S(1)} %collective-permute-done.4.refs_4_) | copy-start | bytes 1376260
  119.4 47.9 %copy-start.18 = (bf16[256,896]{1,0:T(8,128)(2,1)}, bf16[256,896]{1,0:T(8,128)(2,1)S(1)}, u32[]{:S(2)}) copy-start(bf16[256,896]{1,0:T(8,128)(2,1)S(1)} %collective-permute-done.5.refs_5_) | copy-start | bytes 1376260
  119.4 20.9 %collective-permute-start.6 = (bf16[64,7168]{1,0:T(8,128)(2,1)S(1)}, bf16[64,7168]{1,0:T(8,128)(2,1)S(1)}, u32[]{:S(2)}, u32[]{:S(2)}) collective-permute-start(bf16[64,7168]{1,0:T(8,128)(2,1)S(1)} %reshape.167.refs_0_), channel_id=1, source_target_pairs={{0,4},{1,5},{2,6},{3,7},{4,0},{5,1},{6,2},{7,3},{8,12},{9,13},{10,... | collective-permute-start | bytes 2752520 | tf_op jit(solution)/shard_map/ppermute | solution.py:502
  120.1 41.5 %copy-start = (bf16[1,7168,256]{2,1,0:T(8,128)(2,1)S(1)}, bf16[1,7168,256]{2,1,0:T(8,128)(2,1)}, u32[]{:S(2)}) copy-start(bf16[1,7168,256]{2,1,0:T(8,128)(2,1)} %refs_2_.1) | copy-start | bytes 11010052
  120.1 23.0 %collective-permute-start.11 = (bf16[64,7168]{1,0:T(8,128)(2,1)S(1)}, bf16[64,7168]{1,0:T(8,128)(2,1)S(1)}, u32[]{:S(2)}, u32[]{:S(2)}) collective-permute-start(bf16[64,7168]{1,0:T(8,128)(2,1)S(1)} %reshape.167.refs_0_), channel_id=1, source_target_pairs={{0,1},{1,2},{2,3},{3,0},{4,5},{5,6},{6,7},{7,4},{8,9},{9,10},{10,1... | collective-permute-start | bytes 2752520 | tf_op jit(solution)/shard_map/ppermute | solution.py:502
  120.4 22.8 %collective-permute-start.12 = (bf16[64,7168]{1,0:T(8,128)(2,1)S(1)}, bf16[64,7168]{1,0:T(8,128)(2,1)S(1)}, u32[]{:S(2)}, u32[]{:S(2)}) collective-permute-start(bf16[64,7168]{1,0:T(8,128)(2,1)S(1)} %reshape.167.refs_0_), channel_id=1, source_target_pairs={{0,3},{1,0},{2,1},{3,2},{4,7},{5,4},{6,5},{7,6},{8,11},{9,8},{10,9... | collective-permute-start | bytes 2752520 | tf_op jit(solution)/shard_map/ppermute | solution.py:502
  140.3 11.4 %collective-permute-start.7 = (bf16[32,7168]{1,0:T(8,128)(2,1)S(1)}, bf16[32,7168]{1,0:T(8,128)(2,1)S(1)}, u32[]{:S(2)}, u32[]{:S(2)}) collective-permute-start(bf16[32,7168]{1,0:T(8,128)(2,1)S(1)} %get-tuple-element.94), channel_id=1, source_target_pairs={{0,1},{1,2},{2,3},{3,0},{4,5},{5,6},{6,7},{7,4},{8,9},{9,10},{10,1... | collective-permute-start | bytes 1376264 | tf_op jit(solution)/shard_map/ppermute | solution.py:502
  140.7 12.8 %collective-permute-start.9 = (bf16[32,7168]{1,0:T(8,128)(2,1)S(1)}, bf16[32,7168]{1,0:T(8,128)(2,1)S(1)}, u32[]{:S(2)}, u32[]{:S(2)}) collective-permute-start(bf16[32,7168]{1,0:T(8,128)(2,1)S(1)} %get-tuple-element.93), channel_id=1, source_target_pairs={{0,3},{1,0},{2,1},{3,2},{4,7},{5,4},{6,5},{7,6},{8,11},{9,8},{10,9... | collective-permute-start | bytes 1376264 | tf_op jit(solution)/shard_map/ppermute | solution.py:502
  143.1 18.4 %collective-permute-start.13 = (bf16[32,7168]{1,0:T(8,128)(2,1)S(1)}, bf16[32,7168]{1,0:T(8,128)(2,1)S(1)}, u32[]{:S(2)}, u32[]{:S(2)}) collective-permute-start(bf16[32,7168]{1,0:T(8,128)(2,1)S(1)} %get-tuple-element.92), channel_id=1, source_target_pairs={{0,1},{1,2},{2,3},{3,0},{4,5},{5,6},{6,7},{7,4},{8,9},{9,10},{10,1... | collective-permute-start | bytes 1376264 | tf_op jit(solution)/shard_map/ppermute | solution.py:502
  143.3 24.0 %collective-permute-start.14 = (bf16[32,7168]{1,0:T(8,128)(2,1)S(1)}, bf16[32,7168]{1,0:T(8,128)(2,1)S(1)}, u32[]{:S(2)}, u32[]{:S(2)}) collective-permute-start(bf16[32,7168]{1,0:T(8,128)(2,1)S(1)} %get-tuple-element.90), channel_id=1, source_target_pairs={{0,3},{1,0},{2,1},{3,2},{4,7},{5,4},{6,5},{7,6},{8,11},{9,8},{10,9... | collective-permute-start | bytes 1376264 | tf_op jit(solution)/shard_map/ppermute | solution.py:502
  146.0 21.3 %collective-permute-start.15 = (bf16[32,7168]{1,0:T(8,128)(2,1)S(1)}, bf16[32,7168]{1,0:T(8,128)(2,1)S(1)}, u32[]{:S(2)}, u32[]{:S(2)}) collective-permute-start(bf16[32,7168]{1,0:T(8,128)(2,1)S(1)} %get-tuple-element.91), channel_id=1, source_target_pairs={{0,4},{1,5},{2,6},{3,7},{4,0},{5,1},{6,2},{7,3},{8,12},{9,13},{10,... | collective-permute-start | bytes 1376264 | tf_op jit(solution)/shard_map/ppermute | solution.py:502
  151.7 15.6 %collective-permute-start.16 = (bf16[32,7168]{1,0:T(8,128)(2,1)S(1)}, bf16[32,7168]{1,0:T(8,128)(2,1)S(1)}, u32[]{:S(2)}, u32[]{:S(2)}) collective-permute-start(bf16[32,7168]{1,0:T(8,128)(2,1)S(1)} %get-tuple-element.89), channel_id=1, source_target_pairs={{0,4},{1,5},{2,6},{3,7},{4,0},{5,1},{6,2},{7,3},{8,12},{9,13},{10,... | collective-permute-start | bytes 1376264 | tf_op jit(solution)/shard_map/ppermute | solution.py:502
  153.5 17.9 %collective-permute-start.8 = (bf16[32,7168]{1,0:T(8,128)(2,1)S(1)}, bf16[32,7168]{1,0:T(8,128)(2,1)S(1)}, u32[]{:S(2)}, u32[]{:S(2)}) collective-permute-start(bf16[32,7168]{1,0:T(8,128)(2,1)S(1)} %collective-permute-done.7.refs_2_), channel_id=1, source_target_pairs={{0,1},{1,2},{2,3},{3,0},{4,5},{5,6},{6,7},{7,4},{8,9},{9,10},{10,1... | collective-permute-start | bytes 1376264 | tf_op jit(solution)/shard_map/ppermute | solution.py:502
  161.5 9.8 %collective-permute-start.10 = (bf16[32,7168]{1,0:T(8,128)(2,1)S(1)}, bf16[32,7168]{1,0:T(8,128)(2,1)S(1)}, u32[]{:S(2)}, u32[]{:S(2)}) collective-permute-start(bf16[32,7168]{1,0:T(8,128)(2,1)S(1)} %collective-permute-done.9.refs_5_), channel_id=1, source_target_pairs={{0,3},{1,0},{2,1},{3,2},{4,7},{5,4},{6,5},{7,6},{8,11},{9,8},{10,9... | collective-permute-start | bytes 1376264 | tf_op jit(solution)/shard_map/ppermute | solution.py:502
  175.4 14.1 %all-to-all-start.4 = ((bf16[4,512,256]{2,1,0:T(8,128)(2,1)}), bf16[4,512,256]{2,1,0:T(8,128)(2,1)S(1)}, u32[]{:S(2)}, u32[]{:S(2)}) async-start(bf16[4,512,256]{2,1,0:T(8,128)(2,1)} %broadcast_in_dim.50), calls=%async_computation.4 | async-start | bytes 2097152 | tf_op jit(solution)/shard_map/all_to_all | solution.py:534
  179.6 30.1 %copy-start.11 = (f32[8,8]{1,0:T(8,128)S(1)}, f32[8,8]{1,0:T(8,128)}, u32[]{:S(2)}) copy-start(f32[8,8]{1,0:T(8,128)} %param.27) | copy-start | bytes 772
  179.6 30.3 %copy-start.12 = (f32[8,4]{0,1:T(4,128)S(1)}, f32[8,4]{0,1:T(4,128)}, u32[]{:S(2)}) copy-start(f32[8,4]{0,1:T(4,128)} %param.26) | copy-start | bytes 388
  197.2 39.3 %all-to-all-start.5 = ((bf16[128,4,1792]{2,1,0:T(4,128)(2,1)}), bf16[128,4,1792]{2,1,0:T(4,128)(2,1)S(1)}, u32[]{:S(2)}, u32[]{:S(2)}) async-start(bf16[128,4,1792]{2,1,0:T(4,128)(2,1)} %shard_map.162), calls=%async_computation.5 | async-start | bytes 3670016 | tf_op jit(solution)/shard_map/all_to_all | solution.py:543
  (13 other events, 129.3 us)

commit v3 on v2

--- a/solution.py
+++ b/solution.py
@@ -54,37 +54,42 @@
     )(*blocks, w_gate, w_up)
 
 
-def relay_kernel(count, order_ref, weight_ref, *refs):
+def relay_kernel(layout, ring, weight_ref, *refs):
+    count = len(layout)
+    width = weight_ref.shape[2] // (2 * ring)
+    place = lax.axis_index("dev") % ring
     out_refs, held, in_sems, out_sems = refs[:count], *refs[count:]
-    width = out_refs[0].shape[1]
-    arriving, leaving = [], []
+    arriving, leaving, offset = [], [], 0
     for k in range(count):
-        start = pl.multiple_of(order_ref[k] * width, 128)
-        copy = pltpu.make_async_copy(
-            weight_ref.at[0, :, pl.ds(start, width)], held.at[k], in_sems.at[k]
+        size = out_refs[k].shape[1]
+        part = held.at[:, pl.ds(offset, size)]
+        block, half = layout[k]
+        target = (place + block) % ring
+        start = pl.multiple_of((2 * target + half) * width, 128)
+        arriving.append(
+            pltpu.make_async_copy(weight_ref.at[0, :, pl.ds(start, size)], part, in_sems.at[k])
         )
+        leaving.append(pltpu.make_async_copy(part, out_refs[k], out_sems.at[k]))
+        offset += size
+    for copy in arriving:
         copy.start()
-        arriving.append(copy)
     for k in range(count):
         arriving[k].wait()
-        copy = pltpu.make_async_copy(held.at[k], out_refs[k], out_sems.at[k])
-        copy.start()
-        leaving.append(copy)
+        leaving[k].start()
     for copy in leaving:
         copy.wait()
 
 
-def column_blocks(weight, order):
+def column_blocks(weight, layout, ring, widths):
     _, rows, columns = weight.shape
-    count = order.shape[0]
-    width = columns // count
-    return pl.pallas_call(
-        functools.partial(relay_kernel, count),
-        out_shape=[jax.ShapeDtypeStruct((rows, width), weight.dtype)] * count,
-        in_specs=[pl.BlockSpec(memory_space=pltpu.SMEM), pl.BlockSpec(memory_space=pl.ANY)],
-        out_specs=[pl.BlockSpec(memory_space=pl.ANY)] * count,
+    count = len(widths)
+    return pl.pallas_call(
+        functools.partial(relay_kernel, layout, ring),
+        out_shape=[jax.ShapeDtypeStruct((rows, width), weight.dtype) for width in widths],
+        in_specs=[pl.BlockSpec(memory_space=pltpu.HBM)],
+        out_specs=[pl.BlockSpec(memory_space=pltpu.HBM)] * count,
         scratch_shapes=[
-            pltpu.VMEM((count, rows, width), weight.dtype),
+            pltpu.VMEM((rows, columns), weight.dtype),
             pltpu.SemaphoreType.DMA((count,)),
             pltpu.SemaphoreType.DMA((count,)),
         ],
@@ -92,67 +97,74 @@
         cost_estimate=pl.CostEstimate(
             flops=0, bytes_accessed=4 * rows * columns, transcendentals=0
         ),
-    )(order, weight)
-
-
-def down_kernel(groups, order_ref, hidden_ref, *refs):
+    )(weight)
+
+
+def down_kernel(groups, layout, hidden_ref, *refs):
     ring, total, units = hidden_ref.shape
-    pieces = len(refs) - 3
-    down_refs, out_ref, down, sems = refs[:pieces], *refs[pieces:]
-    width = down_refs[0].shape[1]
-    share = pieces // ring
-    copies = [
+    count = len(layout)
+    down_refs, out_ref, hidden, down, hidden_sems, sems = refs[:count], *refs[count:]
+    halves = sems.shape[0]
+    width = out_ref.shape[2] // halves
+    place = lax.axis_index("dev") % ring
+    hidden_copies = [
         pltpu.make_async_copy(
-            down_refs[i],
-            down.at[pl.ds(i // share * units, units), pl.ds(i % share * width, width)],
-            sems.at[i],
+            hidden_ref.at[(place + ring - k) % ring],
+            hidden.at[:, pl.ds(k * units, units)],
+            hidden_sems.at[k],
         )
-        for i in range(pieces)
+        for k in range(ring)
     ]
-    for copy in copies:
+    down_copies = [[] for _ in range(halves)]
+    for ref, (k, first) in zip(down_refs, layout):
+        for half in range(first, first + ref.shape[1] // width):
+            down_copies[half].append(
+                pltpu.make_async_copy(
+                    ref.at[:, pl.ds((half - first) * width, width)],
+                    down.at[pl.ds(k * units, units), pl.ds(half * width, width)],
+                    sems.at[half, k],
+                )
+            )
+    for copy in hidden_copies + [copy for part in down_copies for copy in part]:
         copy.start()
-    for copy in copies:
+    for copy in hidden_copies:
         copy.wait()
     peers = groups * EXP_GRP
     rows = peers * CAP
     places = total // rows
-    parts = 2
-    tall = total // parts
-    for part in range(parts):
-        hidden = jnp.concatenate(
-            [hidden_ref[order_ref[k], part * tall : (part + 1) * tall] for k in range(ring)],
-            axis=1,
-        )
-        value = jnp.dot(hidden, down[...], preferred_element_type=F32).astype(BF16)
-        for place in range(places // parts):
+    for half in range(halves):
+        for copy in down_copies[half]:
+            copy.wait()
+        columns = slice(half * width, (half + 1) * width)
+        value = jnp.dot(hidden[...], down[:, columns], preferred_element_type=F32).astype(BF16)
+        for place in range(places):
             for peer in range(peers):
                 row = place * rows + peer * CAP
-                out_ref[peer * places + part * (places // parts) + place] = value[row : row + CAP]
-
-
-def expert_down(hidden, down, order, groups):
+                out_ref[peer * places + place, :, columns] = value[row : row + CAP]
+
+
+def expert_down(hidden, down, layout, groups, halves):
     ring, rows, units = hidden.shape
-    width = down[0].shape[1] * len(down) // ring
-    return pl.pallas_call(
-        functools.partial(down_kernel, groups),
+    width = sum(piece.shape[1] for piece in down) // ring
+    return pl.pallas_call(
+        functools.partial(down_kernel, groups, layout),
         out_shape=jax.ShapeDtypeStruct((rows // CAP, CAP, width), BF16),
-        in_specs=[
-            pl.BlockSpec(memory_space=pltpu.SMEM),
-            pl.BlockSpec(memory_space=pltpu.VMEM),
-        ]
-        + [pl.BlockSpec(memory_space=pl.ANY)] * len(down),
+        in_specs=[pl.BlockSpec(memory_space=pltpu.VMEM)]
+        + [pl.BlockSpec(memory_space=pltpu.HBM)] * len(down),
         out_specs=pl.BlockSpec(memory_space=pltpu.VMEM),
         scratch_shapes=[
+            pltpu.VMEM((rows, ring * units), BF16),
             pltpu.VMEM((ring * units, width), BF16),
-            pltpu.SemaphoreType.DMA((len(down),)),
-        ],
-        compiler_params=pltpu.CompilerParams(vmem_limit_bytes=LIMIT),
+            pltpu.SemaphoreType.DMA((ring,)),
+            pltpu.SemaphoreType.DMA((halves, ring)),
+        ],
+        compiler_params=pltpu.CompilerParams(vmem_limit_bytes=24 * 1024 * 1024),
         cost_estimate=pl.CostEstimate(
             flops=2 * ring * rows * units * width,
             bytes_accessed=2 * (ring * units * (rows + width) + rows * width),
             transcendentals=0,
         ),
-    )(order, hidden, *down)
+    )(hidden, *down)
 
 
 def absorb_kernel(nope_ref, rope_ref, weight_ref, out_ref, nope, rope, weight, sems):
@@ -182,7 +194,7 @@
     return pl.pallas_call(
         absorb_kernel,
         out_shape=jax.ShapeDtypeStruct((rows, columns), BF16),
-        in_specs=[pl.BlockSpec(memory_space=pl.ANY)] * 3,
+        in_specs=[pl.BlockSpec(memory_space=pltpu.HBM)] * 3,
         out_specs=pl.BlockSpec(memory_space=pltpu.VMEM),
         scratch_shapes=[
             pltpu.VMEM(q_nope.shape, BF16),
@@ -199,84 +211,109 @@
     )(q_nope, q_rope, w_absorb_k)
 
 
-def attend_kernel(heads, scale, length_ref, query_ref, cache_ref, keys_ref, out_ref, wide, total):
-    request = pl.program_id(0)
-    devs = query_ref.shape[0]
+def attend_kernel(heads, scale, length_ref, query_ref, cache_hbm, keys_hbm, weight_hbm, *refs):
+    out_ref, weight_ref, cache_ref, keys_ref, queries, values, sems = refs
+    devs, requests, columns = query_ref.shape
+    rope = keys_ref.shape[1]
     latent = cache_ref.shape[2]
-    rope = keys_ref.shape[1]
-
-    @pl.when(request == 0)
-    def _():
-        wide[...] = query_ref[...].astype(F32)
-
-    query = wide[:, pl.ds(request, 1), :].reshape(devs, wide.shape[2]).astype(BF16)
+    rows = devs * requests
+    keys_copy = pltpu.make_async_copy(keys_hbm, keys_ref, sems.at[requests])
+    cache_copies = [
+        pltpu.make_async_copy(cache_hbm.at[r], cache_ref.at[r], sems.at[r])
+        for r in range(requests)
+    ]
+    keys_copy.start()
+    for copy in cache_copies:
+        copy.start()
+    weight_copy = pltpu.make_async_copy(weight_hbm, weight_ref, sems.at[requests + 1])
+    weight_copy.start()
+    row = lax.broadcasted_iota(jnp.int32, (rows, rows), 0)
+    column = lax.broadcasted_iota(jnp.int32, (rows, rows), 1)
+    by_request = (column == row % devs * requests + row // devs).astype(BF16)
+    by_device = (column == row % requests * devs + row // requests).astype(BF16)
+    queries[...] = jnp.dot(
+        by_request, query_ref[...].reshape(rows, columns), preferred_element_type=F32
+    ).astype(BF16)
     split = heads * latent
-    parts = [query[:, h * latent : (h + 1) * latent] for h in range(heads)]
-    ropes = [query[:, split + h * rope : split + (h + 1) * rope] for h in range(heads)]
-    cache = cache_ref[0]
-    scores = lax.dot_general(
-        jnp.concatenate(parts, axis=0),
-        cache,
-        (((1,), (1,)), ((), ())),
-        preferred_element_type=F32,
-    )
-    scores += jnp.dot(jnp.concatenate(ropes, axis=0), keys_ref[0], preferred_element_type=F32)
-    scores *= scale
-    live = lax.broadcasted_iota(jnp.int32, scores.shape, 1) < length_ref[request]
-    scores = jnp.where(live, scores, -jnp.inf)
-    exponent = jnp.exp(scores - jnp.max(scores, axis=1, keepdims=True))
-    probs = (exponent / jnp.sum(exponent, axis=1, keepdims=True)).astype(BF16)
-    value = jnp.dot(probs, cache, preferred_element_type=F32)
-    value = jnp.concatenate([value[h * devs : (h + 1) * devs] for h in range(heads)], axis=1)
-    total[:, pl.ds(request, 1), :] = value.reshape(devs, 1, split)
-
-    @pl.when(request == pl.num_programs(0) - 1)
-    def _():
-        out_ref[...] = total[...].astype(BF16)
-
-
-def attend(query, latent_cache, rope_keys, lengths, heads, scale):
+    keys_copy.wait()
+    group = 4
+    for first in range(0, requests, group):
+        members = range(first, first + group)
+        for r in members:
+            cache_copies[r].wait()
+        scores = []
+        for r in members:
+            mine = slice(r * devs, (r + 1) * devs)
+            latents = jnp.concatenate(
+                [queries[mine, h * latent : (h + 1) * latent] for h in range(heads)], axis=0
+            )
+            ropes = jnp.concatenate(
+                [queries[mine, split + h * rope : split + (h + 1) * rope] for h in range(heads)],
+                axis=0,
+            )
+            scores.append(
+                lax.dot_general(
+                    latents, cache_ref[r], (((1,), (1,)), ((), ())), preferred_element_type=F32
+                )
+                + jnp.dot(ropes, keys_ref[r], preferred_element_type=F32)
+            )
+        probs = []
+        for r, score in zip(members, scores):
+            live = lax.broadcasted_iota(jnp.int32, score.shape, 1) < length_ref[r]
+            score = jnp.where(live, score * scale, -jnp.inf)
+            exponent = jnp.exp(score - jnp.max(score, axis=1, keepdims=True))
+            probs.append((exponent / jnp.sum(exponent, axis=1, keepdims=True)).astype(BF16))
+        for r, prob in zip(members, probs):
+            value = jnp.dot(prob, cache_ref[r], preferred_element_type=F32).astype(BF16)
+            for h in range(heads):
+                values[r * devs : (r + 1) * devs, h * latent : (h + 1) * latent] = value[
+                    h * devs : (h + 1) * devs
+                ]
+    out_ref[...] = (
+        jnp.dot(by_device, values[...], preferred_element_type=F32)
+        .astype(BF16)
+        .reshape(out_ref.shape)
+    )
+    weight_copy.wait()
+
+
+def attend(query, latent_cache, rope_keys, lengths, w_out, heads, scale):
     devs, requests, columns = query.shape
     _, rope, positions = rope_keys.shape
     latent = latent_cache.shape[2]
     rows = heads * devs
     return pl.pallas_call(
         functools.partial(attend_kernel, heads, scale),
-        grid=(requests,),
-        out_shape=jax.ShapeDtypeStruct((devs, requests, heads * latent), BF16),
+        out_shape=[
+            jax.ShapeDtypeStruct((devs, requests, heads * latent), BF16),
+            jax.ShapeDtypeStruct(w_out.shape, BF16),
+        ],
         in_specs=[
             pl.BlockSpec(memory_space=pltpu.SMEM),
-            pl.BlockSpec((devs, requests, columns), lambda r: (0, 0, 0)),
-            pl.BlockSpec((1, positions, latent), lambda r: (r, 0, 0)),
-            pl.BlockSpec((1, rope, positions), lambda r: (r, 0, 0)),
-        ],
-        out_specs=pl.BlockSpec((devs, requests, heads * latent), lambda r: (0, 0, 0)),
+            pl.BlockSpec(memory_space=pltpu.VMEM),
+            pl.BlockSpec(memory_space=pltpu.HBM),
+            pl.BlockSpec(memory_space=pltpu.HBM),
+            pl.BlockSpec(memory_space=pltpu.HBM),
+        ],
+        out_specs=[pl.BlockSpec(memory_space=pltpu.VMEM)] * 2,
         scratch_shapes=[
-            pltpu.VMEM((devs, requests, columns), F32),
-            pltpu.VMEM((devs, requests, heads * latent), F32),
-        ],
-        compiler_params=pltpu.CompilerParams(vmem_limit_bytes=10 * 1024 * 1024),
+            pltpu.VMEM(latent_cache.shape, BF16),
+            pltpu.VMEM(rope_keys.shape, BF16),
+            pltpu.VMEM((devs * requests, columns), BF16),
+            pltpu.VMEM((devs * requests, heads * latent), BF16),
+            pltpu.SemaphoreType.DMA((requests + 2,)),
+        ],
+        compiler_params=pltpu.CompilerParams(vmem_limit_bytes=28 * 1024 * 1024),
         cost_estimate=pl.CostEstimate(
             flops=2 * requests * rows * positions * (2 * latent + rope),
             bytes_accessed=2 * requests * positions * (latent + rope),
             transcendentals=requests * rows * positions,
         ),
-    )(lengths, query, latent_cache, rope_keys)
-
-
-def project_kernel(latent_ref, absorb_hbm, weight_hbm, out_ref, absorb_ref, weight, sems):
-    heads, latent, width = absorb_ref.shape
-    tiles = sems.shape[0] - 1
-    tile = weight.shape[1] // tiles
-    copies = [pltpu.make_async_copy(absorb_hbm, absorb_ref, sems.at[tiles])] + [
-        pltpu.make_async_copy(
-            weight_hbm.at[:, pl.ds(t * tile, tile)], weight.at[:, pl.ds(t * tile, tile)], sems.at[t]
-        )
-        for t in range(tiles)
-    ]
-    for copy in copies:
-        copy.start()
-    copies[0].wait()
+    )(lengths, query, latent_cache, rope_keys, w_out)
+
+
+def project_kernel(latent_ref, absorb_ref, weight_ref, out_ref):
+    heads, latent, _ = absorb_ref.shape
     values = jnp.concatenate(
         [
             jnp.dot(
@@ -288,31 +325,22 @@
         ],
         axis=1,
     )
-    for t in range(tiles):
-        copies[t + 1].wait()
-        out_ref[:, t * tile : (t + 1) * tile] = jnp.dot(
-            values, weight[:, t * tile : (t + 1) * tile], preferred_element_type=F32
+    tile = 1024
+    for t in range(0, weight_ref.shape[1], tile):
+        out_ref[:, t : t + tile] = jnp.dot(
+            values, weight_ref[:, t : t + tile], preferred_element_type=F32
         ).astype(BF16)
 
 
-def project(head_latent, w_absorb_v, w_out, tiles=7):
+def project(head_latent, w_absorb_v, w_out):
     rows = head_latent.shape[0]
     depth, columns = w_out.shape
     return pl.pallas_call(
         project_kernel,
         out_shape=jax.ShapeDtypeStruct((rows, columns), BF16),
-        in_specs=[
-            pl.BlockSpec(memory_space=pltpu.VMEM),
-            pl.BlockSpec(memory_space=pl.ANY),
-            pl.BlockSpec(memory_space=pl.ANY),
-        ],
+        in_specs=[pl.BlockSpec(memory_space=pltpu.VMEM)] * 3,
         out_specs=pl.BlockSpec(memory_space=pltpu.VMEM),
-        scratch_shapes=[
-            pltpu.VMEM(w_absorb_v.shape, BF16),
-            pltpu.VMEM(w_out.shape, BF16),
-            pltpu.SemaphoreType.DMA((tiles + 1,)),
-        ],
-        compiler_params=pltpu.CompilerParams(vmem_limit_bytes=LIMIT),
+        compiler_params=pltpu.CompilerParams(vmem_limit_bytes=24 * 1024 * 1024),
         cost_estimate=pl.CostEstimate(
             flops=2 * rows * (depth * columns + w_absorb_v.size),
             bytes_accessed=2 * (depth * columns + rows * columns),
@@ -429,28 +457,23 @@
 
     units = w_down.shape[1]
     place = lax.axis_index("dev") % shards
-    step = jnp.arange(ring, dtype=jnp.int32)
-    targets = (place + step) % ring
-    sources = (place + ring - step) % ring
     split = shards // ring
-    down_out = column_blocks(
-        w_down, (targets[:, None] * split + jnp.arange(split, dtype=jnp.int32)).reshape(shards)
-    )
-
-    def relay(k, half):
-        way = [(i, i // ring * ring + (i + k) % ring) for i in range(devs)]
-        return lax.ppermute(down_out[k * split + half], "dev", way)
+    half_width = model_width // shards
+    layout = [(0, 0), (1, 0), (3, 0), (2, 0)]
+    widths = [half_width * split] * ring
+    down_out = column_blocks(w_down, layout, ring, widths)
+
+    def relay(i):
+        way = [(j, j // ring * ring + (j + layout[i][0]) % ring) for j in range(devs)]
+        return lax.ppermute(down_out[i], "dev", way)
 
     query = absorb(q_nope, q_rope, w_absorb_k)
     query = query.reshape(devs, requests, query.shape[1])
     query = lax.all_to_all(query, "dev", split_axis=0, concat_axis=0, tiled=True)
-    down = {(0, half): down_out[half] for half in range(split)}
-    down |= {(1, 0): relay(1, 0), (3, 0): relay(3, 0)}
-    latent_out = attend(
-        query, latent_cache, rope_keys, cache_lengths, heads_local, softmax_scale
-    )
-    latent_out, down, down_out = lax.optimization_barrier((latent_out, down, down_out))
-    down |= {(1, 1): relay(1, 1), (3, 1): relay(3, 1)}
+    down = [down_out[0], relay(1), relay(2)]
+    latent_out, w_out = attend(
+        query, latent_cache, rope_keys, cache_lengths, w_out, heads_local, softmax_scale
+    )
     head_latent = lax.all_to_all(latent_out, "dev", split_axis=0, concat_axis=0, tiled=True)
     partial = project(
         head_latent.reshape(batch_rows, heads_local * latent_width), w_absorb_v, w_out
@@ -464,7 +487,7 @@
         tiled=True,
     )
     partial, down_out = lax.optimization_barrier((partial, down_out))
-    down |= {(2, 0): relay(2, 0), (2, 1): relay(2, 1)}
+    down = [*down, relay(3)]
 
     flat_routes = routes.reshape(requests * top_count)
     chosen = (flat_routes[:, None] == jnp.arange(experts)[None, :]).astype(jnp.int32)
@@ -510,7 +533,8 @@
     beside_below_lo = send(beside[lo], z_up)
     beside_above_hi = send(beside[hi], z_down)
     beside_below_hi = send(below[hi], y_pair)
-    beside_above_lo = send(above[lo], y_pair)
+    above_lo, beside_below_hi = lax.optimization_barrier((above[lo], beside_below_hi))
+    beside_above_lo = send(above_lo, y_pair)
     second = expert_hidden(
         [far_lo, far_hi, beside_below_lo, beside_below_hi, beside_above_lo, beside_above_hi],
         w_gate,
@@ -534,12 +558,7 @@
     everyone = lax.all_to_all(
         everyone, "dev", split_axis=0, concat_axis=0, tiled=True, axis_index_groups=rings
     )
-    result = expert_down(
-        everyone,
-        [down[k, half] for k in range(ring) for half in range(split)],
-        sources,
-        groups,
-    )
+    result = expert_down(everyone, down, layout, groups, split)
     result = lax.all_to_all(result, ("grp", "dev"), split_axis=0, concat_axis=0, tiled=True)
     return mix(slot_weight, result, ring)
 

time: 239 us -> 220 us (0.921)
  blocking collectives: 0 us -> 56.2 us
  waiting for transfers between devices: 124 us -> 86.7 us
  starting transfers between devices: 63.4 us -> 36.7 us
  Pallas kernels: 38.2 us -> 28 us
    all_to_all x0 -> x3, blocking collectives: none -> 56.2 us  [the longest x1 25.3 us: per_device(): lax.all_to_all(outgoing, ('grp', 'dev'), split_axis=0, concat_axis=0, til...]
    all_to_all x3 -> x0, waiting for transfers between devices: 32.3 us -> none  [the longest x1 14.9 us: per_device(): lax.all_to_all(outgoing, ('grp', 'dev'), split_axis=0, concat_axis=0, til...]
    all_to_all x3 -> x0, starting transfers between devices: 17.4 us -> none  [the longest x1 10.2 us: per_device(): lax.all_to_all(outgoing, ('grp', 'dev'), split_axis=0, concat_axis=0, til...]
    ppermute x6 -> x3, waiting for transfers between devices: 7.69 us -> 0.01 us  [relay(): return lax.ppermute(down_out[i], 'dev', way)]
    pallas_call x3, Pallas kernels: 17.5 us -> 11.9 us  [the longest x1 4.73 us: attend(): pl.pallas_call(functools.partial(attend_kernel, heads, scale), out_shape=...]
    all_to_all x1, starting transfers between devices: 12.6 us -> 7.41 us  [per_device(): lax.all_to_all(result, ('grp', 'dev'), split_axis=0, concat_axis=0, tiled...]
    ppermute x6 -> x3, starting transfers between devices: 8.46 us -> 4.37 us  [relay(): return lax.ppermute(down_out[i], 'dev', way)]
    pallas_call x1, Pallas kernels: 5.97 us -> 2.61 us  [project(): pl.pallas_call(project_kernel, out_shape=jax.ShapeDtypeStruct((rows, colu...]
  transfers between devices with their start and end apart: 23 -> 17, of which waited for: 13 -> 7; matrix products, arithmetic and copies ran while one was open for 1% -> 1% of each run, Pallas kernels for 10% -> 8%
where the time goes in v3:
time: 220 us; the launch traced here: 219 us
  waiting for transfers between devices  86.7 us (39%)
  blocking collectives  56.2 us (26%)
  starting transfers between devices  36.7 us (17%)
  Pallas kernels  28 us (13%)
  local copies, waits for them, and re-layouts  10.7 us (5%)
    ppermute x11, waiting for transfers between devices, send(): return lax.ppermute(value, 'dev', way)  31.7 us
    all_to_all x1, waiting for transfers between devices, per_device(): lax.all_to_all(result, ('grp', 'dev'), split_axis=0, concat_axis=0, tiled...  26.6 us
    all_to_all x1, blocking collectives, per_device(): lax.all_to_all(outgoing, ('grp', 'dev'), split_axis=0, concat_axis=0, til...  25.3 us
    all_to_all x1, waiting for transfers between devices, per_device(): lax.all_to_all(partial.reshape(devs, requests, model_width), 'dev', split...  23.3 us
    all_to_all x1, blocking collectives, per_device(): lax.all_to_all(everyone, 'dev', split_axis=0, concat_axis=0, tiled=True,...  15.5 us
    all_to_all x1, blocking collectives, per_device(): lax.all_to_all(latent_out, 'dev', split_axis=0, concat_axis=0, tiled=True)  15.4 us
    ppermute x11, starting transfers between devices, send(): return lax.ppermute(value, 'dev', way)  12 us
    pallas_call x3, Pallas kernels, expert_hidden(): pl.pallas_call(functools.partial(hidden_kernel, len(blocks)), grid=(width...  8.95 us
  transfers between devices with their start and end apart: 17, of which 7 were waited for; matrix products, arithmetic and copies ran while one was open for 1% of the time, Pallas kernels for 8%

profile of v3, /device:TPU:1, one launch (start us, length us, event | category | flops | bytes accessed | tf_op | source)
XLA Modules:
  0.0 219.5 jit_solution(8267324412173512626)
XLA Ops:
  0.0 2.3 %shard_map.154 = bf16[128,2304]{1,0:T(8,128)(2,1)} custom-call(bf16[128,512]{1,0:T(8,128)(2,1)} %nope_ref.1, bf16[128,256]{1,0:T(8,128)(2,1)} %rope_ref.1, bf16[4,128,512]{2,1,0:T(8,128)(2,1)} %weight_ref.2), custom_call_target="tpu_custom_call" | custom-call | flops 67108864 | bytes 1114112 | tf_op jit(solution)/shard_map/pallas_call | solution.py:194
  2.3 8.6 %all-to-all-start = ((bf16[16,8,2304]{2,1,0:T(8,128)(2,1)}), bf16[16,8,2304]{2,1,0:T(8,128)(2,1)S(1)}, u32[]{:S(2)}, u32[]{:S(2)}) async-start(bf16[16,8,2304]{2,1,0:T(8,128)(2,1)} %bitcast.16), calls=%async_computation | async-start | bytes 1179648 | tf_op jit(solution)/shard_map/all_to_all | solution.py:472
  10.9 3.1 %shard_map.157 = (bf16[256,1792]{1,0:T(8,128)(2,1)}, bf16[256,1792]{1,0:T(8,128)(2,1)}, bf16[256,1792]{1,0:T(8,128)(2,1)}, bf16[256,1792]{1,0:T(8,128)(2,1)}) custom-call(bf16[1,256,7168]{2,1,0:T(8,128)(2,1)} %weight_ref.3), custom_call_target="tpu_custom_call" | custom-call | bytes 7340032 | tf_op jit(solution)/shard_map/pallas_call | solution.py:86
  14.1 1.4 collective-permute-start
  15.5 1.3 collective-permute-start.1
  16.8 5.1 %all-to-all-done.query_ref = bf16[16,8,2304]{2,1,0:T(8,128)(2,1)S(1)} async-done(((bf16[16,8,2304]{2,1,0:T(8,128)(2,1)}), bf16[16,8,2304]{2,1,0:T(8,128)(2,1)S(1)}, u32[]{:S(2)}, u32[]{:S(2)}) %all-to-all-start) | async-done | bytes 589856 | tf_op jit(solution)/shard_map/all_to_all | solution.py:472
  22.0 3.1 %copy-done.3 = bf16[512,7168]{1,0:T(8,128)(2,1)S(1)} copy-done((bf16[512,7168]{1,0:T(8,128)(2,1)S(1)}, bf16[512,7168]{1,0:T(8,128)(2,1)}, u32[]{:S(2)}) %copy-start.3) | copy-done | bytes 7340056
  25.1 2.2 copy-done.4
  27.2 4.7 %shard_map.155 = (bf16[16,8,2048]{2,1,0:T(8,128)(2,1)S(1)}, bf16[512,7168]{1,0:T(8,128)(2,1)S(1)}) custom-call(s32[8]{0:T(128)S(1)} %copy-done.9, bf16[16,8,2304]{2,1,0:T(8,128)(2,1)S(1)} %all-to-all-done.query_ref, bf16[8,512,512]{2,1,0:T(8,128)(2,1)S(1)} %copy-done.4, bf16[8,64,512]{2,1,0:T(8,128)(2,1)S(1)} %copy-done.6, bf16[512,7168]{1,0:T(8,128)(2,1)S(1)} %copy-done.3), custom_call_target="tpu_custom_call" | custom-call | flops 570425344 | bytes 4718592 | tf_op jit(solution)/shard_map/pallas_call | solution.py:285
  32.0 15.4 %all_to_all.30 = bf16[16,8,2048]{2,1,0:T(8,128)(2,1)S(1)} all-to-all(bf16[16,8,2048]{2,1,0:T(8,128)(2,1)S(1)} %get-tuple-element.29), channel_id=1, replica_groups=mesh['grp'=8,'dev'=16] {'dev'}, dimensions={0} | all-to-all | bytes 1048576 | tf_op jit(solution)/shard_map/all_to_all | solution.py:477
  47.4 2.6 %shard_map.156 = bf16[128,7168]{1,0:T(8,128)(2,1)} custom-call(bf16[128,2048]{1,0:T(8,128)(2,1)S(1)} %bitcast.13, bf16[4,512,128]{2,1,0:T(8,128)(2,1)S(1)} %copy-done.7, bf16[512,7168]{1,0:T(8,128)(2,1)S(1)} %get-tuple-element.30.weight_ref), custom_call_target="tpu_custom_call" | custom-call | flops 1006632960 | bytes 9175040 | tf_op jit(solution)/shard_map/pallas_call | solution.py:338
  50.0 4.4 %all-to-all-start.2 = ((bf16[16,8,7168]{2,1,0:T(8,128)(2,1)}), bf16[16,8,7168]{2,1,0:T(8,128)(2,1)S(1)}, u32[]{:S(2)}, u32[]{:S(2)}) async-start(bf16[16,8,7168]{2,1,0:T(8,128)(2,1)} %bitcast.3), calls=%async_computation.2 | async-start | bytes 3670016 | tf_op jit(solution)/shard_map/all_to_all | solution.py:482
  55.1 23.3 %all-to-all-done.2.partial_ref = bf16[16,8,7168]{2,1,0:T(8,128)(2,1)S(1)} async-done(((bf16[16,8,7168]{2,1,0:T(8,128)(2,1)}), bf16[16,8,7168]{2,1,0:T(8,128)(2,1)S(1)}, u32[]{:S(2)}, u32[]{:S(2)}) %all-to-all-start.2) | async-done | bytes 1835040 | tf_op jit(solution)/shard_map/all_to_all | solution.py:482
  78.4 1.6 collective-permute-start.2
  81.0 25.3 %all_to_all.31 = bf16[16,4,7168]{2,1,0:T(4,128)(2,1)S(1)} all-to-all(bf16[16,4,7168]{2,1,0:T(4,128)(2,1)S(1)} %shard_map.158), channel_id=1, replica_groups={{0,8,16,24,32,40,48,56,64,72,80,88,96,104,112,120},{1,9,17,25,33,41,49,..., dimensions={0} | all-to-all | bytes 1835008 | tf_op jit(solution)/shard_map/all_to_all | solution.py:510
  107.4 2.7 %collective-permute-start.9 = (bf16[64,7168]{1,0:T(8,128)(2,1)S(1)}, bf16[64,7168]{1,0:T(8,128)(2,1)S(1)}, u32[]{:S(2)}, u32[]{:S(2)}) collective-permute-start(bf16[64,7168]{1,0:T(8,128)(2,1)S(1)} %reshape.146.refs_0_), channel_id=1, source_target_pairs={{0,3},{1,0},{2,1},{3,2},{4,7},{5,4},{6,5},{7,6},{8,11},{9,8},{10,9... | collective-permute-start | bytes 2752520 | tf_op jit(solution)/shard_map/ppermute | solution.py:525
  110.0 18.0 %collective-permute-done.3.refs_3_ = bf16[64,7168]{1,0:T(8,128)(2,1)S(1)} collective-permute-done((bf16[64,7168]{1,0:T(8,128)(2,1)S(1)}, bf16[64,7168]{1,0:T(8,128)(2,1)S(1)}, u32[]{:S(2)}, u32[]{:S(2)}) %collective-permute-start.3) | collective-permute-done | bytes 917536 | tf_op jit(solution)/shard_map/ppermute | solution.py:525
  128.2 2.7 %collective-permute-start.6 = (bf16[32,7168]{1,0:T(8,128)(2,1)S(1)}, bf16[32,7168]{1,0:T(8,128)(2,1)S(1)}, u32[]{:S(2)}, u32[]{:S(2)}) collective-permute-start(bf16[32,7168]{1,0:T(8,128)(2,1)S(1)} %get-tuple-element.57), channel_id=1, source_target_pairs={{0,3},{1,0},{2,1},{3,2},{4,7},{5,4},{6,5},{7,6},{8,11},{9,8},{10,9... | collective-permute-start | bytes 1376264 | tf_op jit(solution)/shard_map/ppermute | solution.py:525
  131.4 2.7 %collective-permute-start.11 = (bf16[32,7168]{1,0:T(8,128)(2,1)S(1)}, bf16[32,7168]{1,0:T(8,128)(2,1)S(1)}, u32[]{:S(2)}, u32[]{:S(2)}) collective-permute-start(bf16[32,7168]{1,0:T(8,128)(2,1)S(1)} %get-tuple-element.56), channel_id=1, source_target_pairs={{0,3},{1,0},{2,1},{3,2},{4,7},{5,4},{6,5},{7,6},{8,11},{9,8},{10,9... | collective-permute-start | bytes 1376264 | tf_op jit(solution)/shard_map/ppermute | solution.py:525
  134.1 7.1 %collective-permute-done.12.refs_3_ = bf16[32,7168]{1,0:T(8,128)(2,1)S(1)} collective-permute-done((bf16[32,7168]{1,0:T(8,128)(2,1)S(1)}, bf16[32,7168]{1,0:T(8,128)(2,1)S(1)}, u32[]{:S(2)}, u32[]{:S(2)}) %collective-permute-start.12) | collective-permute-done | bytes 458784 | tf_op jit(solution)/shard_map/ppermute | solution.py:525
  141.8 2.7 %collective-permute-start.7 = (bf16[32,7168]{1,0:T(8,128)(2,1)S(1)}, bf16[32,7168]{1,0:T(8,128)(2,1)S(1)}, u32[]{:S(2)}, u32[]{:S(2)}) collective-permute-start(bf16[32,7168]{1,0:T(8,128)(2,1)S(1)} %collective-permute-done.6.refs_5_), channel_id=1, source_target_pairs={{0,3},{1,0},{2,1},{3,2},{4,7},{5,4},{6,5},{7,6},{8,11},{9,8},{10,9... | collective-permute-start | bytes 1376264 | tf_op jit(solution)/shard_map/ppermute | solution.py:525
  144.5 2.0 copy-done.1
  146.6 3.6 %shard_map.159 = bf16[256,256]{1,0:T(8,128)(2,1)S(1)} custom-call(bf16[64,7168]{1,0:T(8,128)(2,1)S(1)} %reshape.146.refs_0_, bf16[64,7168]{1,0:T(8,128)(2,1)S(1)} %collective-permute-done.8.refs_1_, bf16[64,7168]{1,0:T(8,128)(2,1)S(1)} %collective-permute-done.9.refs_2_, bf16[64,7168]{1,0:T(8,128)(2,1)S(1)} %collective-permute-done.3.refs_3_, ...), custom_call_target="tpu_custom_call" | custom-call | flops 1879048192 | bytes 11010048 | tf_op jit(solution)/shard_map/pallas_call | solution.py:40
  150.5 3.1 %shard_map.160 = bf16[192,256]{1,0:T(8,128)(2,1)S(1)} custom-call(bf16[32,7168]{1,0:T(8,128)(2,1)S(1)} %collective-permute-done.10.refs_0_, bf16[32,7168]{1,0:T(8,128)(2,1)S(1)} %collective-permute-done.11.refs_1_, bf16[32,7168]{1,0:T(8,128)(2,1)S(1)} %collective-permute-done.4.refs_2_, bf16[32,7168]{1,0:T(8,128)(2,1)S(1)} %collective-permute-done.12.refs_3_, ...), custom_call_target="tpu_custom_call" | custom-call | flops 1409286144 | bytes 10092544 | tf_op jit(solution)/shard_map/pallas_call | solution.py:40
  153.6 6.2 %collective-permute-done.5.refs_0_ = bf16[32,7168]{1,0:T(8,128)(2,1)S(1)} collective-permute-done((bf16[32,7168]{1,0:T(8,128)(2,1)S(1)}, bf16[32,7168]{1,0:T(8,128)(2,1)S(1)}, u32[]{:S(2)}, u32[]{:S(2)}) %collective-permute-start.5) | collective-permute-done | bytes 458784 | tf_op jit(solution)/shard_map/ppermute | solution.py:525
  159.8 2.3 %shard_map.161 = bf16[64,256]{1,0:T(8,128)(2,1)S(1)} custom-call(bf16[32,7168]{1,0:T(8,128)(2,1)S(1)} %collective-permute-done.5.refs_0_, bf16[32,7168]{1,0:T(8,128)(2,1)S(1)} %collective-permute-done.7.refs_1_, bf16[1,7168,256]{2,1,0:T(8,128)(2,1)S(1)} %copy-done, bf16[1,7168,256]{2,1,0:T(8,128)(2,1)S(1)} %copy-done.2), custom_call_target="tpu_custom_call" | custom-call | flops 469762048 | bytes 8257536 | tf_op jit(solution)/shard_map/pallas_call | solution.py:40
  162.8 15.5 %all_to_all.32.hidden_ref = bf16[4,512,256]{2,1,0:T(8,128)(2,1)S(1)} all-to-all(bf16[4,512,256]{2,1,0:T(8,128)(2,1)S(1)} %broadcast_in_dim.48), channel_id=1, replica_groups={{0,1,2,3},{4,5,6,7},{8,9,10,11},{12,13,14,15},{16,17,18,19},{20,21,22,2..., dimensions={0} | all-to-all | bytes 2097152 | tf_op jit(solution)/shard_map/all_to_all | solution.py:558
  178.3 4.0 %shard_map.162 = bf16[128,4,1792]{2,1,0:T(4,128)(2,1)S(1)} custom-call(bf16[4,512,256]{2,1,0:T(8,128)(2,1)S(1)} %all_to_all.32.hidden_ref, bf16[256,1792]{1,0:T(8,128)(2,1)S(1)} %copy-done.10, bf16[256,1792]{1,0:T(8,128)(2,1)S(1)} %collective-permute-done.refs_1_, bf16[256,1792]{1,0:T(8,128)(2,1)} %collective-permute-done.1.refs_2_, ...), custom_call_target="tpu_custom_call" | custom-call | flops 1879048192 | bytes 6553600 | tf_op jit(solution)/shard_map/pallas_call | solution.py:149
  182.4 1.3 copy-done.5
  183.6 7.4 %all-to-all-start.5 = ((bf16[128,4,1792]{2,1,0:T(4,128)(2,1)}), bf16[128,4,1792]{2,1,0:T(4,128)(2,1)S(1)}, u32[]{:S(2)}, u32[]{:S(2)}) async-start(bf16[128,4,1792]{2,1,0:T(4,128)(2,1)} %copy-done.5), calls=%async_computation.5 | async-start | bytes 3670016 | tf_op jit(solution)/shard_map/all_to_all | solution.py:562
  191.3 26.6 %all-to-all-done.5.rows_ref = bf16[128,4,1792]{2,1,0:T(4,128)(2,1)S(1)} async-done(((bf16[128,4,1792]{2,1,0:T(4,128)(2,1)}), bf16[128,4,1792]{2,1,0:T(4,128)(2,1)S(1)}, u32[]{:S(2)}, u32[]{:S(2)}) %all-to-all-start.5) | async-done | bytes 1835040 | tf_op jit(solution)/shard_map/all_to_all | solution.py:562
  217.9 1.6 shard_map.163
  (72 shorter events, 5.3 us)
Async XLA Ops:
  0.0 22.0 %copy-start.9 = (s32[8]{0:T(128)S(1)}, s32[8]{0:T(128)}, u32[]{:S(2)}) copy-start(s32[8]{0:T(128)} %length_ref.1) | copy-start | bytes 100
  0.0 22.0 %copy-start.6 = (bf16[8,64,512]{2,1,0:T(8,128)(2,1)S(1)}, bf16[8,64,512]{2,1,0:T(8,128)(2,1)}, u32[]{:S(2)}) copy-start(bf16[8,64,512]{2,1,0:T(8,128)(2,1)} %keys_hbm.1) | copy-start | bytes 1572868
  2.3 19.6 %all-to-all-start = ((bf16[16,8,2304]{2,1,0:T(8,128)(2,1)}), bf16[16,8,2304]{2,1,0:T(8,128)(2,1)S(1)}, u32[]{:S(2)}, u32[]{:S(2)}) async-start(bf16[16,8,2304]{2,1,0:T(8,128)(2,1)} %bitcast.16), calls=%async_computation | async-start | bytes 1179648 | tf_op jit(solution)/shard_map/all_to_all | solution.py:472
  14.1 36.0 %collective-permute-start = (bf16[256,1792]{1,0:T(8,128)(2,1)}, bf16[256,1792]{1,0:T(8,128)(2,1)S(1)}, u32[]{:S(2)}, u32[]{:S(2)}) collective-permute-start(bf16[256,1792]{1,0:T(8,128)(2,1)} %get-tuple-element.32), channel_id=1, source_target_pairs={{0,1},{1,2},{2,3},{3,0},{4,5},{5,6},{6,7},{7,4},{8,9},{9,10},{10,1... | collective-permute-start | bytes 2752520 | tf_op jit(solution)/shard_map/ppermute | solution.py:468
  15.5 34.6 %collective-permute-start.1 = (bf16[256,1792]{1,0:T(8,128)(2,1)}, bf16[256,1792]{1,0:T(8,128)(2,1)}, u32[]{:S(2)}, u32[]{:S(2)}) collective-permute-start(bf16[256,1792]{1,0:T(8,128)(2,1)} %get-tuple-element.33), channel_id=1, source_target_pairs={{0,3},{1,0},{2,1},{3,2},{4,7},{5,4},{6,5},{7,6},{8,11},{9,8},{10,9... | collective-permute-start | bytes 2752520 | tf_op jit(solution)/shard_map/ppermute | solution.py:468
  22.0 3.1 %copy-start.3 = (bf16[512,7168]{1,0:T(8,128)(2,1)S(1)}, bf16[512,7168]{1,0:T(8,128)(2,1)}, u32[]{:S(2)}) copy-start(bf16[512,7168]{1,0:T(8,128)(2,1)} %weight_hbm.1) | copy-start | bytes 22020100
  25.1 2.2 copy-start.4
  27.2 20.2 %copy-start.7 = (bf16[4,512,128]{2,1,0:T(8,128)(2,1)S(1)}, bf16[4,512,128]{2,1,0:T(8,128)(2,1)}, u32[]{:S(2)}) copy-start(bf16[4,512,128]{2,1,0:T(8,128)(2,1)} %absorb_ref.1) | copy-start | bytes 1572868
  50.0 4.4 %copy-start.12 = (s32[8,4]{0,1:T(4,128)S(1)}, s32[8,4]{0,1:T(4,128)}, u32[]{:S(2)}) copy-start(s32[8,4]{0,1:T(4,128)} %param.25) | copy-start | bytes 388
  50.0 30.2 %copy-start.8 = (f32[7168]{0:T(1024)S(1)}, f32[7168]{0:T(1024)}, u32[]{:S(2)}) copy-start(f32[7168]{0:T(1024)} %param.24) | copy-start | bytes 86020
  50.0 28.4 %all-to-all-start.2 = ((bf16[16,8,7168]{2,1,0:T(8,128)(2,1)}), bf16[16,8,7168]{2,1,0:T(8,128)(2,1)S(1)}, u32[]{:S(2)}, u32[]{:S(2)}) async-start(bf16[16,8,7168]{2,1,0:T(8,128)(2,1)} %bitcast.3), calls=%async_computation.2 | async-start | bytes 3670016 | tf_op jit(solution)/shard_map/all_to_all | solution.py:482
  54.5 52.1 %copy-start.11 = (s32[8]{0:T(128)S(1)}, s32[8]{0:T(128)}, u32[]{:S(2)}) copy-start(s32[8]{0:T(128)} %constant.91.clone) | copy-start | bytes 100
  78.4 28.0 %collective-permute-start.2 = (bf16[256,1792]{1,0:T(8,128)(2,1)}, bf16[256,1792]{1,0:T(8,128)(2,1)}, u32[]{:S(2)}, u32[]{:S(2)}) collective-permute-start(bf16[256,1792]{1,0:T(8,128)(2,1)} %get-tuple-element.41), channel_id=1, source_target_pairs={{0,2},{1,3},{2,0},{3,1},{4,6},{5,7},{6,4},{7,5},{8,10},{9,11},{10,... | collective-permute-start | bytes 2752520 | tf_op jit(solution)/shard_map/ppermute | solution.py:468
  106.4 21.6 %collective-permute-start.3 = (bf16[64,7168]{1,0:T(8,128)(2,1)S(1)}, bf16[64,7168]{1,0:T(8,128)(2,1)S(1)}, u32[]{:S(2)}, u32[]{:S(2)}) collective-permute-start(bf16[64,7168]{1,0:T(8,128)(2,1)S(1)} %reshape.146.refs_0_), channel_id=1, source_target_pairs={{0,4},{1,5},{2,6},{3,7},{4,0},{5,1},{6,2},{7,3},{8,12},{9,13},{10,... | collective-permute-start | bytes 2752520 | tf_op jit(solution)/shard_map/ppermute | solution.py:525
  107.3 37.3 %copy-start = (bf16[1,7168,256]{2,1,0:T(8,128)(2,1)S(1)}, bf16[1,7168,256]{2,1,0:T(8,128)(2,1)}, u32[]{:S(2)}) copy-start(bf16[1,7168,256]{2,1,0:T(8,128)(2,1)} %refs_2_.1) | copy-start | bytes 11010052
  107.3 23.6 %collective-permute-start.8 = (bf16[64,7168]{1,0:T(8,128)(2,1)S(1)}, bf16[64,7168]{1,0:T(8,128)(2,1)S(1)}, u32[]{:S(2)}, u32[]{:S(2)}) collective-permute-start(bf16[64,7168]{1,0:T(8,128)(2,1)S(1)} %reshape.146.refs_0_), channel_id=1, source_target_pairs={{0,1},{1,2},{2,3},{3,0},{4,5},{5,6},{6,7},{7,4},{8,9},{9,10},{10,1... | collective-permute-start | bytes 2752520 | tf_op jit(solution)/shard_map/ppermute | solution.py:525
  107.4 24.0 %collective-permute-start.9 = (bf16[64,7168]{1,0:T(8,128)(2,1)S(1)}, bf16[64,7168]{1,0:T(8,128)(2,1)S(1)}, u32[]{:S(2)}, u32[]{:S(2)}) collective-permute-start(bf16[64,7168]{1,0:T(8,128)(2,1)S(1)} %reshape.146.refs_0_), channel_id=1, source_target_pairs={{0,3},{1,0},{2,1},{3,2},{4,7},{5,4},{6,5},{7,6},{8,11},{9,8},{10,9... | collective-permute-start | bytes 2752520 | tf_op jit(solution)/shard_map/ppermute | solution.py:525
  128.1 13.8 %collective-permute-start.4 = (bf16[32,7168]{1,0:T(8,128)(2,1)S(1)}, bf16[32,7168]{1,0:T(8,128)(2,1)S(1)}, u32[]{:S(2)}, u32[]{:S(2)}) collective-permute-start(bf16[32,7168]{1,0:T(8,128)(2,1)S(1)} %get-tuple-element.58), channel_id=1, source_target_pairs={{0,1},{1,2},{2,3},{3,0},{4,5},{5,6},{6,7},{7,4},{8,9},{9,10},{10,1... | collective-permute-start | bytes 1376264 | tf_op jit(solution)/shard_map/ppermute | solution.py:525
  128.2 13.7 %collective-permute-start.6 = (bf16[32,7168]{1,0:T(8,128)(2,1)S(1)}, bf16[32,7168]{1,0:T(8,128)(2,1)S(1)}, u32[]{:S(2)}, u32[]{:S(2)}) collective-permute-start(bf16[32,7168]{1,0:T(8,128)(2,1)S(1)} %get-tuple-element.57), channel_id=1, source_target_pairs={{0,3},{1,0},{2,1},{3,2},{4,7},{5,4},{6,5},{7,6},{8,11},{9,8},{10,9... | collective-permute-start | bytes 1376264 | tf_op jit(solution)/shard_map/ppermute | solution.py:525
  130.9 19.3 %collective-permute-start.10 = (bf16[32,7168]{1,0:T(8,128)(2,1)S(1)}, bf16[32,7168]{1,0:T(8,128)(2,1)S(1)}, u32[]{:S(2)}, u32[]{:S(2)}) collective-permute-start(bf16[32,7168]{1,0:T(8,128)(2,1)S(1)} %get-tuple-element.54), channel_id=1, source_target_pairs={{0,1},{1,2},{2,3},{3,0},{4,5},{5,6},{6,7},{7,4},{8,9},{9,10},{10,1... | collective-permute-start | bytes 1376264 | tf_op jit(solution)/shard_map/ppermute | solution.py:525
  131.0 10.3 %collective-permute-start.12 = (bf16[32,7168]{1,0:T(8,128)(2,1)S(1)}, bf16[32,7168]{1,0:T(8,128)(2,1)S(1)}, u32[]{:S(2)}, u32[]{:S(2)}) collective-permute-start(bf16[32,7168]{1,0:T(8,128)(2,1)S(1)} %get-tuple-element.53), channel_id=1, source_target_pairs={{0,4},{1,5},{2,6},{3,7},{4,0},{5,1},{6,2},{7,3},{8,12},{9,13},{10,... | collective-permute-start | bytes 1376264 | tf_op jit(solution)/shard_map/ppermute | solution.py:525
  131.4 18.7 %collective-permute-start.11 = (bf16[32,7168]{1,0:T(8,128)(2,1)S(1)}, bf16[32,7168]{1,0:T(8,128)(2,1)S(1)}, u32[]{:S(2)}, u32[]{:S(2)}) collective-permute-start(bf16[32,7168]{1,0:T(8,128)(2,1)S(1)} %get-tuple-element.56), channel_id=1, source_target_pairs={{0,3},{1,0},{2,1},{3,2},{4,7},{5,4},{6,5},{7,6},{8,11},{9,8},{10,9... | collective-permute-start | bytes 1376264 | tf_op jit(solution)/shard_map/ppermute | solution.py:525
  141.2 9.3 %collective-permute-start.13 = (bf16[32,7168]{1,0:T(8,128)(2,1)S(1)}, bf16[32,7168]{1,0:T(8,128)(2,1)S(1)}, u32[]{:S(2)}, u32[]{:S(2)}) collective-permute-start(bf16[32,7168]{1,0:T(8,128)(2,1)S(1)} %get-tuple-element.44), channel_id=1, source_target_pairs={{0,4},{1,5},{2,6},{3,7},{4,0},{5,1},{6,2},{7,3},{8,12},{9,13},{10,... | collective-permute-start | bytes 1376264 | tf_op jit(solution)/shard_map/ppermute | solution.py:525
  141.8 17.9 %collective-permute-start.5 = (bf16[32,7168]{1,0:T(8,128)(2,1)S(1)}, bf16[32,7168]{1,0:T(8,128)(2,1)S(1)}, u32[]{:S(2)}, u32[]{:S(2)}) collective-permute-start(bf16[32,7168]{1,0:T(8,128)(2,1)S(1)} %collective-permute-done.4.refs_2_), channel_id=1, source_target_pairs={{0,1},{1,2},{2,3},{3,0},{4,5},{5,6},{6,7},{7,4},{8,9},{9,10},{10,1... | collective-permute-start | bytes 1376264 | tf_op jit(solution)/shard_map/ppermute | solution.py:525
  141.8 17.9 %collective-permute-start.7 = (bf16[32,7168]{1,0:T(8,128)(2,1)S(1)}, bf16[32,7168]{1,0:T(8,128)(2,1)S(1)}, u32[]{:S(2)}, u32[]{:S(2)}) collective-permute-start(bf16[32,7168]{1,0:T(8,128)(2,1)S(1)} %collective-permute-done.6.refs_5_), channel_id=1, source_target_pairs={{0,3},{1,0},{2,1},{3,2},{4,7},{5,4},{6,5},{7,6},{8,11},{9,8},{10,9... | collective-permute-start | bytes 1376264 | tf_op jit(solution)/shard_map/ppermute | solution.py:525
  144.5 2.0 copy-start.1
  150.1 9.6 %copy-start.2 = (bf16[1,7168,256]{2,1,0:T(8,128)(2,1)S(1)}, bf16[1,7168,256]{2,1,0:T(8,128)(2,1)}, u32[]{:S(2)}) copy-start(bf16[1,7168,256]{2,1,0:T(8,128)(2,1)} %refs_3_.1) | copy-start | bytes 11010052
  162.1 16.2 %copy-start.10 = (bf16[256,1792]{1,0:T(8,128)(2,1)S(1)}, bf16[256,1792]{1,0:T(8,128)(2,1)}, u32[]{:S(2)}) copy-start(bf16[256,1792]{1,0:T(8,128)(2,1)} %get-tuple-element.49.refs_0_) | copy-start | bytes 2752516
  178.3 12.7 %copy-start.13 = (f32[8,8]{1,0:T(8,128)S(1)}, f32[8,8]{1,0:T(8,128)}, u32[]{:S(2)}) copy-start(f32[8,8]{1,0:T(8,128)} %param.27) | copy-start | bytes 772
  178.3 12.9 %copy-start.14 = (f32[8,4]{0,1:T(4,128)S(1)}, f32[8,4]{0,1:T(4,128)}, u32[]{:S(2)}) copy-start(f32[8,4]{0,1:T(4,128)} %param.26) | copy-start | bytes 388
  182.3 1.3 copy-start.5
  183.6 34.3 %all-to-all-start.5 = ((bf16[128,4,1792]{2,1,0:T(4,128)(2,1)}), bf16[128,4,1792]{2,1,0:T(4,128)(2,1)S(1)}, u32[]{:S(2)}, u32[]{:S(2)}) async-start(bf16[128,4,1792]{2,1,0:T(4,128)(2,1)} %copy-done.5), calls=%async_computation.5 | async-start | bytes 3670016 | tf_op jit(solution)/shard_map/all_to_all | solution.py:562

commit v4 on v3

--- a/solution.py
+++ b/solution.py
@@ -34,7 +34,7 @@
         out_ref[...] = (gate * jax.nn.sigmoid(gate) * up_sum[...]).astype(BF16)
 
 
-def expert_hidden(blocks, w_gate, w_up, tile=1024):
+def expert_hidden(blocks, w_gate, w_up, tile=1792):
     rows = sum(block.shape[0] for block in blocks)
     width, units = w_gate.shape[1:]
     return pl.pallas_call(
@@ -45,7 +45,7 @@
         + [pl.BlockSpec((1, tile, units), lambda i: (0, i, 0))] * 2,
         out_specs=pl.BlockSpec((rows, units), lambda i: (0, 0)),
         scratch_shapes=[pltpu.VMEM((rows, units), F32)] * 2,
-        compiler_params=pltpu.CompilerParams(vmem_limit_bytes=24 * 1024 * 1024),
+        compiler_params=pltpu.CompilerParams(vmem_limit_bytes=14 * 1024 * 1024),
         cost_estimate=pl.CostEstimate(
             flops=4 * rows * width * units,
             bytes_accessed=2 * width * (2 * units + rows),
@@ -486,9 +486,6 @@
         concat_axis=0,
         tiled=True,
     )
-    partial, down_out = lax.optimization_barrier((partial, down_out))
-    down = [*down, relay(3)]
-
     flat_routes = routes.reshape(requests * top_count)
     chosen = (flat_routes[:, None] == jnp.arange(experts)[None, :]).astype(jnp.int32)
     earlier = jnp.cumsum(chosen, axis=0) - chosen
@@ -501,6 +498,12 @@
     group_weight = jnp.sum(jnp.where(group_match, group_probs[:, None, :], 0.0), axis=2)
     pair_weight = group_weight * expert_probs
     slot_weight = jnp.sum(jnp.where(placed, pair_weight[None], 0.0), axis=2).T
+
+    partial, down_out, dispatch, slot_weight = lax.optimization_barrier(
+        (partial, down_out, dispatch, slot_weight)
+    )
+    down = [*down, relay(3)]
+
     outgoing = dispatch_rows(partial, norm_gain[None, :], dispatch)
 
     peers = [
@@ -524,16 +527,18 @@
     def send(value, way):
         return lax.ppermute(value, "dev", way)
 
-    below = send(own, z_up)
-    above = send(own, z_down)
+    below_lo = send(own[lo], z_up)
+    above_hi = send(own[hi], z_down)
     beside = send(own, y_pair)
-    first = expert_hidden([own, below, above, beside], w_gate, w_up)
-    far_lo = send(below[lo], z_up)
-    far_hi = send(above[hi], z_down)
+    below_hi = send(own[hi], z_up)
+    above_lo = send(own[lo], z_down)
+    first = expert_hidden([own, below_lo, below_hi, above_lo, above_hi, beside], w_gate, w_up)
+    far_lo = send(below_lo, z_up)
+    far_hi = send(above_hi, z_down)
     beside_below_lo = send(beside[lo], z_up)
     beside_above_hi = send(beside[hi], z_down)
-    beside_below_hi = send(below[hi], y_pair)
-    above_lo, beside_below_hi = lax.optimization_barrier((above[lo], beside_below_hi))
+    beside_below_hi = send(below_hi, y_pair)
+    above_lo, beside_below_hi = lax.optimization_barrier((above_lo, beside_below_hi))
     beside_above_lo = send(above_lo, y_pair)
     second = expert_hidden(
         [far_lo, far_hi, beside_below_lo, beside_below_hi, beside_above_lo, beside_above_hi],

time: 220 us -> 219 us (level)
  blocking collectives: 56.2 us -> 89.6 us
  waiting for transfers between devices: 86.7 us -> 56.2 us
  starting transfers between devices: 36.7 us -> 29 us
  local copies, waits for them, and re-layouts: 10.7 us -> 13.3 us
    all_to_all x0 -> x1, blocking collectives: none -> 35 us  [per_device(): lax.all_to_all(result, ('grp', 'dev'), split_axis=0, concat_axis=0, tiled...]
    all_to_all x1 -> x0, waiting for transfers between devices: 26.6 us -> none  [per_device(): lax.all_to_all(result, ('grp', 'dev'), split_axis=0, concat_axis=0, tiled...]
    all_to_all x1 -> x0, starting transfers between devices: 7.41 us -> none  [per_device(): lax.all_to_all(result, ('grp', 'dev'), split_axis=0, concat_axis=0, tiled...]
    ppermute x11 -> x13, waiting for transfers between devices: 31.7 us -> 28.2 us  [send(): return lax.ppermute(value, 'dev', way)]
    unnamed x31 -> x33, local copies, waits for them, and re-layouts: 8.69 us -> 9.48 us
    ppermute x11 -> x13, starting transfers between devices: 12 us -> 11.5 us  [send(): return lax.ppermute(value, 'dev', way)]
  transfers between devices with their start and end apart: 17 -> 18, of which waited for: 7 -> 10; matrix products, arithmetic and copies ran while one was open for 1% -> 2% of each run, Pallas kernels for 8% -> 9%
where the time goes in v4:
time: 219 us; the launch traced here: 218 us
  blocking collectives  89.6 us (41%)
  waiting for transfers between devices  56.2 us (26%)
  Pallas kernels  29 us (13%)
  starting transfers between devices  29 us (13%)
  local copies, waits for them, and re-layouts  13.3 us (6%)
    all_to_all x1, blocking collectives, per_device(): lax.all_to_all(result, ('grp', 'dev'), split_axis=0, concat_axis=0, tiled...  35 us
    ppermute x13, waiting for transfers between devices, send(): return lax.ppermute(value, 'dev', way)  28.2 us
    all_to_all x1, blocking collectives, per_device(): lax.all_to_all(outgoing, ('grp', 'dev'), split_axis=0, concat_axis=0, til...  25.3 us
    all_to_all x1, waiting for transfers between devices, per_device(): lax.all_to_all(partial.reshape(devs, requests, model_width), 'dev', split...  22.7 us
    all_to_all x1, blocking collectives, per_device(): lax.all_to_all(latent_out, 'dev', split_axis=0, concat_axis=0, tiled=True)  15.4 us
    all_to_all x1, blocking collectives, per_device(): lax.all_to_all(everyone, 'dev', split_axis=0, concat_axis=0, tiled=True,...  13.9 us
    ppermute x13, starting transfers between devices, send(): return lax.ppermute(value, 'dev', way)  11.5 us
    pallas_call x3, Pallas kernels, expert_hidden(): pl.pallas_call(functools.partial(hidden_kernel, len(blocks)), grid=(width...  9.95 us
  transfers between devices with their start and end apart: 18, of which 10 were waited for; matrix products, arithmetic and copies ran while one was open for 2% of the time, Pallas kernels for 9%

profile of v4, /device:TPU:1, one launch (start us, length us, event | category | flops | bytes accessed | tf_op | source)
XLA Modules:
  0.0 218.1 jit_solution(8548538724265426106)
XLA Ops:
  0.0 2.3 %shard_map.154 = bf16[128,2304]{1,0:T(8,128)(2,1)} custom-call(bf16[128,512]{1,0:T(8,128)(2,1)} %nope_ref.1, bf16[128,256]{1,0:T(8,128)(2,1)} %rope_ref.1, bf16[4,128,512]{2,1,0:T(8,128)(2,1)} %weight_ref.2), custom_call_target="tpu_custom_call" | custom-call | flops 67108864 | bytes 1114112 | tf_op jit(solution)/shard_map/pallas_call | solution.py:194
  2.3 8.6 %all-to-all-start = ((bf16[16,8,2304]{2,1,0:T(8,128)(2,1)}), bf16[16,8,2304]{2,1,0:T(8,128)(2,1)S(1)}, u32[]{:S(2)}, u32[]{:S(2)}) async-start(bf16[16,8,2304]{2,1,0:T(8,128)(2,1)} %bitcast.16), calls=%async_computation | async-start | bytes 1179648 | tf_op jit(solution)/shard_map/all_to_all | solution.py:472
  10.9 3.1 %shard_map.157 = (bf16[256,1792]{1,0:T(8,128)(2,1)}, bf16[256,1792]{1,0:T(8,128)(2,1)}, bf16[256,1792]{1,0:T(8,128)(2,1)}, bf16[256,1792]{1,0:T(8,128)(2,1)}) custom-call(bf16[1,256,7168]{2,1,0:T(8,128)(2,1)} %weight_ref.3), custom_call_target="tpu_custom_call" | custom-call | bytes 7340032 | tf_op jit(solution)/shard_map/pallas_call | solution.py:86
  14.0 1.4 collective-permute-start
  16.8 5.2 %all-to-all-done.query_ref = bf16[16,8,2304]{2,1,0:T(8,128)(2,1)S(1)} async-done(((bf16[16,8,2304]{2,1,0:T(8,128)(2,1)}), bf16[16,8,2304]{2,1,0:T(8,128)(2,1)S(1)}, u32[]{:S(2)}, u32[]{:S(2)}) %all-to-all-start) | async-done | bytes 589856 | tf_op jit(solution)/shard_map/all_to_all | solution.py:472
  22.0 3.1 %copy-done.3 = bf16[512,7168]{1,0:T(8,128)(2,1)S(1)} copy-done((bf16[512,7168]{1,0:T(8,128)(2,1)S(1)}, bf16[512,7168]{1,0:T(8,128)(2,1)}, u32[]{:S(2)}) %copy-start.3) | copy-done | bytes 7340056
  25.1 2.2 %copy-done.4 = bf16[8,512,512]{2,1,0:T(8,128)(2,1)S(1)} copy-done((bf16[8,512,512]{2,1,0:T(8,128)(2,1)S(1)}, bf16[8,512,512]{2,1,0:T(8,128)(2,1)}, u32[]{:S(2)}) %copy-start.4) | copy-done | bytes 4194328
  27.2 4.7 %shard_map.155 = (bf16[16,8,2048]{2,1,0:T(8,128)(2,1)S(1)}, bf16[512,7168]{1,0:T(8,128)(2,1)S(1)}) custom-call(s32[8]{0:T(128)S(1)} %copy-done.8, bf16[16,8,2304]{2,1,0:T(8,128)(2,1)S(1)} %all-to-all-done.query_ref, bf16[8,512,512]{2,1,0:T(8,128)(2,1)S(1)} %copy-done.4, bf16[8,64,512]{2,1,0:T(8,128)(2,1)S(1)} %copy-done.5, bf16[512,7168]{1,0:T(8,128)(2,1)S(1)} %copy-done.3), custom_call_target="tpu_custom_call" | custom-call | flops 570425344 | bytes 4718592 | tf_op jit(solution)/shard_map/pallas_call | solution.py:285
  32.0 15.4 %all_to_all.30 = bf16[16,8,2048]{2,1,0:T(8,128)(2,1)S(1)} all-to-all(bf16[16,8,2048]{2,1,0:T(8,128)(2,1)S(1)} %get-tuple-element.31), channel_id=1, replica_groups=mesh['grp'=8,'dev'=16] {'dev'}, dimensions={0} | all-to-all | bytes 1048576 | tf_op jit(solution)/shard_map/all_to_all | solution.py:477
  47.4 2.6 %shard_map.156 = bf16[128,7168]{1,0:T(8,128)(2,1)} custom-call(bf16[128,2048]{1,0:T(8,128)(2,1)S(1)} %bitcast.13, bf16[4,512,128]{2,1,0:T(8,128)(2,1)S(1)} %copy-done.6, bf16[512,7168]{1,0:T(8,128)(2,1)S(1)} %get-tuple-element.32.weight_ref), custom_call_target="tpu_custom_call" | custom-call | flops 1006632960 | bytes 9175040 | tf_op jit(solution)/shard_map/pallas_call | solution.py:338
  50.1 4.4 %all-to-all-start.2 = ((bf16[16,8,7168]{2,1,0:T(8,128)(2,1)}), bf16[16,8,7168]{2,1,0:T(8,128)(2,1)S(1)}, u32[]{:S(2)}, u32[]{:S(2)}) async-start(bf16[16,8,7168]{2,1,0:T(8,128)(2,1)} %bitcast.2), calls=%async_computation.2 | async-start | bytes 3670016 | tf_op jit(solution)/shard_map/all_to_all | solution.py:482
  55.6 22.7 %all-to-all-done.2.partial_ref = bf16[16,8,7168]{2,1,0:T(8,128)(2,1)S(1)} async-done(((bf16[16,8,7168]{2,1,0:T(8,128)(2,1)}), bf16[16,8,7168]{2,1,0:T(8,128)(2,1)S(1)}, u32[]{:S(2)}, u32[]{:S(2)}) %all-to-all-start.2) | async-done | bytes 1835040 | tf_op jit(solution)/shard_map/all_to_all | solution.py:482
  78.4 1.7 collective-permute-start.2
  80.8 25.3 %all_to_all.31 = bf16[16,4,7168]{2,1,0:T(4,128)(2,1)S(1)} all-to-all(bf16[16,4,7168]{2,1,0:T(4,128)(2,1)S(1)} %shard_map.158), channel_id=1, replica_groups={{0,8,16,24,32,40,48,56,64,72,80,88,96,104,112,120},{1,9,17,25,33,41,49,..., dimensions={0} | all-to-all | bytes 1835008 | tf_op jit(solution)/shard_map/all_to_all | solution.py:513
  108.7 1.4 collective-permute-start.10
  110.1 1.4 collective-permute-start.11
  111.6 8.9 %collective-permute-done.9.refs_2_ = bf16[32,7168]{1,0:T(8,128)(2,1)S(1)} collective-permute-done((bf16[32,7168]{1,0:T(8,128)(2,1)}, bf16[32,7168]{1,0:T(8,128)(2,1)S(1)}, u32[]{:S(2)}, u32[]{:S(2)}) %collective-permute-start.9) | collective-permute-done | bytes 458784 | tf_op jit(solution)/shard_map/ppermute | solution.py:528
  121.6 6.3 %collective-permute-done.3.refs_5_ = bf16[64,7168]{1,0:T(8,128)(2,1)S(1)} collective-permute-done((bf16[64,7168]{1,0:T(8,128)(2,1)S(1)}, bf16[64,7168]{1,0:T(8,128)(2,1)S(1)}, u32[]{:S(2)}, u32[]{:S(2)}) %collective-permute-start.3) | collective-permute-done | bytes 917536 | tf_op jit(solution)/shard_map/ppermute | solution.py:528
  132.6 2.5 %collective-permute-start.13 = (bf16[32,7168]{1,0:T(8,128)(2,1)}, bf16[32,7168]{1,0:T(8,128)(2,1)S(1)}, u32[]{:S(2)}, u32[]{:S(2)}) collective-permute-start(bf16[32,7168]{1,0:T(8,128)(2,1)} %collective-permute-done.11.refs_4_), channel_id=1, source_target_pairs={{0,3},{1,0},{2,1},{3,2},{4,7},{5,4},{6,5},{7,6},{8,11},{9,8},{10,9... | collective-permute-start | bytes 1376264 | tf_op jit(solution)/shard_map/ppermute | solution.py:528
  135.1 2.7 %collective-permute-done.14.refs_3_ = bf16[32,7168]{1,0:T(8,128)(2,1)} collective-permute-done((bf16[32,7168]{1,0:T(8,128)(2,1)S(1)}, bf16[32,7168]{1,0:T(8,128)(2,1)}, u32[]{:S(2)}, u32[]{:S(2)}) %collective-permute-start.14) | collective-permute-done | bytes 458784 | tf_op jit(solution)/shard_map/ppermute | solution.py:528
  138.1 2.3 %collective-permute-done.4.refs_2_ = bf16[32,7168]{1,0:T(8,128)(2,1)} collective-permute-done((bf16[32,7168]{1,0:T(8,128)(2,1)}, bf16[32,7168]{1,0:T(8,128)(2,1)}, u32[]{:S(2)}, u32[]{:S(2)}) %collective-permute-start.4) | collective-permute-done | bytes 458784 | tf_op jit(solution)/shard_map/ppermute | solution.py:528
  141.4 1.8 collective-permute-start.7
  143.2 2.0 copy-done
  145.2 2.0 copy-done.2
  147.3 4.0 %shard_map.159 = bf16[256,256]{1,0:T(8,128)(2,1)S(1)} custom-call(bf16[64,7168]{1,0:T(8,128)(2,1)S(1)} %reshape.146.refs_0_, bf16[32,7168]{1,0:T(8,128)(2,1)S(1)} %collective-permute-done.8.refs_1_, bf16[32,7168]{1,0:T(8,128)(2,1)S(1)} %collective-permute-done.9.refs_2_, bf16[32,7168]{1,0:T(8,128)(2,1)S(1)} %collective-permute-done.10.refs_3_, ...), custom_call_target="tpu_custom_call" | custom-call | flops 1879048192 | bytes 11010048 | tf_op jit(solution)/shard_map/pallas_call | solution.py:40
  151.3 4.0 %shard_map.160 = bf16[192,256]{1,0:T(8,128)(2,1)S(1)} custom-call(bf16[32,7168]{1,0:T(8,128)(2,1)S(1)} %collective-permute-done.12.refs_0_, bf16[32,7168]{1,0:T(8,128)(2,1)S(1)} %collective-permute-done.13.refs_1_, bf16[32,7168]{1,0:T(8,128)(2,1)} %collective-permute-done.4.refs_2_, bf16[32,7168]{1,0:T(8,128)(2,1)} %collective-permute-done.14.refs_3_, ...), custom_call_target="tpu_custom_call" | custom-call | flops 1409286144 | bytes 10092544 | tf_op jit(solution)/shard_map/pallas_call | solution.py:40
  155.3 4.7 %collective-permute-done.5.refs_0_ = bf16[32,7168]{1,0:T(8,128)(2,1)S(1)} collective-permute-done((bf16[32,7168]{1,0:T(8,128)(2,1)}, bf16[32,7168]{1,0:T(8,128)(2,1)S(1)}, u32[]{:S(2)}, u32[]{:S(2)}) %collective-permute-start.5) | collective-permute-done | bytes 458784 | tf_op jit(solution)/shard_map/ppermute | solution.py:528
  161.0 1.9 shard_map.161
  163.6 13.9 %all_to_all.32.hidden_ref = bf16[4,512,256]{2,1,0:T(8,128)(2,1)S(1)} all-to-all(bf16[4,512,256]{2,1,0:T(8,128)(2,1)S(1)} %broadcast_in_dim.48), channel_id=1, replica_groups={{0,1,2,3},{4,5,6,7},{8,9,10,11},{12,13,14,15},{16,17,18,19},{20,21,22,2..., dimensions={0} | all-to-all | bytes 2097152 | tf_op jit(solution)/shard_map/all_to_all | solution.py:563
  177.5 4.0 %shard_map.162 = bf16[128,4,1792]{2,1,0:T(4,128)(2,1)S(1)} custom-call(bf16[4,512,256]{2,1,0:T(8,128)(2,1)S(1)} %all_to_all.32.hidden_ref, bf16[256,1792]{1,0:T(8,128)(2,1)S(1)} %copy-done.9, bf16[256,1792]{1,0:T(8,128)(2,1)S(1)} %copy-done.11, bf16[256,1792]{1,0:T(8,128)(2,1)} %collective-permute-done.1.refs_2_, ...), custom_call_target="tpu_custom_call" | custom-call | flops 1879048192 | bytes 6553600 | tf_op jit(solution)/shard_map/pallas_call | solution.py:149
  181.5 35.0 %all_to_all.33.rows_ref = bf16[128,4,1792]{2,1,0:T(4,128)(2,1)S(1)} all-to-all(bf16[128,4,1792]{2,1,0:T(4,128)(2,1)S(1)} %shard_map.162), channel_id=1, replica_groups=mesh['grp'=8,'dev'=16] {'grp','dev'}, dimensions={0} | all-to-all | bytes 3670016 | tf_op jit(solution)/shard_map/all_to_all | solution.py:567
  216.5 1.6 shard_map.163
  (76 shorter events, 14.4 us)
Async XLA Ops:
  0.0 22.0 %copy-start.8 = (s32[8]{0:T(128)S(1)}, s32[8]{0:T(128)}, u32[]{:S(2)}) copy-start(s32[8]{0:T(128)} %length_ref.1) | copy-start | bytes 100
  0.0 22.0 %copy-start.5 = (bf16[8,64,512]{2,1,0:T(8,128)(2,1)S(1)}, bf16[8,64,512]{2,1,0:T(8,128)(2,1)}, u32[]{:S(2)}) copy-start(bf16[8,64,512]{2,1,0:T(8,128)(2,1)} %keys_hbm.1) | copy-start | bytes 1572868
  2.3 19.6 %all-to-all-start = ((bf16[16,8,2304]{2,1,0:T(8,128)(2,1)}), bf16[16,8,2304]{2,1,0:T(8,128)(2,1)S(1)}, u32[]{:S(2)}, u32[]{:S(2)}) async-start(bf16[16,8,2304]{2,1,0:T(8,128)(2,1)} %bitcast.16), calls=%async_computation | async-start | bytes 1179648 | tf_op jit(solution)/shard_map/all_to_all | solution.py:472
  14.0 36.0 %collective-permute-start = (bf16[256,1792]{1,0:T(8,128)(2,1)}, bf16[256,1792]{1,0:T(8,128)(2,1)S(1)}, u32[]{:S(2)}, u32[]{:S(2)}) collective-permute-start(bf16[256,1792]{1,0:T(8,128)(2,1)} %get-tuple-element.34), channel_id=1, source_target_pairs={{0,1},{1,2},{2,3},{3,0},{4,5},{5,6},{6,7},{7,4},{8,9},{9,10},{10,1... | collective-permute-start | bytes 2752520 | tf_op jit(solution)/shard_map/ppermute | solution.py:468
  15.5 34.6 %collective-permute-start.1 = (bf16[256,1792]{1,0:T(8,128)(2,1)}, bf16[256,1792]{1,0:T(8,128)(2,1)}, u32[]{:S(2)}, u32[]{:S(2)}) collective-permute-start(bf16[256,1792]{1,0:T(8,128)(2,1)} %get-tuple-element.35), channel_id=1, source_target_pairs={{0,3},{1,0},{2,1},{3,2},{4,7},{5,4},{6,5},{7,6},{8,11},{9,8},{10,9... | collective-permute-start | bytes 2752520 | tf_op jit(solution)/shard_map/ppermute | solution.py:468
  22.0 3.1 %copy-start.3 = (bf16[512,7168]{1,0:T(8,128)(2,1)S(1)}, bf16[512,7168]{1,0:T(8,128)(2,1)}, u32[]{:S(2)}) copy-start(bf16[512,7168]{1,0:T(8,128)(2,1)} %weight_hbm.1) | copy-start | bytes 22020100
  25.1 2.2 %copy-start.4 = (bf16[8,512,512]{2,1,0:T(8,128)(2,1)S(1)}, bf16[8,512,512]{2,1,0:T(8,128)(2,1)}, u32[]{:S(2)}) copy-start(bf16[8,512,512]{2,1,0:T(8,128)(2,1)} %cache_hbm.1) | copy-start | bytes 12582916
  27.2 20.2 %copy-start.6 = (bf16[4,512,128]{2,1,0:T(8,128)(2,1)S(1)}, bf16[4,512,128]{2,1,0:T(8,128)(2,1)}, u32[]{:S(2)}) copy-start(bf16[4,512,128]{2,1,0:T(8,128)(2,1)} %absorb_ref.1) | copy-start | bytes 1572868
  50.1 4.4 %copy-start.13 = (s32[8,4]{0,1:T(4,128)S(1)}, s32[8,4]{0,1:T(4,128)}, u32[]{:S(2)}) copy-start(s32[8,4]{0,1:T(4,128)} %param.25) | copy-start | bytes 388
  50.1 5.3 %copy-start.14 = (f32[8,8]{1,0:T(8,128)S(1)}, f32[8,8]{1,0:T(8,128)}, u32[]{:S(2)}) copy-start(f32[8,8]{1,0:T(8,128)} %param.27) | copy-start | bytes 772
  50.1 5.5 %copy-start.15 = (f32[8,4]{0,1:T(4,128)S(1)}, f32[8,4]{0,1:T(4,128)}, u32[]{:S(2)}) copy-start(f32[8,4]{0,1:T(4,128)} %param.26) | copy-start | bytes 388
  50.1 30.0 %copy-start.7 = (f32[7168]{0:T(1024)S(1)}, f32[7168]{0:T(1024)}, u32[]{:S(2)}) copy-start(f32[7168]{0:T(1024)} %param.24) | copy-start | bytes 86020
  50.1 56.0 %copy-start.10 = (bf16[256,1792]{1,0:T(8,128)(2,1)}, bf16[256,1792]{1,0:T(8,128)(2,1)S(1)}, u32[]{:S(2)}) copy-start(bf16[256,1792]{1,0:T(8,128)(2,1)S(1)} %collective-permute-done.refs_1_) | copy-start | bytes 2752516
  50.1 28.3 %all-to-all-start.2 = ((bf16[16,8,7168]{2,1,0:T(8,128)(2,1)}), bf16[16,8,7168]{2,1,0:T(8,128)(2,1)S(1)}, u32[]{:S(2)}, u32[]{:S(2)}) async-start(bf16[16,8,7168]{2,1,0:T(8,128)(2,1)} %bitcast.2), calls=%async_computation.2 | async-start | bytes 3670016 | tf_op jit(solution)/shard_map/all_to_all | solution.py:482
  78.4 27.9 %collective-permute-start.2 = (bf16[256,1792]{1,0:T(8,128)(2,1)}, bf16[256,1792]{1,0:T(8,128)(2,1)}, u32[]{:S(2)}, u32[]{:S(2)}) collective-permute-start(bf16[256,1792]{1,0:T(8,128)(2,1)} %get-tuple-element.45), channel_id=1, source_target_pairs={{0,2},{1,3},{2,0},{3,1},{4,6},{5,7},{6,4},{7,5},{8,10},{9,11},{10,... | collective-permute-start | bytes 2752520 | tf_op jit(solution)/shard_map/ppermute | solution.py:468
  80.8 50.9 %copy-start.12 = (s32[8]{0:T(128)S(1)}, s32[8]{0:T(128)}, u32[]{:S(2)}) copy-start(s32[8]{0:T(128)} %constant.91.clone) | copy-start | bytes 100
  106.3 21.7 %collective-permute-start.3 = (bf16[64,7168]{1,0:T(8,128)(2,1)S(1)}, bf16[64,7168]{1,0:T(8,128)(2,1)S(1)}, u32[]{:S(2)}, u32[]{:S(2)}) collective-permute-start(bf16[64,7168]{1,0:T(8,128)(2,1)S(1)} %reshape.146.refs_0_), channel_id=1, source_target_pairs={{0,4},{1,5},{2,6},{3,7},{4,0},{5,1},{6,2},{7,3},{8,12},{9,13},{10,... | collective-permute-start | bytes 2752520 | tf_op jit(solution)/shard_map/ppermute | solution.py:528
  107.4 13.1 %collective-permute-start.9 = (bf16[32,7168]{1,0:T(8,128)(2,1)}, bf16[32,7168]{1,0:T(8,128)(2,1)S(1)}, u32[]{:S(2)}, u32[]{:S(2)}) collective-permute-start(bf16[32,7168]{1,0:T(8,128)(2,1)} %get-tuple-element.57), channel_id=1, source_target_pairs={{0,1},{1,2},{2,3},{3,0},{4,5},{5,6},{6,7},{7,4},{8,9},{9,10},{10,1... | collective-permute-start | bytes 1376264 | tf_op jit(solution)/shard_map/ppermute | solution.py:528
  107.4 22.9 %collective-permute-start.8 = (bf16[32,7168]{1,0:T(8,128)(2,1)}, bf16[32,7168]{1,0:T(8,128)(2,1)S(1)}, u32[]{:S(2)}, u32[]{:S(2)}) collective-permute-start(bf16[32,7168]{1,0:T(8,128)(2,1)} %get-tuple-element.58), channel_id=1, source_target_pairs={{0,1},{1,2},{2,3},{3,0},{4,5},{5,6},{6,7},{7,4},{8,9},{9,10},{10,1... | collective-permute-start | bytes 1376264 | tf_op jit(solution)/shard_map/ppermute | solution.py:528
  108.7 23.6 %collective-permute-start.10 = (bf16[32,7168]{1,0:T(8,128)(2,1)}, bf16[32,7168]{1,0:T(8,128)(2,1)S(1)}, u32[]{:S(2)}, u32[]{:S(2)}) collective-permute-start(bf16[32,7168]{1,0:T(8,128)(2,1)} %get-tuple-element.58), channel_id=1, source_target_pairs={{0,3},{1,0},{2,1},{3,2},{4,7},{5,4},{6,5},{7,6},{8,11},{9,8},{10,9... | collective-permute-start | bytes 1376264 | tf_op jit(solution)/shard_map/ppermute | solution.py:528
  110.1 22.4 %collective-permute-start.11 = (bf16[32,7168]{1,0:T(8,128)(2,1)}, bf16[32,7168]{1,0:T(8,128)(2,1)}, u32[]{:S(2)}, u32[]{:S(2)}) collective-permute-start(bf16[32,7168]{1,0:T(8,128)(2,1)} %get-tuple-element.57), channel_id=1, source_target_pairs={{0,3},{1,0},{2,1},{3,2},{4,7},{5,4},{6,5},{7,6},{8,11},{9,8},{10,9... | collective-permute-start | bytes 1376264 | tf_op jit(solution)/shard_map/ppermute | solution.py:528
  120.5 17.3 %collective-permute-start.14 = (bf16[32,7168]{1,0:T(8,128)(2,1)S(1)}, bf16[32,7168]{1,0:T(8,128)(2,1)}, u32[]{:S(2)}, u32[]{:S(2)}) collective-permute-start(bf16[32,7168]{1,0:T(8,128)(2,1)S(1)} %collective-permute-done.9.refs_2_), channel_id=1, source_target_pairs={{0,4},{1,5},{2,6},{3,7},{4,0},{5,1},{6,2},{7,3},{8,12},{9,13},{10,... | collective-permute-start | bytes 1376264 | tf_op jit(solution)/shard_map/ppermute | solution.py:528
  129.0 11.5 %collective-permute-start.4 = (bf16[32,7168]{1,0:T(8,128)(2,1)}, bf16[32,7168]{1,0:T(8,128)(2,1)}, u32[]{:S(2)}, u32[]{:S(2)}) collective-permute-start(bf16[32,7168]{1,0:T(8,128)(2,1)} %get-tuple-element.60), channel_id=1, source_target_pairs={{0,1},{1,2},{2,3},{3,0},{4,5},{5,6},{6,7},{7,4},{8,9},{9,10},{10,1... | collective-permute-start | bytes 1376264 | tf_op jit(solution)/shard_map/ppermute | solution.py:528
  130.3 11.1 %collective-permute-start.6 = (bf16[32,7168]{1,0:T(8,128)(2,1)}, bf16[32,7168]{1,0:T(8,128)(2,1)}, u32[]{:S(2)}, u32[]{:S(2)}) collective-permute-start(bf16[32,7168]{1,0:T(8,128)(2,1)} %get-tuple-element.59), channel_id=1, source_target_pairs={{0,3},{1,0},{2,1},{3,2},{4,7},{5,4},{6,5},{7,6},{8,11},{9,8},{10,9... | collective-permute-start | bytes 1376264 | tf_op jit(solution)/shard_map/ppermute | solution.py:528
  132.3 19.0 %collective-permute-start.12 = (bf16[32,7168]{1,0:T(8,128)(2,1)S(1)}, bf16[32,7168]{1,0:T(8,128)(2,1)S(1)}, u32[]{:S(2)}, u32[]{:S(2)}) collective-permute-start(bf16[32,7168]{1,0:T(8,128)(2,1)S(1)} %collective-permute-done.8.refs_1_), channel_id=1, source_target_pairs={{0,1},{1,2},{2,3},{3,0},{4,5},{5,6},{6,7},{7,4},{8,9},{9,10},{10,1... | collective-permute-start | bytes 1376264 | tf_op jit(solution)/shard_map/ppermute | solution.py:528
  132.6 18.7 %collective-permute-start.13 = (bf16[32,7168]{1,0:T(8,128)(2,1)}, bf16[32,7168]{1,0:T(8,128)(2,1)S(1)}, u32[]{:S(2)}, u32[]{:S(2)}) collective-permute-start(bf16[32,7168]{1,0:T(8,128)(2,1)} %collective-permute-done.11.refs_4_), channel_id=1, source_target_pairs={{0,3},{1,0},{2,1},{3,2},{4,7},{5,4},{6,5},{7,6},{8,11},{9,8},{10,9... | collective-permute-start | bytes 1376264 | tf_op jit(solution)/shard_map/ppermute | solution.py:528
  137.8 13.5 %collective-permute-start.15 = (bf16[32,7168]{1,0:T(8,128)(2,1)S(1)}, bf16[32,7168]{1,0:T(8,128)(2,1)S(1)}, u32[]{:S(2)}, u32[]{:S(2)}) collective-permute-start(bf16[32,7168]{1,0:T(8,128)(2,1)S(1)} %collective-permute-done.10.refs_3_), channel_id=1, source_target_pairs={{0,4},{1,5},{2,6},{3,7},{4,0},{5,1},{6,2},{7,3},{8,12},{9,13},{10,... | collective-permute-start | bytes 1376264 | tf_op jit(solution)/shard_map/ppermute | solution.py:528
  140.5 19.6 %collective-permute-start.5 = (bf16[32,7168]{1,0:T(8,128)(2,1)}, bf16[32,7168]{1,0:T(8,128)(2,1)S(1)}, u32[]{:S(2)}, u32[]{:S(2)}) collective-permute-start(bf16[32,7168]{1,0:T(8,128)(2,1)} %collective-permute-done.4.refs_2_), channel_id=1, source_target_pairs={{0,1},{1,2},{2,3},{3,0},{4,5},{5,6},{6,7},{7,4},{8,9},{9,10},{10,1... | collective-permute-start | bytes 1376264 | tf_op jit(solution)/shard_map/ppermute | solution.py:528
  141.4 19.6 %collective-permute-start.7 = (bf16[32,7168]{1,0:T(8,128)(2,1)}, bf16[32,7168]{1,0:T(8,128)(2,1)S(1)}, u32[]{:S(2)}, u32[]{:S(2)}) collective-permute-start(bf16[32,7168]{1,0:T(8,128)(2,1)} %collective-permute-done.6.refs_5_), channel_id=1, source_target_pairs={{0,3},{1,0},{2,1},{3,2},{4,7},{5,4},{6,5},{7,6},{8,11},{9,8},{10,9... | collective-permute-start | bytes 1376264 | tf_op jit(solution)/shard_map/ppermute | solution.py:528
  151.3 9.7 %copy-start.1 = (bf16[1,7168,256]{2,1,0:T(8,128)(2,1)S(1)}, bf16[1,7168,256]{2,1,0:T(8,128)(2,1)}, u32[]{:S(2)}) copy-start(bf16[1,7168,256]{2,1,0:T(8,128)(2,1)} %refs_2_.1) | copy-start | bytes 11010052
  162.9 14.6 %copy-start.9 = (bf16[256,1792]{1,0:T(8,128)(2,1)S(1)}, bf16[256,1792]{1,0:T(8,128)(2,1)}, u32[]{:S(2)}) copy-start(bf16[256,1792]{1,0:T(8,128)(2,1)} %get-tuple-element.53.refs_0_) | copy-start | bytes 2752516
  162.9 14.6 %copy-start.11 = (bf16[256,1792]{1,0:T(8,128)(2,1)S(1)}, bf16[256,1792]{1,0:T(8,128)(2,1)}, u32[]{:S(2)}) copy-start(bf16[256,1792]{1,0:T(8,128)(2,1)} %copy-done.10) | copy-start | bytes 2752516
  (2 other events, 4.1 us)

commit v5 on v4

--- a/solution.py
+++ b/solution.py
@@ -303,7 +303,7 @@
             pltpu.VMEM((devs * requests, heads * latent), BF16),
             pltpu.SemaphoreType.DMA((requests + 2,)),
         ],
-        compiler_params=pltpu.CompilerParams(vmem_limit_bytes=28 * 1024 * 1024),
+        compiler_params=pltpu.CompilerParams(vmem_limit_bytes=41 * 1024 * 1024),
         cost_estimate=pl.CostEstimate(
             flops=2 * requests * rows * positions * (2 * latent + rope),
             bytes_accessed=2 * requests * positions * (latent + rope),

time: 219 us -> 219 us (level)
  blocking collectives: 89.6 us -> 93.2 us
  local copies, waits for them, and re-layouts: 13.3 us -> 10.2 us
    all_to_all x1, blocking collectives: 15.4 us -> 19 us  [per_device(): lax.all_to_all(latent_out, 'dev', split_axis=0, concat_axis=0, tiled=True)]
    unnamed x33 -> x31, local copies, waits for them, and re-layouts: 9.48 us -> 6.39 us
where the time goes in v5:
time: 219 us; the launch traced here: 218 us
  blocking collectives  93.2 us (43%)
  waiting for transfers between devices  56.2 us (26%)
  starting transfers between devices  28.9 us (13%)
  Pallas kernels  28.5 us (13%)
  local copies, waits for them, and re-layouts  10.2 us (5%)
    all_to_all x1, blocking collectives, per_device(): lax.all_to_all(result, ('grp', 'dev'), split_axis=0, concat_axis=0, tiled...  35 us
    ppermute x13, waiting for transfers between devices, send(): return lax.ppermute(value, 'dev', way)  28.2 us
    all_to_all x1, blocking collectives, per_device(): lax.all_to_all(outgoing, ('grp', 'dev'), split_axis=0, concat_axis=0, til...  25.3 us
    all_to_all x1, waiting for transfers between devices, per_device(): lax.all_to_all(partial.reshape(devs, requests, model_width), 'dev', split...  22.8 us
    all_to_all x1, blocking collectives, per_device(): lax.all_to_all(latent_out, 'dev', split_axis=0, concat_axis=0, tiled=True)  19 us
    all_to_all x1, blocking collectives, per_device(): lax.all_to_all(everyone, 'dev', split_axis=0, concat_axis=0, tiled=True,...  13.9 us
    ppermute x13, starting transfers between devices, send(): return lax.ppermute(value, 'dev', way)  11.6 us
    pallas_call x3, Pallas kernels, expert_hidden(): pl.pallas_call(functools.partial(hidden_kernel, len(blocks)), grid=(width...  9.95 us
  transfers between devices with their start and end apart: 18, of which 10 were waited for; matrix products, arithmetic and copies ran while one was open for 2% of the time, Pallas kernels for 9%

profile of v5, /device:TPU:1, one launch (start us, length us, event | category | flops | bytes accessed | tf_op | source)
XLA Modules:
  0.0 218.1 jit_solution(14388933160794565926)
XLA Ops:
  0.0 2.3 %shard_map.154 = bf16[128,2304]{1,0:T(8,128)(2,1)} custom-call(bf16[128,512]{1,0:T(8,128)(2,1)} %nope_ref.1, bf16[128,256]{1,0:T(8,128)(2,1)} %rope_ref.1, bf16[4,128,512]{2,1,0:T(8,128)(2,1)} %weight_ref.2), custom_call_target="tpu_custom_call" | custom-call | flops 67108864 | bytes 1114112 | tf_op jit(solution)/shard_map/pallas_call | solution.py:194
  2.3 8.6 %all-to-all-start = ((bf16[16,8,2304]{2,1,0:T(8,128)(2,1)}), bf16[16,8,2304]{2,1,0:T(8,128)(2,1)S(1)}, u32[]{:S(2)}, u32[]{:S(2)}) async-start(bf16[16,8,2304]{2,1,0:T(8,128)(2,1)} %bitcast.16), calls=%async_computation | async-start | bytes 1179648 | tf_op jit(solution)/shard_map/all_to_all | solution.py:472
  10.9 3.1 %shard_map.157 = (bf16[256,1792]{1,0:T(8,128)(2,1)}, bf16[256,1792]{1,0:T(8,128)(2,1)}, bf16[256,1792]{1,0:T(8,128)(2,1)}, bf16[256,1792]{1,0:T(8,128)(2,1)}) custom-call(bf16[1,256,7168]{2,1,0:T(8,128)(2,1)} %weight_ref.3), custom_call_target="tpu_custom_call" | custom-call | bytes 7340032 | tf_op jit(solution)/shard_map/pallas_call | solution.py:86
  14.0 1.4 collective-permute-start
  15.5 1.3 collective-permute-start.1
  16.8 5.2 %all-to-all-done.query_ref = bf16[16,8,2304]{2,1,0:T(8,128)(2,1)S(1)} async-done(((bf16[16,8,2304]{2,1,0:T(8,128)(2,1)}), bf16[16,8,2304]{2,1,0:T(8,128)(2,1)S(1)}, u32[]{:S(2)}, u32[]{:S(2)}) %all-to-all-start) | async-done | bytes 589856 | tf_op jit(solution)/shard_map/all_to_all | solution.py:472
  22.0 2.2 %copy-done.3 = bf16[8,512,512]{2,1,0:T(8,128)(2,1)S(1)} copy-done((bf16[8,512,512]{2,1,0:T(8,128)(2,1)S(1)}, bf16[8,512,512]{2,1,0:T(8,128)(2,1)}, u32[]{:S(2)}) %copy-start.3) | copy-done | bytes 4194328
  24.1 4.2 %shard_map.155 = (bf16[16,8,2048]{2,1,0:T(8,128)(2,1)S(1)}, bf16[512,7168]{1,0:T(8,128)(2,1)S(1)}) custom-call(s32[8]{0:T(128)S(1)} %copy-done.7, bf16[16,8,2304]{2,1,0:T(8,128)(2,1)S(1)} %all-to-all-done.query_ref, bf16[8,512,512]{2,1,0:T(8,128)(2,1)S(1)} %copy-done.3, bf16[8,64,512]{2,1,0:T(8,128)(2,1)S(1)} %copy-done.4, bf16[512,7168]{1,0:T(8,128)(2,1)} %weight_hbm.1), custom_call_target="tpu_custom_call" | custom-call | flops 570425344 | bytes 4718592 | tf_op jit(solution)/shard_map/pallas_call | solution.py:285
  28.4 19.0 %all_to_all.30 = bf16[16,8,2048]{2,1,0:T(8,128)(2,1)S(1)} all-to-all(bf16[16,8,2048]{2,1,0:T(8,128)(2,1)S(1)} %get-tuple-element.31), channel_id=1, replica_groups=mesh['grp'=8,'dev'=16] {'dev'}, dimensions={0} | all-to-all | bytes 1048576 | tf_op jit(solution)/shard_map/all_to_all | solution.py:477
  47.4 2.6 %shard_map.156 = bf16[128,7168]{1,0:T(8,128)(2,1)} custom-call(bf16[128,2048]{1,0:T(8,128)(2,1)S(1)} %bitcast.13, bf16[4,512,128]{2,1,0:T(8,128)(2,1)S(1)} %copy-done.5, bf16[512,7168]{1,0:T(8,128)(2,1)S(1)} %get-tuple-element.32.weight_ref), custom_call_target="tpu_custom_call" | custom-call | flops 1006632960 | bytes 9175040 | tf_op jit(solution)/shard_map/pallas_call | solution.py:338
  50.1 4.4 %all-to-all-start.2 = ((bf16[16,8,7168]{2,1,0:T(8,128)(2,1)}), bf16[16,8,7168]{2,1,0:T(8,128)(2,1)S(1)}, u32[]{:S(2)}, u32[]{:S(2)}) async-start(bf16[16,8,7168]{2,1,0:T(8,128)(2,1)} %bitcast.2), calls=%async_computation.2 | async-start | bytes 3670016 | tf_op jit(solution)/shard_map/all_to_all | solution.py:482
  55.6 22.8 %all-to-all-done.2.partial_ref = bf16[16,8,7168]{2,1,0:T(8,128)(2,1)S(1)} async-done(((bf16[16,8,7168]{2,1,0:T(8,128)(2,1)}), bf16[16,8,7168]{2,1,0:T(8,128)(2,1)S(1)}, u32[]{:S(2)}, u32[]{:S(2)}) %all-to-all-start.2) | async-done | bytes 1835040 | tf_op jit(solution)/shard_map/all_to_all | solution.py:482
  78.4 1.6 collective-permute-start.2
  80.8 25.3 %all_to_all.31 = bf16[16,4,7168]{2,1,0:T(4,128)(2,1)S(1)} all-to-all(bf16[16,4,7168]{2,1,0:T(4,128)(2,1)S(1)} %shard_map.158), channel_id=1, replica_groups={{0,8,16,24,32,40,48,56,64,72,80,88,96,104,112,120},{1,9,17,25,33,41,49,..., dimensions={0} | all-to-all | bytes 1835008 | tf_op jit(solution)/shard_map/all_to_all | solution.py:513
  108.7 1.4 collective-permute-start.10
  110.1 1.4 collective-permute-start.11
  111.5 8.9 %collective-permute-done.9.refs_2_ = bf16[32,7168]{1,0:T(8,128)(2,1)S(1)} collective-permute-done((bf16[32,7168]{1,0:T(8,128)(2,1)}, bf16[32,7168]{1,0:T(8,128)(2,1)S(1)}, u32[]{:S(2)}, u32[]{:S(2)}) %collective-permute-start.9) | collective-permute-done | bytes 458784 | tf_op jit(solution)/shard_map/ppermute | solution.py:528
  121.6 6.4 %collective-permute-done.3.refs_5_ = bf16[64,7168]{1,0:T(8,128)(2,1)S(1)} collective-permute-done((bf16[64,7168]{1,0:T(8,128)(2,1)S(1)}, bf16[64,7168]{1,0:T(8,128)(2,1)S(1)}, u32[]{:S(2)}, u32[]{:S(2)}) %collective-permute-start.3) | collective-permute-done | bytes 917536 | tf_op jit(solution)/shard_map/ppermute | solution.py:528
  132.5 2.5 %collective-permute-start.13 = (bf16[32,7168]{1,0:T(8,128)(2,1)}, bf16[32,7168]{1,0:T(8,128)(2,1)S(1)}, u32[]{:S(2)}, u32[]{:S(2)}) collective-permute-start(bf16[32,7168]{1,0:T(8,128)(2,1)} %collective-permute-done.11.refs_4_), channel_id=1, source_target_pairs={{0,3},{1,0},{2,1},{3,2},{4,7},{5,4},{6,5},{7,6},{8,11},{9,8},{10,9... | collective-permute-start | bytes 1376264 | tf_op jit(solution)/shard_map/ppermute | solution.py:528
  135.1 2.7 %collective-permute-done.14.refs_3_ = bf16[32,7168]{1,0:T(8,128)(2,1)} collective-permute-done((bf16[32,7168]{1,0:T(8,128)(2,1)S(1)}, bf16[32,7168]{1,0:T(8,128)(2,1)}, u32[]{:S(2)}, u32[]{:S(2)}) %collective-permute-start.14) | collective-permute-done | bytes 458784 | tf_op jit(solution)/shard_map/ppermute | solution.py:528
  138.1 2.3 %collective-permute-done.4.refs_2_ = bf16[32,7168]{1,0:T(8,128)(2,1)} collective-permute-done((bf16[32,7168]{1,0:T(8,128)(2,1)}, bf16[32,7168]{1,0:T(8,128)(2,1)}, u32[]{:S(2)}, u32[]{:S(2)}) %collective-permute-start.4) | collective-permute-done | bytes 458784 | tf_op jit(solution)/shard_map/ppermute | solution.py:528
  141.4 1.8 collective-permute-start.7
  143.2 2.0 copy-done
  145.2 2.0 copy-done.2
  147.2 4.0 %shard_map.159 = bf16[256,256]{1,0:T(8,128)(2,1)S(1)} custom-call(bf16[64,7168]{1,0:T(8,128)(2,1)S(1)} %reshape.146.refs_0_, bf16[32,7168]{1,0:T(8,128)(2,1)S(1)} %collective-permute-done.8.refs_1_, bf16[32,7168]{1,0:T(8,128)(2,1)S(1)} %collective-permute-done.9.refs_2_, bf16[32,7168]{1,0:T(8,128)(2,1)S(1)} %collective-permute-done.10.refs_3_, ...), custom_call_target="tpu_custom_call" | custom-call | flops 1879048192 | bytes 11010048 | tf_op jit(solution)/shard_map/pallas_call | solution.py:40
  151.3 4.0 %shard_map.160 = bf16[192,256]{1,0:T(8,128)(2,1)S(1)} custom-call(bf16[32,7168]{1,0:T(8,128)(2,1)S(1)} %collective-permute-done.12.refs_0_, bf16[32,7168]{1,0:T(8,128)(2,1)S(1)} %collective-permute-done.13.refs_1_, bf16[32,7168]{1,0:T(8,128)(2,1)} %collective-permute-done.4.refs_2_, bf16[32,7168]{1,0:T(8,128)(2,1)} %collective-permute-done.14.refs_3_, ...), custom_call_target="tpu_custom_call" | custom-call | flops 1409286144 | bytes 10092544 | tf_op jit(solution)/shard_map/pallas_call | solution.py:40
  155.3 4.7 %collective-permute-done.5.refs_0_ = bf16[32,7168]{1,0:T(8,128)(2,1)S(1)} collective-permute-done((bf16[32,7168]{1,0:T(8,128)(2,1)}, bf16[32,7168]{1,0:T(8,128)(2,1)S(1)}, u32[]{:S(2)}, u32[]{:S(2)}) %collective-permute-start.5) | collective-permute-done | bytes 458784 | tf_op jit(solution)/shard_map/ppermute | solution.py:528
  160.9 1.9 shard_map.161
  163.6 13.9 %all_to_all.32.hidden_ref = bf16[4,512,256]{2,1,0:T(8,128)(2,1)S(1)} all-to-all(bf16[4,512,256]{2,1,0:T(8,128)(2,1)S(1)} %broadcast_in_dim.48), channel_id=1, replica_groups={{0,1,2,3},{4,5,6,7},{8,9,10,11},{12,13,14,15},{16,17,18,19},{20,21,22,2..., dimensions={0} | all-to-all | bytes 2097152 | tf_op jit(solution)/shard_map/all_to_all | solution.py:563
  177.5 4.0 %shard_map.162 = bf16[128,4,1792]{2,1,0:T(4,128)(2,1)S(1)} custom-call(bf16[4,512,256]{2,1,0:T(8,128)(2,1)S(1)} %all_to_all.32.hidden_ref, bf16[256,1792]{1,0:T(8,128)(2,1)S(1)} %copy-done.8, bf16[256,1792]{1,0:T(8,128)(2,1)S(1)} %copy-done.10, bf16[256,1792]{1,0:T(8,128)(2,1)} %collective-permute-done.1.refs_2_, ...), custom_call_target="tpu_custom_call" | custom-call | flops 1879048192 | bytes 6553600 | tf_op jit(solution)/shard_map/pallas_call | solution.py:149
  181.5 35.0 %all_to_all.33.rows_ref = bf16[128,4,1792]{2,1,0:T(4,128)(2,1)S(1)} all-to-all(bf16[128,4,1792]{2,1,0:T(4,128)(2,1)S(1)} %shard_map.162), channel_id=1, replica_groups=mesh['grp'=8,'dev'=16] {'grp','dev'}, dimensions={0} | all-to-all | bytes 3670016 | tf_op jit(solution)/shard_map/all_to_all | solution.py:567
  216.5 1.6 shard_map.163
  (74 shorter events, 13.0 us)
Async XLA Ops:
  0.0 22.0 %copy-start.7 = (s32[8]{0:T(128)S(1)}, s32[8]{0:T(128)}, u32[]{:S(2)}) copy-start(s32[8]{0:T(128)} %length_ref.1) | copy-start | bytes 100
  0.0 22.0 %copy-start.4 = (bf16[8,64,512]{2,1,0:T(8,128)(2,1)S(1)}, bf16[8,64,512]{2,1,0:T(8,128)(2,1)}, u32[]{:S(2)}) copy-start(bf16[8,64,512]{2,1,0:T(8,128)(2,1)} %keys_hbm.1) | copy-start | bytes 1572868
  2.3 19.6 %all-to-all-start = ((bf16[16,8,2304]{2,1,0:T(8,128)(2,1)}), bf16[16,8,2304]{2,1,0:T(8,128)(2,1)S(1)}, u32[]{:S(2)}, u32[]{:S(2)}) async-start(bf16[16,8,2304]{2,1,0:T(8,128)(2,1)} %bitcast.16), calls=%async_computation | async-start | bytes 1179648 | tf_op jit(solution)/shard_map/all_to_all | solution.py:472
  14.0 36.0 %collective-permute-start = (bf16[256,1792]{1,0:T(8,128)(2,1)}, bf16[256,1792]{1,0:T(8,128)(2,1)S(1)}, u32[]{:S(2)}, u32[]{:S(2)}) collective-permute-start(bf16[256,1792]{1,0:T(8,128)(2,1)} %get-tuple-element.34), channel_id=1, source_target_pairs={{0,1},{1,2},{2,3},{3,0},{4,5},{5,6},{6,7},{7,4},{8,9},{9,10},{10,1... | collective-permute-start | bytes 2752520 | tf_op jit(solution)/shard_map/ppermute | solution.py:468
  15.5 34.6 %collective-permute-start.1 = (bf16[256,1792]{1,0:T(8,128)(2,1)}, bf16[256,1792]{1,0:T(8,128)(2,1)}, u32[]{:S(2)}, u32[]{:S(2)}) collective-permute-start(bf16[256,1792]{1,0:T(8,128)(2,1)} %get-tuple-element.35), channel_id=1, source_target_pairs={{0,3},{1,0},{2,1},{3,2},{4,7},{5,4},{6,5},{7,6},{8,11},{9,8},{10,9... | collective-permute-start | bytes 2752520 | tf_op jit(solution)/shard_map/ppermute | solution.py:468
  22.0 2.2 %copy-start.3 = (bf16[8,512,512]{2,1,0:T(8,128)(2,1)S(1)}, bf16[8,512,512]{2,1,0:T(8,128)(2,1)}, u32[]{:S(2)}) copy-start(bf16[8,512,512]{2,1,0:T(8,128)(2,1)} %cache_hbm.1) | copy-start | bytes 12582916
  24.1 23.3 %copy-start.5 = (bf16[4,512,128]{2,1,0:T(8,128)(2,1)S(1)}, bf16[4,512,128]{2,1,0:T(8,128)(2,1)}, u32[]{:S(2)}) copy-start(bf16[4,512,128]{2,1,0:T(8,128)(2,1)} %absorb_ref.1) | copy-start | bytes 1572868
  50.0 4.4 %copy-start.12 = (s32[8,4]{0,1:T(4,128)S(1)}, s32[8,4]{0,1:T(4,128)}, u32[]{:S(2)}) copy-start(s32[8,4]{0,1:T(4,128)} %param.25) | copy-start | bytes 388
  50.0 5.3 %copy-start.13 = (f32[8,8]{1,0:T(8,128)S(1)}, f32[8,8]{1,0:T(8,128)}, u32[]{:S(2)}) copy-start(f32[8,8]{1,0:T(8,128)} %param.27) | copy-start | bytes 772
  50.0 5.5 %copy-start.14 = (f32[8,4]{0,1:T(4,128)S(1)}, f32[8,4]{0,1:T(4,128)}, u32[]{:S(2)}) copy-start(f32[8,4]{0,1:T(4,128)} %param.26) | copy-start | bytes 388
  50.1 30.0 %copy-start.6 = (f32[7168]{0:T(1024)S(1)}, f32[7168]{0:T(1024)}, u32[]{:S(2)}) copy-start(f32[7168]{0:T(1024)} %param.24) | copy-start | bytes 86020
  50.1 56.0 %copy-start.9 = (bf16[256,1792]{1,0:T(8,128)(2,1)}, bf16[256,1792]{1,0:T(8,128)(2,1)S(1)}, u32[]{:S(2)}) copy-start(bf16[256,1792]{1,0:T(8,128)(2,1)S(1)} %collective-permute-done.refs_1_) | copy-start | bytes 2752516
  50.1 28.4 %all-to-all-start.2 = ((bf16[16,8,7168]{2,1,0:T(8,128)(2,1)}), bf16[16,8,7168]{2,1,0:T(8,128)(2,1)S(1)}, u32[]{:S(2)}, u32[]{:S(2)}) async-start(bf16[16,8,7168]{2,1,0:T(8,128)(2,1)} %bitcast.2), calls=%async_computation.2 | async-start | bytes 3670016 | tf_op jit(solution)/shard_map/all_to_all | solution.py:482
  78.4 27.8 %collective-permute-start.2 = (bf16[256,1792]{1,0:T(8,128)(2,1)}, bf16[256,1792]{1,0:T(8,128)(2,1)}, u32[]{:S(2)}, u32[]{:S(2)}) collective-permute-start(bf16[256,1792]{1,0:T(8,128)(2,1)} %get-tuple-element.45), channel_id=1, source_target_pairs={{0,2},{1,3},{2,0},{3,1},{4,6},{5,7},{6,4},{7,5},{8,10},{9,11},{10,... | collective-permute-start | bytes 2752520 | tf_op jit(solution)/shard_map/ppermute | solution.py:468
  80.8 50.9 %copy-start.11 = (s32[8]{0:T(128)S(1)}, s32[8]{0:T(128)}, u32[]{:S(2)}) copy-start(s32[8]{0:T(128)} %constant.91.clone) | copy-start | bytes 100
  106.3 21.7 %collective-permute-start.3 = (bf16[64,7168]{1,0:T(8,128)(2,1)S(1)}, bf16[64,7168]{1,0:T(8,128)(2,1)S(1)}, u32[]{:S(2)}, u32[]{:S(2)}) collective-permute-start(bf16[64,7168]{1,0:T(8,128)(2,1)S(1)} %reshape.146.refs_0_), channel_id=1, source_target_pairs={{0,4},{1,5},{2,6},{3,7},{4,0},{5,1},{6,2},{7,3},{8,12},{9,13},{10,... | collective-permute-start | bytes 2752520 | tf_op jit(solution)/shard_map/ppermute | solution.py:528
  107.4 13.1 %collective-permute-start.9 = (bf16[32,7168]{1,0:T(8,128)(2,1)}, bf16[32,7168]{1,0:T(8,128)(2,1)S(1)}, u32[]{:S(2)}, u32[]{:S(2)}) collective-permute-start(bf16[32,7168]{1,0:T(8,128)(2,1)} %get-tuple-element.57), channel_id=1, source_target_pairs={{0,1},{1,2},{2,3},{3,0},{4,5},{5,6},{6,7},{7,4},{8,9},{9,10},{10,1... | collective-permute-start | bytes 1376264 | tf_op jit(solution)/shard_map/ppermute | solution.py:528
  107.4 22.9 %collective-permute-start.8 = (bf16[32,7168]{1,0:T(8,128)(2,1)}, bf16[32,7168]{1,0:T(8,128)(2,1)S(1)}, u32[]{:S(2)}, u32[]{:S(2)}) collective-permute-start(bf16[32,7168]{1,0:T(8,128)(2,1)} %get-tuple-element.58), channel_id=1, source_target_pairs={{0,1},{1,2},{2,3},{3,0},{4,5},{5,6},{6,7},{7,4},{8,9},{9,10},{10,1... | collective-permute-start | bytes 1376264 | tf_op jit(solution)/shard_map/ppermute | solution.py:528
  108.7 23.6 %collective-permute-start.10 = (bf16[32,7168]{1,0:T(8,128)(2,1)}, bf16[32,7168]{1,0:T(8,128)(2,1)S(1)}, u32[]{:S(2)}, u32[]{:S(2)}) collective-permute-start(bf16[32,7168]{1,0:T(8,128)(2,1)} %get-tuple-element.58), channel_id=1, source_target_pairs={{0,3},{1,0},{2,1},{3,2},{4,7},{5,4},{6,5},{7,6},{8,11},{9,8},{10,9... | collective-permute-start | bytes 1376264 | tf_op jit(solution)/shard_map/ppermute | solution.py:528
  110.1 22.4 %collective-permute-start.11 = (bf16[32,7168]{1,0:T(8,128)(2,1)}, bf16[32,7168]{1,0:T(8,128)(2,1)}, u32[]{:S(2)}, u32[]{:S(2)}) collective-permute-start(bf16[32,7168]{1,0:T(8,128)(2,1)} %get-tuple-element.57), channel_id=1, source_target_pairs={{0,3},{1,0},{2,1},{3,2},{4,7},{5,4},{6,5},{7,6},{8,11},{9,8},{10,9... | collective-permute-start | bytes 1376264 | tf_op jit(solution)/shard_map/ppermute | solution.py:528
  120.5 17.3 %collective-permute-start.14 = (bf16[32,7168]{1,0:T(8,128)(2,1)S(1)}, bf16[32,7168]{1,0:T(8,128)(2,1)}, u32[]{:S(2)}, u32[]{:S(2)}) collective-permute-start(bf16[32,7168]{1,0:T(8,128)(2,1)S(1)} %collective-permute-done.9.refs_2_), channel_id=1, source_target_pairs={{0,4},{1,5},{2,6},{3,7},{4,0},{5,1},{6,2},{7,3},{8,12},{9,13},{10,... | collective-permute-start | bytes 1376264 | tf_op jit(solution)/shard_map/ppermute | solution.py:528
  129.0 11.5 %collective-permute-start.4 = (bf16[32,7168]{1,0:T(8,128)(2,1)}, bf16[32,7168]{1,0:T(8,128)(2,1)}, u32[]{:S(2)}, u32[]{:S(2)}) collective-permute-start(bf16[32,7168]{1,0:T(8,128)(2,1)} %get-tuple-element.60), channel_id=1, source_target_pairs={{0,1},{1,2},{2,3},{3,0},{4,5},{5,6},{6,7},{7,4},{8,9},{9,10},{10,1... | collective-permute-start | bytes 1376264 | tf_op jit(solution)/shard_map/ppermute | solution.py:528
  130.3 11.1 %collective-permute-start.6 = (bf16[32,7168]{1,0:T(8,128)(2,1)}, bf16[32,7168]{1,0:T(8,128)(2,1)}, u32[]{:S(2)}, u32[]{:S(2)}) collective-permute-start(bf16[32,7168]{1,0:T(8,128)(2,1)} %get-tuple-element.59), channel_id=1, source_target_pairs={{0,3},{1,0},{2,1},{3,2},{4,7},{5,4},{6,5},{7,6},{8,11},{9,8},{10,9... | collective-permute-start | bytes 1376264 | tf_op jit(solution)/shard_map/ppermute | solution.py:528
  132.3 19.0 %collective-permute-start.12 = (bf16[32,7168]{1,0:T(8,128)(2,1)S(1)}, bf16[32,7168]{1,0:T(8,128)(2,1)S(1)}, u32[]{:S(2)}, u32[]{:S(2)}) collective-permute-start(bf16[32,7168]{1,0:T(8,128)(2,1)S(1)} %collective-permute-done.8.refs_1_), channel_id=1, source_target_pairs={{0,1},{1,2},{2,3},{3,0},{4,5},{5,6},{6,7},{7,4},{8,9},{9,10},{10,1... | collective-permute-start | bytes 1376264 | tf_op jit(solution)/shard_map/ppermute | solution.py:528
  132.5 18.8 %collective-permute-start.13 = (bf16[32,7168]{1,0:T(8,128)(2,1)}, bf16[32,7168]{1,0:T(8,128)(2,1)S(1)}, u32[]{:S(2)}, u32[]{:S(2)}) collective-permute-start(bf16[32,7168]{1,0:T(8,128)(2,1)} %collective-permute-done.11.refs_4_), channel_id=1, source_target_pairs={{0,3},{1,0},{2,1},{3,2},{4,7},{5,4},{6,5},{7,6},{8,11},{9,8},{10,9... | collective-permute-start | bytes 1376264 | tf_op jit(solution)/shard_map/ppermute | solution.py:528
  137.8 13.5 %collective-permute-start.15 = (bf16[32,7168]{1,0:T(8,128)(2,1)S(1)}, bf16[32,7168]{1,0:T(8,128)(2,1)S(1)}, u32[]{:S(2)}, u32[]{:S(2)}) collective-permute-start(bf16[32,7168]{1,0:T(8,128)(2,1)S(1)} %collective-permute-done.10.refs_3_), channel_id=1, source_target_pairs={{0,4},{1,5},{2,6},{3,7},{4,0},{5,1},{6,2},{7,3},{8,12},{9,13},{10,... | collective-permute-start | bytes 1376264 | tf_op jit(solution)/shard_map/ppermute | solution.py:528
  140.5 19.6 %collective-permute-start.5 = (bf16[32,7168]{1,0:T(8,128)(2,1)}, bf16[32,7168]{1,0:T(8,128)(2,1)S(1)}, u32[]{:S(2)}, u32[]{:S(2)}) collective-permute-start(bf16[32,7168]{1,0:T(8,128)(2,1)} %collective-permute-done.4.refs_2_), channel_id=1, source_target_pairs={{0,1},{1,2},{2,3},{3,0},{4,5},{5,6},{6,7},{7,4},{8,9},{9,10},{10,1... | collective-permute-start | bytes 1376264 | tf_op jit(solution)/shard_map/ppermute | solution.py:528
  141.4 19.6 %collective-permute-start.7 = (bf16[32,7168]{1,0:T(8,128)(2,1)}, bf16[32,7168]{1,0:T(8,128)(2,1)S(1)}, u32[]{:S(2)}, u32[]{:S(2)}) collective-permute-start(bf16[32,7168]{1,0:T(8,128)(2,1)} %collective-permute-done.6.refs_5_), channel_id=1, source_target_pairs={{0,3},{1,0},{2,1},{3,2},{4,7},{5,4},{6,5},{7,6},{8,11},{9,8},{10,9... | collective-permute-start | bytes 1376264 | tf_op jit(solution)/shard_map/ppermute | solution.py:528
  143.2 2.0 copy-start
  151.3 9.7 %copy-start.1 = (bf16[1,7168,256]{2,1,0:T(8,128)(2,1)S(1)}, bf16[1,7168,256]{2,1,0:T(8,128)(2,1)}, u32[]{:S(2)}) copy-start(bf16[1,7168,256]{2,1,0:T(8,128)(2,1)} %refs_2_.1) | copy-start | bytes 11010052
  162.9 14.6 %copy-start.8 = (bf16[256,1792]{1,0:T(8,128)(2,1)S(1)}, bf16[256,1792]{1,0:T(8,128)(2,1)}, u32[]{:S(2)}) copy-start(bf16[256,1792]{1,0:T(8,128)(2,1)} %get-tuple-element.53.refs_0_) | copy-start | bytes 2752516
  162.9 14.6 %copy-start.10 = (bf16[256,1792]{1,0:T(8,128)(2,1)S(1)}, bf16[256,1792]{1,0:T(8,128)(2,1)}, u32[]{:S(2)}) copy-start(bf16[256,1792]{1,0:T(8,128)(2,1)} %copy-done.9) | copy-start | bytes 2752516
  (1 other events, 2.0 us)
